TPU v7x, 32 devices: a whole 2x2x4 slice. The times are simulated.
32 devices in a mesh: leaf: 8 (over z, y), front: 4 (over x, core).
Axes of the slice: x: 2, y: 2, z: 4, core: 2. Of those that a mesh axis runs over, the one named last changes fastest.
Arguments:
- sub_rhs: float32 [98304, 128], P(('leaf', 'front')), may hold values from -6 to 6
- sub_dinv: float32 [768, 128, 128], P(('leaf', 'front')), as said below
- sub_off: float32 [736, 2, 128, 128], P(('leaf', 'front')), may hold values from -0.25 to 0.25
- sub_pattern: int32 [736, 2], P(('leaf', 'front')), may hold values from 0 to 22, as said below
- sub_update: float32 [8192, 3072], P(('leaf', 'front')), may hold values from -0.0546875 to 0.0546875
- sub_map: int32 [32, 2], replicated, may hold values from 0 to 31, as said below
- front_rhs: float32 [30720, 128], P(('leaf', 'front')), may hold values from -6 to 6
- piv_inverse: float32 [30720, 2048], P(('leaf', 'front')), as said below
- upd_factor: float32 [28672, 2048], P(('leaf', 'front')), may hold values from -0.0625 to 0.0625
- front_map: int32 [14, 16], replicated, may hold values from 0 to 31, as said below
Outputs:
- sub_solution: float32 [98304, 128], P(('leaf', 'front'))
- front_solution: float32 [30720, 128], P(('leaf', 'front'))
Inputs may be any that keep to these rules, and one draw needn't show every extreme that they name: `sub_pattern`: in entry row i - 1 of a subtree (its block row i) the first index is i - 1 and every index is below i. `sub_map`: each row names 2 different blocks of a level-1 front. `front_map`: rows are ordered by level, then by front; each row names 16 different parent blocks, and the last two rows (children of the root) name only the 16 pivot blocks. `sub_dinv`: each inverse diagonal block is full. `piv_inverse`: each front's inverse pivot block is lower triangular with a unit diagonal.
All inputs are finite; a program needn't handle non-finite values.
Results may differ from a plain program's by a relative error of at most 0.0001.
Values sent between devices are 32-bit elements; how exact they have to be, the bound alone decides.
No kernel may reach another device: no remote copies, remote signals or barrier semaphores. Data moves between devices by JAX's collectives and lax.ppermute only.
A program may use at most 128 MiB of HBM per device.

v0:
```python
import jax
import jax.numpy as jnp
from jax import lax
from jax.sharding import PartitionSpec as P

B = 128
P_SIZE = 2048
U = 2048
SB = 24
USB = 2
K = 2


def swapped(value, axis, apart):
    mask = 2**apart
    pairs = [(source, source ^ mask) for source in range(lax.axis_size(axis))]
    return lax.ppermute(value, axis, pairs)


def lookup(lookup_table, indices):
    hits = indices[:, None] == jnp.arange(lookup_table.shape[0])[None, :]
    return jnp.sum(jnp.where(hits, lookup_table[None, :], 0), axis=1)


def target(frontal_row, piv_rows, upd_rows):
    is_pivot = frontal_row < P_SIZE
    upd_part = jnp.maximum(frontal_row - P_SIZE, 0)
    divisor = max(upd_rows, 1)
    owners = jnp.where(is_pivot, frontal_row // piv_rows, upd_part // divisor)
    position = jnp.where(is_pivot, frontal_row % piv_rows, piv_rows + upd_part % divisor)
    return (owners, position)


def doubling(gathered, bit_count):
    leaf_pos = lax.axis_index("leaf")
    for which_bit in range(bit_count):
        partner_rows = swapped(gathered, "leaf", which_bit)
        upper_side = leaf_pos >> which_bit & 1 == 1
        gathered = jnp.where(
            upper_side,
            jnp.concatenate([partner_rows, gathered], 0),
            jnp.concatenate([gathered, partner_rows], 0),
        )
    return gathered


def group_gather(local_rows, bit_count):
    gathered = lax.all_gather(local_rows, "front", axis=0, tiled=True)
    return doubling(gathered, bit_count)


def per_device(
    sub_rhs,
    sub_dinv,
    sub_off,
    sub_pattern,
    sub_update,
    sub_map,
    front_rhs,
    piv_inverse,
    upd_factor,
    front_map,
):
    highest = lax.Precision.HIGHEST
    front_size = lax.axis_size("front")
    leaf_size = lax.axis_size("leaf")
    level_count = leaf_size.bit_length()
    leaf_pos = lax.axis_index("leaf")
    front_pos = lax.axis_index("front")
    num_cols = sub_rhs.shape[1]
    blocks = sub_rhs.reshape(SB, B, num_cols)
    solved = jnp.zeros((SB, B, num_cols), jnp.float32)
    solved = solved.at[0].set(
        jnp.dot(sub_dinv[0], blocks[0], precision=highest, preferred_element_type=jnp.float32)
    )

    def advance(block_id, solved):
        remain = blocks[block_id]
        for which in range(K):
            remain = remain - jnp.dot(
                sub_off[block_id - 1, which],
                solved[sub_pattern[block_id - 1, which]],
                precision=highest,
                preferred_element_type=jnp.float32,
            )
        return solved.at[block_id].set(
            jnp.dot(
                sub_dinv[block_id], remain, precision=highest, preferred_element_type=jnp.float32
            )
        )

    solved = lax.fori_loop(1, SB, advance, solved)
    flat_rows = solved.reshape(SB * B, num_cols)
    child_update = -jnp.dot(
        sub_update, flat_rows, precision=highest, preferred_element_type=jnp.float32
    )
    first_piv = P_SIZE // front_size
    first_stride = first_piv + U // front_size
    gathered = lax.all_gather(child_update, "front", axis=0, tiled=True)
    child_maps = lax.dynamic_slice_in_dim(sub_map, leaf_pos * front_size, front_size, 0).reshape(
        front_size * USB
    )
    row_ids = jnp.arange(front_size * USB * B)
    child_ids = row_ids // (USB * B)
    inner_rows = row_ids % (USB * B)
    parent_block = lookup(child_maps, child_ids * USB + inner_rows // B)
    owners, position = target(parent_block * B + inner_rows % B, first_piv, U // front_size)
    target_slot = jnp.where(owners == front_pos, position, first_stride)
    shared = (
        jnp.zeros((first_stride, num_cols), jnp.float32).at[target_slot].add(gathered, mode="drop")
    )
    results = []
    piv_offset = 0
    upd_offset = 0
    map_offset = 0
    for level in range(1, level_count + 1):
        group_span = 2 ** (level - 1)
        group_size = front_size * group_span
        piv_rows = P_SIZE // group_size
        pivot_side = shared[:piv_rows] + front_rhs[piv_offset : piv_offset + piv_rows]
        piv_all = group_gather(pivot_side, level - 1)
        solution = jnp.dot(
            piv_inverse[piv_offset : piv_offset + piv_rows],
            piv_all,
            precision=highest,
            preferred_element_type=jnp.float32,
        )
        results.append(solution)
        if level < level_count:
            upd_rows = U // group_size
            update_side = shared[piv_rows:]
            solution_all = group_gather(solution, level - 1)
            update = update_side - jnp.dot(
                upd_factor[upd_offset : upd_offset + upd_rows],
                solution_all,
                precision=highest,
                preferred_element_type=jnp.float32,
            )
            parent_piv = P_SIZE // (2 * group_size)
            parent_upd = U // (2 * group_size) if level + 1 < level_count else 0
            stride = parent_piv + parent_upd
            node_index = leaf_pos >> level - 1
            map_row = lax.dynamic_index_in_dim(
                front_map, map_offset + node_index, 0, keepdims=False
            )
            my_rank = (leaf_pos & group_span - 1) * front_size + front_pos
            row_ids = my_rank * upd_rows + jnp.arange(upd_rows)
            parent_block = lookup(map_row, row_ids // B)
            owners, position = target(parent_block * B + row_ids % B, parent_piv, parent_upd)
            buffer = (
                jnp.zeros((2 * group_size * stride, num_cols), jnp.float32)
                .at[owners * stride + position]
                .add(update)
            )
            for which_bit in reversed(range(level)):
                half_rows = buffer.shape[0] // 2
                upper_side = leaf_pos >> which_bit & 1 == 1
                kept = jnp.where(upper_side, buffer[half_rows:], buffer[:half_rows])
                given = jnp.where(upper_side, buffer[:half_rows], buffer[half_rows:])
                buffer = kept + swapped(given, "leaf", which_bit)
            shared = lax.psum_scatter(buffer, "front", scatter_dimension=0, tiled=True)
            upd_offset += upd_rows
            map_offset += leaf_size >> level - 1
        piv_offset += piv_rows
    return (flat_rows, jnp.concatenate(results, 0))


def solution(mesh):
    return jax.shard_map(
        per_device,
        mesh=mesh,
        in_specs=(
            P(("leaf", "front"), None),
            P(("leaf", "front"), None, None),
            P(("leaf", "front"), None, None, None),
            P(("leaf", "front"), None),
            P(("leaf", "front"), None),
            P(),
            P(("leaf", "front"), None),
            P(("leaf", "front"), None),
            P(("leaf", "front"), None),
            P(),
        ),
        out_specs=(P(("leaf", "front"), None), P(("leaf", "front"), None)),
        check_vma=False,
    )
```

profile of v0, /device:TPU:0, one launch (start us, length us, event | category | flops | bytes accessed | tf_op | source)
XLA Modules:
  0.0 706.4 jit_solution(16050703459151711307)
XLA Ops:
  9.8 249.8 %while.21 = (s32[]{:T(128)}, f32[24,128,128]{2,1,0:T(8,128)}, f32[24,128,128]{2,1,0:T(8,128)}, f32[24,128,128]{2,1,0:T(8,128)}, f32[23,2,128,128]{3,2,1,0:T(8,12...) while((s32[]{:T(128)}, f32[24,128,128]{2,1,0:T(8,128)}, ...), condition=%wide.region_2.3_spmd, body=%wide.region_0.2_spmd.sunk | while | flops 75546648 | bytes 788764 | solution.py:92
  18.3 2.3 fusion.151
  29.2 2.3 fusion.151
  40.0 2.3 fusion.151
  50.9 2.3 fusion.151
  61.8 2.3 fusion.151
  72.6 2.3 fusion.151
  83.5 2.3 fusion.151
  94.3 2.3 fusion.151
  105.2 2.3 fusion.151
  116.1 2.3 fusion.151
  126.9 2.3 fusion.151
  137.8 2.3 fusion.151
  159.5 2.3 fusion.151
  170.4 2.3 fusion.151
  192.1 2.3 fusion.151
  202.9 2.3 fusion.151
  224.7 2.3 fusion.151
  235.5 2.3 fusion.151
  246.4 2.3 fusion.151
  260.0 4.1 fusion.33
  264.0 9.1 %all_gather.24 = f32[1024,128]{0,1:T(8,128)} all-gather(f32[256,128]{0,1:T(8,128)S(1)} %fusion.33), channel_id=1, replica_groups=mesh['leaf'=8,'front'=4] {'front'}, dimensions={0}, use_global_device_ids=true | all-gather | bytes 655360 | tf_op jit(solution)/shard_map/all_gather | solution.py:99
  275.2 7.2 %scatter_custom_fusion = f32[1024,128]{1,0:T(8,128)} fusion(s32[1024]{0:T(1024)S(1)} %bitcast.105, f32[1024,128]{1,0:T(8,128)} %copy.36, f32[]{:T(128)} %constant.446.clone.1), kind=kCustom, calls=%fused_computation.104 | custom fusion | flops 131072 | bytes 524800 | tf_op jit(solution)/shard_map/scatter-add | solution.py:110
  284.3 17.7 %all-gather.3.cloned.1.call-done = f32[2048,128]{1,0:T(8,128)} async-done(((f32[512,128]{1,0:T(8,128)}), f32[2048,128]{1,0:T(8,128)}) %all-gather.3.cloned.1.call-update) | async-done | bytes 1048592 | tf_op jit(solution)/shard_map/all_gather | solution.py:48
  302.0 7.7 %fusion.24 = f32[512,128]{0,1:T(8,128)} fusion(f32[2048,128]{1,0:T(8,128)} %all-gather.3.cloned.1.call-done, f32[960,2048]{1,0:T(8,128)} %param.23), kind=kOutput, calls=%fused_computation.34 | convolution fusion | flops 1610612736 | bytes 5505024 | tf_op jit(solution)/shard_map/dot_general | solution.py:122
  311.7 14.9 %all-gather.5.cloned.1.call-done = f32[2048,128]{0,1:T(8,128)} async-done(((f32[512,128]{0,1:T(8,128)}), f32[2048,128]{0,1:T(8,128)}) %all-gather.5.cloned.1.call-update) | async-done | bytes 1048592 | tf_op jit(solution)/shard_map/all_gather | solution.py:48
  326.6 6.9 fusion.30
  334.3 4.1 scatter_custom_fusion.1
  338.4 3.0 fusion.132
  341.4 2.5 copy.54
  343.9 2.6 copy.53
  349.5 23.8 %collective-permute-done = f32[2048,128]{0,1:T(8,128)S(1)} collective-permute-done((f32[2048,128]{0,1:T(8,128)S(1)}, f32[2048,128]{0,1:T(8,128)S(1)}, u32[]{:S(2)}, u32[]{:S(2)}) %collective-permute-start) | collective-permute-done | bytes 1048608 | tf_op jit(solution)/shard_map/ppermute | solution.py:17
  374.7 24.9 %reduce-scatter.4.cloned.1.call-done = f32[512,128]{0,1:T(8,128)} async-done(((f32[2048,128]{0,1:T(8,128)}), f32[512,128]{0,1:T(8,128)}) %reduce-scatter.4.cloned.1.call-update) | async-done | bytes 262160 | tf_op jit(solution)/shard_map/reduce_scatter | solution.py:161
  400.5 7.2 %all_gather.27 = f32[1024,128]{0,1:T(8,128)} all-gather(f32[256,128]{0,1:T(8,128)S(1)} %slice_add_fusion.1), channel_id=1, replica_groups=mesh['leaf'=8,'front'=4] {'front'}, dimensions={0}, use_global_device_ids=true | all-gather | bytes 655360 | tf_op jit(solution)/shard_map/all_gather | solution.py:48
  409.2 13.0 %collective-permute-done.1 = f32[1024,128]{0,1:T(8,128)} collective-permute-done((f32[1024,128]{0,1:T(8,128)}, f32[1024,128]{0,1:T(8,128)}, u32[]{:S(2)}, u32[]{:S(2)}) %collective-permute-start.1) | collective-permute-done | bytes 524320 | tf_op jit(solution)/shard_map/ppermute | solution.py:17
  422.2 4.5 fusion.34
  426.7 6.8 all_gather.28
  435.1 12.6 %collective-permute-done.2 = f32[1024,128]{0,1:T(8,128)S(1)} collective-permute-done((f32[1024,128]{0,1:T(8,128)S(1)}, f32[1024,128]{0,1:T(8,128)S(1)}, u32[]{:S(2)}, u32[]{:S(2)}) %collective-permute-start.2) | collective-permute-done | bytes 524320 | tf_op jit(solution)/shard_map/ppermute | solution.py:17
  447.7 3.8 slice_subtract_fusion
  451.6 2.8 scatter_custom_fusion.2
  454.5 3.0 fusion.131
  457.4 2.5 copy.57
  460.0 2.6 copy.56
  465.6 23.1 %collective-permute-done.3 = f32[2048,128]{0,1:T(8,128)S(1)} collective-permute-done((f32[2048,128]{0,1:T(8,128)S(1)}, f32[2048,128]{0,1:T(8,128)S(1)}, u32[]{:S(2)}, u32[]{:S(2)}) %collective-permute-start.3) | collective-permute-done | bytes 1048608 | tf_op jit(solution)/shard_map/ppermute | solution.py:17
  490.5 11.0 %collective-permute-done.4 = f32[1024,128]{0,1:T(8,128)S(1)} collective-permute-done((f32[1024,128]{0,1:T(8,128)S(1)}, f32[1024,128]{0,1:T(8,128)S(1)}, u32[]{:S(2)}, u32[]{:S(2)}) %collective-permute-start.4) | collective-permute-done | bytes 524320 | tf_op jit(solution)/shard_map/ppermute | solution.py:17
  502.6 22.2 %reduce-scatter.6.cloned.1.call-done = f32[256,128]{0,1:T(8,128)} async-done(((f32[1024,128]{0,1:T(8,128)}), f32[256,128]{0,1:T(8,128)}) %reduce-scatter.6.cloned.1.call-update) | async-done | bytes 131088 | tf_op jit(solution)/shard_map/reduce_scatter | solution.py:161
  525.7 5.8 all_gather.29
  532.9 7.1 %collective-permute-done.5 = f32[512,128]{0,1:T(8,128)S(1)} collective-permute-done((f32[512,128]{0,1:T(8,128)S(1)}, f32[512,128]{0,1:T(8,128)S(1)}, u32[]{:S(2)}, u32[]{:S(2)}) %collective-permute-start.5) | collective-permute-done | bytes 262176 | tf_op jit(solution)/shard_map/ppermute | solution.py:17
  541.6 11.9 %collective-permute-done.6 = f32[1024,128]{0,1:T(8,128)S(1)} collective-permute-done((f32[1024,128]{0,1:T(8,128)S(1)}, f32[1024,128]{0,1:T(8,128)S(1)}, u32[]{:S(2)}, u32[]{:S(2)}) %collective-permute-start.6) | collective-permute-done | bytes 524320 | tf_op jit(solution)/shard_map/ppermute | solution.py:17
  555.8 5.8 all_gather.30
  563.0 7.1 %collective-permute-done.7 = f32[512,128]{0,1:T(8,128)S(1)} collective-permute-done((f32[512,128]{0,1:T(8,128)S(1)}, f32[512,128]{0,1:T(8,128)S(1)}, u32[]{:S(2)}, u32[]{:S(2)}) %collective-permute-start.7) | collective-permute-done | bytes 262176 | tf_op jit(solution)/shard_map/ppermute | solution.py:17
  572.6 12.1 %collective-permute-done.8 = f32[1024,128]{0,1:T(8,128)} collective-permute-done((f32[1024,128]{0,1:T(8,128)}, f32[1024,128]{0,1:T(8,128)}, u32[]{:S(2)}, u32[]{:S(2)}) %collective-permute-start.8) | collective-permute-done | bytes 524320 | tf_op jit(solution)/shard_map/ppermute | solution.py:17
  584.6 2.9 slice_subtract_fusion.1
  591.0 2.5 collective-permute-start.9
  593.5 22.2 %collective-permute-done.9 = f32[1024,128]{1,0:T(8,128)S(1)} collective-permute-done((f32[1024,128]{1,0:T(8,128)S(1)}, f32[1024,128]{1,0:T(8,128)S(1)}, u32[]{:S(2)}, u32[]{:S(2)}) %collective-permute-start.9) | collective-permute-done | bytes 524320 | tf_op jit(solution)/shard_map/ppermute | solution.py:17
  616.3 6.7 collective-permute-done.10
  624.7 3.5 collective-permute-done.11
  628.9 20.7 %reduce-scatter.8.cloned.1.call-done = f32[64,128]{1,0:T(8,128)} async-done(((f32[256,128]{1,0:T(8,128)}), f32[64,128]{1,0:T(8,128)}) %reduce-scatter.8.cloned.1.call-update) | async-done | bytes 32784 | tf_op jit(solution)/shard_map/reduce_scatter | solution.py:161
  650.4 5.4 all_gather.31
  657.3 4.3 collective-permute-done.12
  663.1 6.3 collective-permute-done.13
  669.4 2.5 collective-permute-start.14
  671.9 22.2 %collective-permute-done.14 = f32[1024,128]{1,0:T(8,128)S(1)} collective-permute-done((f32[1024,128]{1,0:T(8,128)S(1)}, f32[1024,128]{1,0:T(8,128)S(1)}, u32[]{:S(2)}, u32[]{:S(2)}) %collective-permute-start.14) | collective-permute-done | bytes 524320 | tf_op jit(solution)/shard_map/ppermute | solution.py:17
  694.1 2.8 convolution_bitcast_fusion.1
  (197 shorter events, 170.6 us)
Async XLA Ops:
  7.2 252.8 %copy-start = (f32[256,3072]{1,0:T(8,128)S(1)}, f32[256,3072]{1,0:T(8,128)}, u32[]{:S(2)}) copy-start(f32[256,3072]{1,0:T(8,128)} %param.20) | copy-start | bytes 9437188
  7.2 294.9 %all-gather.3.cloned.1.call-start = ((), (), s32[]{:S(2)}) async-start(), calls=%async_computation.3 | async-start | bytes 1310720 | tf_op jit(solution)/shard_map/all_gather | solution.py:48
  9.8 249.8 %copy-start.10 = (s32[32,2]{0,1:T(2,128)S(1)}, s32[32,2]{0,1:T(2,128)}, u32[]{:S(2)}) copy-start(s32[32,2]{0,1:T(2,128)} %param.21) | copy-start | bytes 772
  284.3 42.3 %all-gather.5.cloned.1.call-start = ((), (), s32[]{:S(2)}) async-start(), calls=%async_computation.4 | async-start | bytes 1310720 | tf_op jit(solution)/shard_map/all_gather | solution.py:48
  309.7 89.9 %reduce-scatter.4.cloned.1.call-start = ((), (), s32[]{:S(2)}) async-start(), calls=%async_computation.5 | async-start | bytes 1310720 | tf_op jit(solution)/shard_map/reduce_scatter | solution.py:161
  346.5 26.9 %copy-start.1 = (f32[2048,128]{0,1:T(8,128)S(1)}, f32[2048,128]{0,1:T(8,128)}, u32[]{:S(2)}) copy-start(f32[2048,128]{0,1:T(8,128)} %copy.54) | copy-start | bytes 3145732
  346.5 26.9 %copy-start.4 = (f32[2048,128]{0,1:T(8,128)S(1)}, f32[2048,128]{0,1:T(8,128)}, u32[]{:S(2)}) copy-start(f32[2048,128]{0,1:T(8,128)} %copy.53) | copy-start | bytes 3145732
  348.0 26.6 %slice-start = ((f32[960,128]{1,0:T(8,128)}), f32[256,128]{1,0:T(8,128)S(1)}, s32[]{:S(2)}) async-start(f32[960,128]{1,0:T(8,128)} %param.22), calls=%async_computation.8 | async-start | bytes 262144 | tf_op jit(solution)/shard_map/slice | solution.py:120
  348.0 25.4 %collective-permute-start = (f32[2048,128]{0,1:T(8,128)S(1)}, f32[2048,128]{0,1:T(8,128)S(1)}, u32[]{:S(2)}, u32[]{:S(2)}) collective-permute-start(f32[2048,128]{0,1:T(8,128)S(1)} %broadcast_select_fusion.1), channel_id=1, source_target_pairs={{0,4},{4,0},{8,12},{12,8},{16,20},{20,16},{24,28},{28,24},{1,5},{5... | collective-permute-start | bytes 3145736 | tf_op jit(solution)/shard_map/ppermute | solution.py:17
  374.5 150.3 %reduce-scatter.6.cloned.1.call-start = ((), (), s32[]{:S(2)}) async-start(), calls=%async_computation.6 | async-start | bytes 655360 | tf_op jit(solution)/shard_map/reduce_scatter | solution.py:161
  407.7 14.5 %collective-permute-start.1 = (f32[1024,128]{0,1:T(8,128)}, f32[1024,128]{0,1:T(8,128)}, u32[]{:S(2)}, u32[]{:S(2)}) collective-permute-start(f32[1024,128]{0,1:T(8,128)} %all_gather.27), channel_id=1, source_target_pairs={{0,4},{4,0},{8,12},{12,8},{16,20},{20,16},{24,28},{28,24},{1,5},{5... | collective-permute-start | bytes 1572872 | tf_op jit(solution)/shard_map/ppermute | solution.py:17
  433.5 14.2 %collective-permute-start.2 = (f32[1024,128]{0,1:T(8,128)S(1)}, f32[1024,128]{0,1:T(8,128)S(1)}, u32[]{:S(2)}, u32[]{:S(2)}) collective-permute-start(f32[1024,128]{0,1:T(8,128)S(1)} %all_gather.28), channel_id=1, source_target_pairs={{0,4},{4,0},{8,12},{12,8},{16,20},{20,16},{24,28},{28,24},{1,5},{5... | collective-permute-start | bytes 1572872 | tf_op jit(solution)/shard_map/ppermute | solution.py:17
  462.5 26.2 %copy-start.2 = (f32[2048,128]{0,1:T(8,128)S(1)}, f32[2048,128]{0,1:T(8,128)}, u32[]{:S(2)}) copy-start(f32[2048,128]{0,1:T(8,128)} %copy.57) | copy-start | bytes 3145732
  462.5 26.2 %copy-start.5 = (f32[2048,128]{0,1:T(8,128)S(1)}, f32[2048,128]{0,1:T(8,128)}, u32[]{:S(2)}) copy-start(f32[2048,128]{0,1:T(8,128)} %copy.56) | copy-start | bytes 3145732
  464.0 24.7 %collective-permute-start.3 = (f32[2048,128]{0,1:T(8,128)S(1)}, f32[2048,128]{0,1:T(8,128)S(1)}, u32[]{:S(2)}, u32[]{:S(2)}) collective-permute-start(f32[2048,128]{0,1:T(8,128)S(1)} %broadcast_select_fusion), channel_id=1, source_target_pairs={{0,8},{4,12},{8,0},{12,4},{16,24},{20,28},{24,16},{28,20},{1,9},{5... | collective-permute-start | bytes 3145736 | tf_op jit(solution)/shard_map/ppermute | solution.py:17
  488.9 13.6 %slice-start.1 = ((f32[960,128]{1,0:T(8,128)}), f32[128,128]{1,0:T(8,128)S(1)}, s32[]{:S(2)}) async-start(f32[960,128]{1,0:T(8,128)} %param.22), calls=%async_computation.9 | async-start | bytes 131072 | tf_op jit(solution)/shard_map/slice | solution.py:120
  489.0 12.5 %collective-permute-start.4 = (f32[1024,128]{0,1:T(8,128)S(1)}, f32[1024,128]{0,1:T(8,128)S(1)}, u32[]{:S(2)}, u32[]{:S(2)}) collective-permute-start(f32[1024,128]{0,1:T(8,128)S(1)} %slice_select_fusion.1), channel_id=1, source_target_pairs={{0,4},{4,0},{8,12},{12,8},{16,20},{20,16},{24,28},{28,24},{1,5},{5... | collective-permute-start | bytes 1572872 | tf_op jit(solution)/shard_map/ppermute | solution.py:17
  502.4 147.1 %reduce-scatter.8.cloned.1.call-start = ((), (), s32[]{:S(2)}) async-start(), calls=%async_computation.7 | async-start | bytes 163840 | tf_op jit(solution)/shard_map/reduce_scatter | solution.py:161
  531.4 8.6 %collective-permute-start.5 = (f32[512,128]{0,1:T(8,128)S(1)}, f32[512,128]{0,1:T(8,128)S(1)}, u32[]{:S(2)}, u32[]{:S(2)}) collective-permute-start(f32[512,128]{0,1:T(8,128)S(1)} %all_gather.29), channel_id=1, source_target_pairs={{0,4},{4,0},{8,12},{12,8},{16,20},{20,16},{24,28},{28,24},{1,5},{5... | collective-permute-start | bytes 786440 | tf_op jit(solution)/shard_map/ppermute | solution.py:17
  540.0 44.6 %copy-start.9 = (f32[256,128]{0,1:T(8,128)S(1)}, f32[256,128]{0,1:T(8,128)}, u32[]{:S(2)}) copy-start(f32[256,128]{0,1:T(8,128)} %reduce-scatter.6.cloned.1.call-done) | copy-start | bytes 393220
  540.0 13.4 %collective-permute-start.6 = (f32[1024,128]{0,1:T(8,128)S(1)}, f32[1024,128]{0,1:T(8,128)S(1)}, u32[]{:S(2)}, u32[]{:S(2)}) collective-permute-start(f32[1024,128]{0,1:T(8,128)S(1)} %maximum_select_fusion.10), channel_id=1, source_target_pairs={{0,8},{4,12},{8,0},{12,4},{16,24},{20,28},{24,16},{28,20},{1,9},{5... | collective-permute-start | bytes 1572872 | tf_op jit(solution)/shard_map/ppermute | solution.py:17
  555.8 15.2 %copy-start.7 = (f32[128,128]{0,1:T(8,128)}, f32[128,128]{0,1:T(8,128)S(1)}, u32[]{:S(2)}) copy-start(f32[128,128]{0,1:T(8,128)S(1)} %convolution_bitcast_fusion.3) | copy-start | bytes 196612
  561.6 8.6 %collective-permute-start.7 = (f32[512,128]{0,1:T(8,128)S(1)}, f32[512,128]{0,1:T(8,128)S(1)}, u32[]{:S(2)}, u32[]{:S(2)}) collective-permute-start(f32[512,128]{0,1:T(8,128)S(1)} %all_gather.30), channel_id=1, source_target_pairs={{0,4},{4,0},{8,12},{12,8},{16,20},{20,16},{24,28},{28,24},{1,5},{5... | collective-permute-start | bytes 786440 | tf_op jit(solution)/shard_map/ppermute | solution.py:17
  571.0 13.7 %collective-permute-start.8 = (f32[1024,128]{0,1:T(8,128)}, f32[1024,128]{0,1:T(8,128)}, u32[]{:S(2)}, u32[]{:S(2)}) collective-permute-start(f32[1024,128]{0,1:T(8,128)} %maximum_select_fusion.11), channel_id=1, source_target_pairs={{0,8},{4,12},{8,0},{12,4},{16,24},{20,28},{24,16},{28,20},{1,9},{5... | collective-permute-start | bytes 1572872 | tf_op jit(solution)/shard_map/ppermute | solution.py:17
  589.6 26.0 %copy-start.3 = (f32[2048,128]{1,0:T(8,128)S(1)}, f32[2048,128]{1,0:T(8,128)}, u32[]{:S(2)}) copy-start(f32[2048,128]{1,0:T(8,128)} %scatter_custom_fusion.3) | copy-start | bytes 3145732
  591.0 24.7 %collective-permute-start.9 = (f32[1024,128]{1,0:T(8,128)S(1)}, f32[1024,128]{1,0:T(8,128)S(1)}, u32[]{:S(2)}, u32[]{:S(2)}) collective-permute-start(f32[1024,128]{1,0:T(8,128)S(1)} %slice_select_fusion), channel_id=1, source_target_pairs={{0,16},{4,20},{8,24},{12,28},{16,0},{20,4},{24,8},{28,12},{1,17},{... | collective-permute-start | bytes 1572872 | tf_op jit(solution)/shard_map/ppermute | solution.py:17
  615.8 7.3 %collective-permute-start.10 = (f32[512,128]{1,0:T(8,128)S(1)}, f32[512,128]{1,0:T(8,128)S(1)}, u32[]{:S(2)}, u32[]{:S(2)}) collective-permute-start(f32[512,128]{1,0:T(8,128)S(1)} %slice_select_fusion.2), channel_id=1, source_target_pairs={{0,8},{4,12},{8,0},{12,4},{16,24},{20,28},{24,16},{28,20},{1,9},{5... | collective-permute-start | bytes 786440 | tf_op jit(solution)/shard_map/ppermute | solution.py:17
  623.2 5.0 collective-permute-start.11
  628.9 68.1 %copy-start.6 = (f32[512,128]{0,1:T(8,128)S(1)}, f32[512,128]{0,1:T(8,128)}, u32[]{:S(2)}) copy-start(f32[512,128]{0,1:T(8,128)} %fusion.24) | copy-start | bytes 786436
  649.6 47.4 %copy-start.8 = (f32[128,128]{0,1:T(8,128)S(1)}, f32[128,128]{0,1:T(8,128)}, u32[]{:S(2)}) copy-start(f32[128,128]{0,1:T(8,128)} %copy-done.7) | copy-start | bytes 196612
  655.8 5.7 collective-permute-start.12
  661.6 7.8 %collective-permute-start.13 = (f32[512,128]{1,0:T(8,128)S(1)}, f32[512,128]{1,0:T(8,128)S(1)}, u32[]{:S(2)}, u32[]{:S(2)}) collective-permute-start(f32[512,128]{1,0:T(8,128)S(1)} %maximum_select_fusion.13), channel_id=1, source_target_pairs={{0,8},{4,12},{8,0},{12,4},{16,24},{20,28},{24,16},{28,20},{1,9},{5... | collective-permute-start | bytes 786440 | tf_op jit(solution)/shard_map/ppermute | solution.py:17
  669.4 24.7 %collective-permute-start.14 = (f32[1024,128]{1,0:T(8,128)S(1)}, f32[1024,128]{1,0:T(8,128)S(1)}, u32[]{:S(2)}, u32[]{:S(2)}) collective-permute-start(f32[1024,128]{1,0:T(8,128)S(1)} %maximum_select_fusion.12), channel_id=1, source_target_pairs={{0,16},{4,20},{8,24},{12,28},{16,0},{20,4},{24,8},{28,12},{1,17},{... | collective-permute-start | bytes 1572872 | tf_op jit(solution)/shard_map/ppermute | solution.py:17
Sparse Core Ops, SparseCore 0:
  284.4 17.5 all-gather.2
  309.8 16.7 all-gather.4
  374.6 24.9 reduce-scatter.3
  502.6 22.1 reduce-scatter.5
  629.0 20.5 reduce-scatter.7
where the time goes:
time: 713 us; the launch traced here: 706 us
  waiting for transfers between devices  287 us (40%)
  matrix products  140 us (20%)
  loops' own time  82.1 us (12%)
  other arithmetic  62.4 us (9%)
  local copies, waits for them, and re-layouts  55.9 us (8%)
  blocking collectives  40.1 us (6%)
  starting transfers between devices  24 us (3%)
  between operations  14.1 us (2%)
    ppermute x15, waiting for transfers between devices, swapped(): return lax.ppermute(value, axis, pairs)  187 us
    another operation x1, loops' own time, per_device(): solved = lax.fori_loop(1, SB, advance, solved)  82.1 us
    reduce_scatter x3, waiting for transfers between devices, per_device(): shared = lax.psum_scatter(buffer, 'front', scatter_dimension=0, tiled=True)  67.8 us
    dot_general x23, matrix products, advance(): jnp.dot(sub_dinv[block_id], remain, precision=highest, preferred_element_...  53.9 us
    dot_general x46, matrix products, advance(): jnp.dot(sub_off[block_id - 1, which], solved[sub_pattern[block_id - 1, wh...  50.5 us
    all_gather x2, waiting for transfers between devices, group_gather(): gathered = lax.all_gather(local_rows, 'front', axis=0, tiled=True)  32.6 us
    another operation x23, other arithmetic  32.1 us
    dynamic_slice x23, local copies, waits for them, and re-layouts, advance(): sub_pattern[block_id - 1, which]  31.2 us
  transfers between devices with their start and end apart: 20, of which 20 were waited for; matrix products, arithmetic and copies ran while one was open for 0% of the time, Pallas kernels for 0%

commit v1 on v0

v1 whole, which is shorter than its diff:
```python
import functools

import jax
import jax.numpy as jnp
from jax import lax
from jax.experimental import pallas as pl
from jax.experimental.pallas import tpu as pltpu
from jax.sharding import PartitionSpec as P

AXES = ("leaf", "front")
B = 128
BF16 = jnp.bfloat16
F32 = jnp.float32
VMEM = pl.BlockSpec(memory_space=pltpu.VMEM)
SMEM = pl.BlockSpec(memory_space=pltpu.SMEM)
MIB = 2**20


def halves(x):
    high = x.astype(BF16)
    return high, (x - high.astype(F32)).astype(BF16)


def tall(x):
    return jnp.concatenate(halves(x), 0)


def wide(x):
    return jnp.concatenate(halves(x), 1)


def product(left, right):
    both = jnp.dot(left, right, preferred_element_type=F32)
    rows, cols = left.shape[0] // 2, right.shape[1] // 2
    return both[:rows, :cols] + both[:rows, cols:] + both[rows:, :cols]


def subtree_kernel(pattern, rhs, dinv, off, upd, y, w, coef, lead, solved):
    count = dinv.shape[0]

    def put(i, value):
        rows = pl.ds(i * B, B)
        y[rows, :] = value
        solved[rows, :] = wide(value)

    def prepare(i):
        right = jnp.concatenate([off[i - 1, 0], off[i - 1, 1], rhs[pl.ds(i * B, B), :]], 1)
        out = product(tall(dinv[i]), wide(right))
        lead[i] = out[:, 2 * B :]
        coef[i] = tall(-out[:, : 2 * B])

    def step(i):
        first = pl.multiple_of(pattern[i - 1, 0] * B, B)
        second = pl.multiple_of(pattern[i - 1, 1] * B, B)
        known = jnp.concatenate([solved[pl.ds(first, B), :], solved[pl.ds(second, B), :]], 0)
        put(i, lead[i] + product(coef[i], known))

    put(0, product(tall(dinv[0]), wide(rhs[:B, :])))
    prepare(1)
    for i in range(1, count):
        if i + 1 < count:
            prepare(i + 1)
        step(i)
    w[...] = -product(tall(upd[...]), solved[...])


def solve_subtree(rhs, dinv, off, pattern, upd):
    count = dinv.shape[0]
    return pl.pallas_call(
        subtree_kernel,
        out_shape=(
            jax.ShapeDtypeStruct(rhs.shape, F32),
            jax.ShapeDtypeStruct((upd.shape[0], rhs.shape[1]), F32),
        ),
        in_specs=[SMEM, VMEM, VMEM, VMEM, VMEM],
        out_specs=(VMEM, VMEM),
        scratch_shapes=[
            pltpu.VMEM((count, 2 * B, 2 * B), BF16),
            pltpu.VMEM((count, B, B), F32),
            pltpu.VMEM((count * B, 2 * B), BF16),
        ],
        compiler_params=pltpu.CompilerParams(vmem_limit_bytes=40 * MIB),
        cost_estimate=pl.CostEstimate(flops=2 * 10**9, bytes_accessed=12 * 10**6, transcendentals=0),
        name="subtree",
    )(pattern, rhs, dinv, off, upd)


def exchange(x, mask):
    size = lax.axis_size("leaf") * lax.axis_size("front")
    return lax.ppermute(x, AXES, [(source, source ^ mask) for source in range(size)])


def spread(x, group):
    masks = [0]
    apart = group // 2
    while apart >= 16:
        x = jnp.concatenate([x, exchange(x, apart)], 0)
        masks = masks + [mask ^ apart for mask in masks]
        apart //= 2
    low = 2 * apart
    arrays = [(0, x)]
    for mask in range(low - 2, 0, -2):
        arrays.append((mask, exchange(x, mask)))
    arrays += [(mask ^ 1, exchange(array, 1)) for mask, array in arrays]
    return [(array, [mask ^ high for high in masks]) for mask, array in arrays]


def pivot_kernel(masks, shape, me, maps, *refs):
    count = len(masks)
    pieces = refs[:count]
    h, factor = refs[count : count + 2]
    earlier = refs[count + 2 : count + 2 + shape["earlier"]]
    rest = refs[count + 2 + shape["earlier"] :]
    front = shape["front"]
    p_size, child_rows, span = shape["p_size"], shape["child_rows"], shape["child_span"]
    upd_rows = shape["upd_rows"]
    device = me[0]
    frontal, right = rest[-2:]
    frontal[:p_size, :] = h[...]
    if upd_rows:
        frontal[p_size:, :] = jnp.zeros_like(frontal[p_size:, :])
    step = min(child_rows, B)
    for piece, piece_masks in zip(pieces, masks, strict=True):
        for part, mask in enumerate(piece_masks):
            source = jnp.bitwise_xor(device, mask)
            if span:
                leaf = source // front
                row_of_map = shape["map_offset"] + leaf // span
                offset = (lax.rem(leaf, span) * front + lax.rem(source, front)) * child_rows
            else:
                row_of_map, offset = source, 0
            for at in range(0, child_rows, step):
                row = offset + at
                target = maps[row_of_map, row // B] * B + lax.rem(row, B)
                where = pl.ds(pl.multiple_of(target, 8), step)
                here = part * child_rows + at
                frontal[where, :] += piece[here : here + step, :]
    right[...] = wide(frontal[:p_size, :])
    z = product(tall(factor[...]), right[...])
    if shape["earlier"]:
        at = 0
        for array in earlier:
            rest[0][at : at + array.shape[0], :] = array[...]
            at += array.shape[0]
        rest[0][at : at + z.shape[0], :] = z
    else:
        rest[0][...] = z
    if upd_rows:
        group_mask = shape["group"] - 1
        rank = jnp.bitwise_and(device, group_mask)
        rest[1][...] = frontal[pl.ds(pl.multiple_of(p_size + rank * upd_rows, 8), upd_rows), :]


def solve_pivots(me, maps, pieces, h, factor, block, earlier, **shape):
    rows = block[1]
    columns = h.shape[1]
    p_size = h.shape[0]
    upd_rows = shape["upd_rows"]
    shape |= {"p_size": p_size, "earlier": len(earlier)}
    total = rows + sum(array.shape[0] for array in earlier)
    outs = [jax.ShapeDtypeStruct((total, columns), F32)]
    if upd_rows:
        outs.append(jax.ShapeDtypeStruct((upd_rows, columns), F32))
    frontal_rows = p_size + upd_rows * shape["group"]
    return pl.pallas_call(
        functools.partial(pivot_kernel, [masks for _, masks in pieces], shape),
        grid=(1,),
        out_shape=tuple(outs),
        in_specs=[SMEM, SMEM]
        + [VMEM] * (len(pieces) + 1)
        + [pl.BlockSpec((rows, p_size), lambda i: (block[0], 0))]
        + [VMEM] * len(earlier),
        out_specs=tuple(VMEM for _ in outs),
        scratch_shapes=[
            pltpu.VMEM((frontal_rows, columns), F32),
            pltpu.VMEM((p_size, 2 * columns), BF16),
        ],
        compiler_params=pltpu.CompilerParams(vmem_limit_bytes=40 * MIB),
        cost_estimate=pl.CostEstimate(
            flops=2 * rows * p_size * columns * 3, bytes_accessed=8 * 10**6, transcendentals=0
        ),
        name="pivots",
    )(me, maps, *[array for array, _ in pieces], h, factor, *earlier)


def update_kernel(masks, group, me, *refs):
    count = len(masks)
    pieces = refs[:count]
    side, factor, w, right = refs[count:]
    rank = jnp.bitwise_and(me[0], group - 1)
    for piece, piece_masks in zip(pieces, masks, strict=True):
        rows = piece.shape[0] // len(piece_masks)
        for part, mask in enumerate(piece_masks):
            source = jnp.bitwise_xor(rank, mask)
            where = pl.ds(pl.multiple_of(source * rows, 16), rows)
            right[where, :] = wide(piece[part * rows : (part + 1) * rows, :])
    w[...] = side[...] - product(tall(factor[...]), right[...])


def solve_update(me, pieces, side, factor, block, group):
    rows = block[1]
    columns = side.shape[1]
    p_size = factor.shape[1]
    return pl.pallas_call(
        functools.partial(update_kernel, [masks for _, masks in pieces], group),
        grid=(1,),
        out_shape=jax.ShapeDtypeStruct((rows, columns), F32),
        in_specs=[SMEM]
        + [VMEM] * (len(pieces) + 1)
        + [pl.BlockSpec((rows, p_size), lambda i: (block[0], 0))],
        out_specs=VMEM,
        scratch_shapes=[pltpu.VMEM((p_size, 2 * columns), BF16)],
        compiler_params=pltpu.CompilerParams(vmem_limit_bytes=40 * MIB),
        cost_estimate=pl.CostEstimate(
            flops=2 * rows * p_size * columns * 3, bytes_accessed=8 * 10**6, transcendentals=0
        ),
        name="update",
    )(me, *[array for array, _ in pieces], side, factor)


def per_device(
    sub_rhs,
    sub_dinv,
    sub_off,
    sub_pattern,
    sub_update,
    sub_map,
    front_rhs,
    piv_inverse,
    upd_factor,
    front_map,
):
    front_size = lax.axis_size("front")
    leaf_size = lax.axis_size("leaf")
    level_count = leaf_size.bit_length()
    p_size = piv_inverse.shape[1]
    u_size = upd_factor.shape[0] * front_size * leaf_size // (2 * (leaf_size - 1))
    me = (lax.axis_index("leaf") * front_size + lax.axis_index("front")).reshape(1)

    known = []
    offset = 0
    for level in range(1, level_count + 1):
        group = front_size * 2 ** (level - 1)
        rows = p_size // group
        mine = front_rhs[offset : offset + rows]
        groups = [
            list(range(first, first + group))
            for first in range(0, front_size * leaf_size, group)
        ]
        known.append(lax.all_gather(mine, AXES, axis=0, tiled=True, axis_index_groups=groups))
        offset += rows

    flat, update = solve_subtree(sub_rhs, sub_dinv, sub_off, sub_pattern, sub_update)
    pieces = spread(update, front_size)
    maps, map_offset, child_span = sub_map, 0, 0
    earlier = []
    for level in range(1, level_count + 1):
        group = front_size * 2 ** (level - 1)
        rows = p_size // group
        last = level == level_count
        out = solve_pivots(
            me,
            maps,
            pieces,
            known[level - 1],
            piv_inverse,
            (2**level - 2, rows),
            earlier if last else [],
            front=front_size,
            child_rows=update.shape[0],
            child_span=child_span,
            map_offset=map_offset,
            upd_rows=0 if last else u_size // group,
            group=group,
        )
        if last:
            return flat, out[0]
        z, side = out
        earlier.append(z)
        z_pieces = spread(z, group)
        update = solve_update(me, z_pieces, side, upd_factor, (2**level - 2, u_size // group), group)
        pieces = spread(update, 2 * group)
        map_offset = 0 if level == 1 else map_offset + leaf_size // child_span
        child_span = 2 ** (level - 1)
        maps = front_map


def solution(mesh):
    split = P(AXES)
    return jax.shard_map(
        per_device,
        mesh=mesh,
        in_specs=(split, split, split, split, split, P(), split, split, split, P()),
        out_specs=(split, split),
        check_vma=False,
    )
```

time: 713 us -> 182 us (0.26)
  waiting for transfers between devices: 287 us -> 59.5 us
  matrix products: 140 us -> 0 us
  loops' own time: 82.1 us -> 0 us
  other arithmetic: 62.4 us -> 0.01 us
  blocking collectives: 40.1 us -> 0 us
  starting transfers between devices: 24 us -> 49.2 us
  Pallas kernels: 0 us -> 19.8 us
  local copies, waits for them, and re-layouts: 55.9 us -> 38.5 us
    dot_general x78 -> x0, matrix products: 140 us -> none  [the longest x23 53.9 us: advance(): jnp.dot(sub_dinv[block_id], remain, precision=highest, preferred_element_...]
    ppermute x15 -> x66, waiting for transfers between devices: 187 us -> 59.4 us  [exchange(): lax.ppermute(x, AXES, [(source, source ^ mask) for source in range(size)])]
    another operation x1 -> x0, loops' own time: 82.1 us -> none  [per_device(): solved = lax.fori_loop(1, SB, advance, solved)]
    reduce_scatter x3 -> x0, waiting for transfers between devices: 67.8 us -> none  [per_device(): shared = lax.psum_scatter(buffer, 'front', scatter_dimension=0, tiled=True)]
    all_gather x6 -> x0, blocking collectives: 40.1 us -> none  [the longest x5 31.1 us: group_gather(): gathered = lax.all_gather(local_rows, 'front', axis=0, tiled=True)]
    all_gather x2 -> x4, waiting for transfers between devices: 32.6 us -> 0.01 us  [per_device(): lax.all_gather(mine, AXES, axis=0, tiled=True, axis_index_groups=groups)]
    another operation x23 -> x0, other arithmetic: 32.1 us -> none
    dynamic_slice x25 -> x0, local copies, waits for them, and re-layouts: 31.4 us -> none  [the longest x23 31.2 us: advance(): sub_pattern[block_id - 1, which]]
  transfers between devices with their start and end apart: 20 -> 70, of which waited for: 20 -> 43; matrix products, arithmetic and copies ran while one was open for 0% -> 3% of each run, Pallas kernels for 0% -> 10%
where the time goes in v1:
time: 182 us; the launch traced here: 181 us
  waiting for transfers between devices  59.5 us (33%)
  starting transfers between devices  49.2 us (27%)
  local copies, waits for them, and re-layouts  38.5 us (21%)
  Pallas kernels  19.8 us (11%)
  between operations  13.9 us (8%)
    ppermute x66, waiting for transfers between devices, exchange(): lax.ppermute(x, AXES, [(source, source ^ mask) for source in range(size)])  59.4 us
    ppermute x66, starting transfers between devices, exchange(): lax.ppermute(x, AXES, [(source, source ^ mask) for source in range(size)])  49 us
    unnamed x40, local copies, waits for them, and re-layouts  32.4 us
    pallas_call x4, Pallas kernels, solve_pivots(): pl.pallas_call(functools.partial(pivot_kernel, [masks for _, masks in pie...  8.46 us
    pallas_call x1, Pallas kernels, solve_subtree(): pl.pallas_call(subtree_kernel, out_shape=(jax.ShapeDtypeStruct(rhs.shape,...  8.1 us
    slice x4, local copies, waits for them, and re-layouts, per_device(): mine = front_rhs[offset:offset + rows]  6.09 us
  transfers between devices with their start and end apart: 70, of which 43 were waited for; matrix products, arithmetic and copies ran while one was open for 3% of the time, Pallas kernels for 10%

profile of v1, /device:TPU:0, one launch (start us, length us, event | category | flops | bytes accessed | tf_op | source)
XLA Modules:
  0.0 180.9 jit_solution(6584010566682474991)
XLA Ops:
  7.2 1.7 slice.12
  9.0 1.6 slice.13
  10.6 1.5 slice.14
  12.9 1.9 %copy-done.6 = f32[256,3072]{1,0:T(8,128)S(1)} copy-done((f32[256,3072]{1,0:T(8,128)S(1)}, f32[256,3072]{1,0:T(8,128)}, u32[]{:S(2)}) %copy-start.6) | copy-done | bytes 3145752
  14.8 1.9 %copy-done.7 = f32[23,2,128,128]{3,2,1,0:T(8,128)S(1)} copy-done((f32[23,2,128,128]{3,2,1,0:T(8,128)S(1)}, f32[23,2,128,128]{3,2,1,0:T(8,128)}, u32[]{:S(2)}) %copy-start.7) | copy-done | bytes 3014680
  16.7 1.4 copy-done.8
  18.1 1.5 copy-done.9
  19.5 8.1 %subtree.1 = (f32[3072,128]{1,0:T(8,128)}, f32[256,128]{1,0:T(8,128)S(1)}) custom-call(s32[23,2]{1,0:T(8,128)S(1)} %copy.12.pattern, f32[3072,128]{1,0:T(8,128)S(1)} %copy-done.8, f32[24,128,128]{2,1,0:T(8,128)S(1)} %copy-done.9, f32[23,2,128,128]{3,2,1,0:T(8,128)S(1)} %copy-done.7, f32[256,3072]{1,0:T(8,128)S(1)} %copy-done.6), custom_call_target="tpu_custom_call" | custom-call | flops 2000000000 | bytes 12000000 | tf_op jit(solution)/shard_map/subtree/pallas_call | solution.py:69
  27.6 3.0 %collective-permute-start = (f32[256,128]{1,0:T(8,128)S(1)}, f32[256,128]{1,0:T(8,128)S(1)}, u32[]{:S(2)}, u32[]{:S(2)}) collective-permute-start(f32[256,128]{1,0:T(8,128)S(1)} %get-tuple-element.11.refs_0_), channel_id=1, source_target_pairs={{0,2},{1,3},{2,0},{3,1},{4,6},{5,7},{6,4},{7,5},{8,10},{9,11},{10,... | collective-permute-start | bytes 393224 | tf_op jit(solution)/shard_map/ppermute | solution.py:90
  30.6 3.5 %collective-permute-done.refs_1_ = f32[256,128]{1,0:T(8,128)S(1)} collective-permute-done((f32[256,128]{1,0:T(8,128)S(1)}, f32[256,128]{1,0:T(8,128)S(1)}, u32[]{:S(2)}, u32[]{:S(2)}) %collective-permute-start) | collective-permute-done | bytes 131104 | tf_op jit(solution)/shard_map/ppermute | solution.py:90
  35.6 3.3 %copy-done = f32[960,2048]{1,0:T(8,128)S(1)} copy-done((f32[960,2048]{1,0:T(8,128)S(1)}, f32[960,2048]{1,0:T(8,128)}, u32[]{:S(2)}) %copy-start) | copy-done | bytes 7864344
  38.9 1.2 copy-done.12
  40.1 2.6 %pivots.4 = (f32[512,128]{1,0:T(8,128)S(1)}, f32[512,128]{1,0:T(8,128)S(1)}) custom-call(s32[1]{0:T(128)} %bitcast.me, s32[32,2]{1,0:T(8,128)S(1)} %copy.13.maps, f32[256,128]{1,0:T(8,128)S(1)} %get-tuple-element.11.refs_0_, f32[256,128]{1,0:T(8,128)S(1)} %collective-permute-done.refs_1_, f32[256,128]{1,0:T(8,128)S(1)} %collective-permute-done.1.refs_2_, ...), custom_call_target="tpu_custom_call" | custom-call | flops 805306368 | bytes 8000000 | tf_op jit(solution)/shard_map/pivots/pallas_call | solution.py:165
  42.7 1.8 %collective-permute-start.3 = (f32[512,128]{1,0:T(8,128)S(1)}, f32[512,128]{1,0:T(8,128)S(1)}, u32[]{:S(2)}, u32[]{:S(2)}) collective-permute-start(f32[512,128]{1,0:T(8,128)S(1)} %get-tuple-element.12.refs_0_.refs_18_), channel_id=1, source_target_pairs={{0,2},{1,3},{2,0},{3,1},{4,6},{5,7},{6,4},{7,5},{8,10},{9,11},{10,... | collective-permute-start | bytes 786440 | tf_op jit(solution)/shard_map/ppermute | solution.py:90
  44.6 8.5 %collective-permute-done.3.refs_1_ = f32[512,128]{1,0:T(8,128)S(1)} collective-permute-done((f32[512,128]{1,0:T(8,128)S(1)}, f32[512,128]{1,0:T(8,128)S(1)}, u32[]{:S(2)}, u32[]{:S(2)}) %collective-permute-start.3) | collective-permute-done | bytes 262176 | tf_op jit(solution)/shard_map/ppermute | solution.py:90
  53.0 1.5 collective-permute-done.5.refs_3_
  54.6 1.5 update.3.refs_0_
  56.1 3.3 %collective-permute-start.6 = (f32[512,128]{1,0:T(8,128)S(1)}, f32[512,128]{1,0:T(8,128)S(1)}, u32[]{:S(2)}, u32[]{:S(2)}) collective-permute-start(f32[512,128]{1,0:T(8,128)S(1)} %update.3.refs_0_), channel_id=1, source_target_pairs={{0,6},{1,7},{2,4},{3,5},{4,2},{5,3},{6,0},{7,1},{8,14},{9,15},{10,... | collective-permute-start | bytes 786440 | tf_op jit(solution)/shard_map/ppermute | solution.py:90
  60.1 1.4 slice.15
  61.6 5.3 %collective-permute-done.6.refs_1_ = f32[512,128]{1,0:T(8,128)S(1)} collective-permute-done((f32[512,128]{1,0:T(8,128)S(1)}, f32[512,128]{1,0:T(8,128)S(1)}, u32[]{:S(2)}, u32[]{:S(2)}) %collective-permute-start.6) | collective-permute-done | bytes 262176 | tf_op jit(solution)/shard_map/ppermute | solution.py:90
  66.9 4.8 %collective-permute-done.7.refs_2_ = f32[512,128]{1,0:T(8,128)S(1)} collective-permute-done((f32[512,128]{1,0:T(8,128)S(1)}, f32[512,128]{1,0:T(8,128)S(1)}, u32[]{:S(2)}, u32[]{:S(2)}) %collective-permute-start.7) | collective-permute-done | bytes 262176 | tf_op jit(solution)/shard_map/ppermute | solution.py:90
  71.8 1.0 collective-permute-done.8.refs_3_
  73.2 1.1 collective-permute-done.12.refs_7_
  74.3 3.3 %copy-done.1 = f32[960,2048]{1,0:T(8,128)S(1)} copy-done((f32[960,2048]{1,0:T(8,128)S(1)}, f32[960,2048]{1,0:T(8,128)}, u32[]{:S(2)}) %copy-start.1) | copy-done | bytes 7864344
  77.6 1.2 copy-done.11
  78.9 1.9 %pivots.5 = (f32[256,128]{1,0:T(8,128)S(1)}, f32[256,128]{1,0:T(8,128)S(1)}) custom-call(s32[1]{0:T(128)} %bitcast.me, s32[14,16]{1,0:T(8,128)S(1)} %copy-done.16, f32[512,128]{1,0:T(8,128)S(1)} %update.3.refs_0_, f32[512,128]{1,0:T(8,128)S(1)} %collective-permute-done.6.refs_1_, f32[512,128]{1,0:T(8,128)S(1)} %collective-permute-done.7.refs_2_, ...), custom_call_target="tpu_custom_call" | custom-call | flops 402653184 | bytes 8000000 | tf_op jit(solution)/shard_map/pivots/pallas_call | solution.py:165
  80.7 2.8 %collective-permute-start.13 = (f32[256,128]{1,0:T(8,128)S(1)}, f32[256,128]{1,0:T(8,128)S(1)}, u32[]{:S(2)}, u32[]{:S(2)}) collective-permute-start(f32[256,128]{1,0:T(8,128)S(1)} %get-tuple-element.14.refs_0_.refs_19_), channel_id=1, source_target_pairs={{0,6},{1,7},{2,4},{3,5},{4,2},{5,3},{6,0},{7,1},{8,14},{9,15},{10,... | collective-permute-start | bytes 393224 | tf_op jit(solution)/shard_map/ppermute | solution.py:90
  83.5 1.2 collective-permute-start.14
  84.7 3.8 %collective-permute-done.13.refs_1_ = f32[256,128]{1,0:T(8,128)S(1)} collective-permute-done((f32[256,128]{1,0:T(8,128)S(1)}, f32[256,128]{1,0:T(8,128)S(1)}, u32[]{:S(2)}, u32[]{:S(2)}) %collective-permute-start.13) | collective-permute-done | bytes 131104 | tf_op jit(solution)/shard_map/ppermute | solution.py:90
  88.5 1.8 collective-permute-done.14.refs_2_
  90.8 0.8 collective-permute-done.18.refs_6_
  91.8 3.1 %copy-done.4 = f32[896,2048]{1,0:T(8,128)S(1)} copy-done((f32[896,2048]{1,0:T(8,128)S(1)}, f32[896,2048]{1,0:T(8,128)}, u32[]{:S(2)}) %copy-start.4) | copy-done | bytes 7340056
  94.9 1.1 update.4.refs_0_
  96.0 3.3 %collective-permute-start.20 = (f32[256,128]{1,0:T(8,128)S(1)}, f32[256,128]{1,0:T(8,128)S(1)}, u32[]{:S(2)}, u32[]{:S(2)}) collective-permute-start(f32[256,128]{1,0:T(8,128)S(1)} %update.4.refs_0_), channel_id=1, source_target_pairs={{0,14},{1,15},{2,12},{3,13},{4,10},{5,11},{6,8},{7,9},{8,6},{9,7},... | collective-permute-start | bytes 393224 | tf_op jit(solution)/shard_map/ppermute | solution.py:90
  100.2 1.2 collective-permute-start.22
  102.0 2.4 %collective-permute-start.24 = (f32[256,128]{1,0:T(8,128)S(1)}, f32[256,128]{1,0:T(8,128)S(1)}, u32[]{:S(2)}, u32[]{:S(2)}) collective-permute-start(f32[256,128]{1,0:T(8,128)S(1)} %update.4.refs_0_), channel_id=1, source_target_pairs={{0,6},{1,7},{2,4},{3,5},{4,2},{5,3},{6,0},{7,1},{8,14},{9,15},{10,... | collective-permute-start | bytes 393224 | tf_op jit(solution)/shard_map/ppermute | solution.py:90
  104.4 1.1 collective-permute-start.25
  105.4 3.5 %collective-permute-done.21.refs_2_ = f32[256,128]{1,0:T(8,128)S(1)} collective-permute-done((f32[256,128]{1,0:T(8,128)S(1)}, f32[256,128]{1,0:T(8,128)S(1)}, u32[]{:S(2)}, u32[]{:S(2)}) %collective-permute-start.21) | collective-permute-done | bytes 131104 | tf_op jit(solution)/shard_map/ppermute | solution.py:90
  109.6 0.9 collective-permute-done.22.refs_3_
  110.5 1.8 collective-permute-done.23.refs_4_
  112.9 1.0 collective-permute-done.26.refs_7_
  115.9 3.2 %copy-done.2 = f32[960,2048]{1,0:T(8,128)S(1)} copy-done((f32[960,2048]{1,0:T(8,128)S(1)}, f32[960,2048]{1,0:T(8,128)}, u32[]{:S(2)}) %copy-start.2) | copy-done | bytes 7864344
  119.1 1.2 copy-done.10
  120.4 1.6 pivots.6
  122.0 2.5 %collective-permute-start.35 = (f32[128,128]{1,0:T(8,128)S(1)}, f32[128,128]{1,0:T(8,128)S(1)}, u32[]{:S(2)}, u32[]{:S(2)}) collective-permute-start(f32[128,128]{1,0:T(8,128)S(1)} %get-tuple-element.16.refs_0_.refs_20_), channel_id=1, source_target_pairs={{0,14},{1,15},{2,12},{3,13},{4,10},{5,11},{6,8},{7,9},{8,6},{9,7},... | collective-permute-start | bytes 196616 | tf_op jit(solution)/shard_map/ppermute | solution.py:90
  124.5 0.9 collective-permute-start.36
  125.5 2.0 %collective-permute-start.37 = (f32[128,128]{1,0:T(8,128)S(1)}, f32[128,128]{1,0:T(8,128)S(1)}, u32[]{:S(2)}, u32[]{:S(2)}) collective-permute-start(f32[128,128]{1,0:T(8,128)S(1)} %get-tuple-element.16.refs_0_.refs_20_), channel_id=1, source_target_pairs={{0,10},{1,11},{2,8},{3,9},{4,14},{5,15},{6,12},{7,13},{8,2},{9,3},... | collective-permute-start | bytes 196616 | tf_op jit(solution)/shard_map/ppermute | solution.py:90
  127.9 1.7 collective-permute-start.39
  132.6 1.4 collective-permute-done.39.refs_5_
  137.0 3.2 %copy-done.5 = f32[896,2048]{1,0:T(8,128)S(1)} copy-done((f32[896,2048]{1,0:T(8,128)S(1)}, f32[896,2048]{1,0:T(8,128)}, u32[]{:S(2)}) %copy-start.5) | copy-done | bytes 7340056
  140.9 3.0 %collective-permute-start.50 = (f32[128,128]{1,0:T(8,128)S(1)}, f32[128,128]{1,0:T(8,128)S(1)}, u32[]{:S(2)}, u32[]{:S(2)}) collective-permute-start(f32[128,128]{1,0:T(8,128)S(1)} %update.5), channel_id=1, source_target_pairs={{0,16},{1,17},{2,18},{3,19},{4,20},{5,21},{6,22},{7,23},{8,24},{9,... | collective-permute-start | bytes 196616 | tf_op jit(solution)/shard_map/ppermute | solution.py:90
  143.9 5.4 %collective-permute-done.50 = f32[128,128]{1,0:T(8,128)S(1)} collective-permute-done((f32[128,128]{1,0:T(8,128)S(1)}, f32[128,128]{1,0:T(8,128)S(1)}, u32[]{:S(2)}, u32[]{:S(2)}) %collective-permute-start.50) | collective-permute-done | bytes 65568 | tf_op jit(solution)/shard_map/ppermute | solution.py:90
  149.3 1.1 collective-permute-start.51
  150.3 2.0 %collective-permute-start.52 = (f32[256,128]{1,0:T(8,128)S(1)}, f32[256,128]{1,0:T(8,128)S(1)}, u32[]{:S(2)}, u32[]{:S(2)}) collective-permute-start(f32[256,128]{1,0:T(8,128)S(1)} %pad_maximum_fusion.refs_0_), channel_id=1, source_target_pairs={{0,12},{1,13},{2,14},{3,15},{4,8},{5,9},{6,10},{7,11},{8,4},{9,5},... | collective-permute-start | bytes 393224 | tf_op jit(solution)/shard_map/ppermute | solution.py:90
  153.1 2.1 %collective-permute-start.54 = (f32[256,128]{1,0:T(8,128)S(1)}, f32[256,128]{1,0:T(8,128)S(1)}, u32[]{:S(2)}, u32[]{:S(2)}) collective-permute-start(f32[256,128]{1,0:T(8,128)S(1)} %pad_maximum_fusion.refs_0_), channel_id=1, source_target_pairs={{0,8},{1,9},{2,10},{3,11},{4,12},{5,13},{6,14},{7,15},{8,0},{9,1},... | collective-permute-start | bytes 393224 | tf_op jit(solution)/shard_map/ppermute | solution.py:90
  155.2 1.5 collective-permute-start.55
  156.7 1.6 collective-permute-done.51.refs_1_
  158.9 1.6 collective-permute-done.52.refs_2_
  160.5 1.1 collective-permute-start.57
  161.6 1.0 collective-permute-done.53.refs_3_
  162.7 1.3 collective-permute-done.54.refs_4_
  167.5 3.2 %copy-done.3 = f32[960,2048]{1,0:T(8,128)S(1)} copy-done((f32[960,2048]{1,0:T(8,128)S(1)}, f32[960,2048]{1,0:T(8,128)}, u32[]{:S(2)}) %copy-start.3) | copy-done | bytes 7864344
  170.8 1.2 copy-done.13
  172.0 2.4 %pivots.7 = f32[960,128]{1,0:T(8,128)} custom-call(s32[1]{0:T(128)} %bitcast.me, s32[14,16]{1,0:T(8,128)S(1)} %copy-done.16, f32[256,128]{1,0:T(8,128)S(1)} %pad_maximum_fusion.refs_0_, f32[256,128]{1,0:T(8,128)S(1)} %collective-permute-done.51.refs_1_, f32[256,128]{1,0:T(8,128)S(1)} %collective-permute-done.52.refs_2_, ...), custom_call_target="tpu_custom_call" | custom-call | flops 100663296 | bytes 8000000 | tf_op jit(solution)/shard_map/pivots/pallas_call | solution.py:165
  (134 shorter events, 21.3 us)
Async XLA Ops:
  7.2 28.4 %all-gather.5.cloned.1.call-start = ((), (), s32[]{:S(2)}) async-start(), calls=%async_computation | async-start | bytes 1310720 | tf_op jit(solution)/shard_map/all_gather | solution.py:250
  8.9 63.9 %all-gather.7.cloned.1.call-start = ((), (), s32[]{:S(2)}) async-start(), calls=%async_computation.1 | async-start | bytes 1179648 | tf_op jit(solution)/shard_map/all_gather | solution.py:250
  10.5 104.3 %all-gather.9.cloned.1.call-start = ((), (), s32[]{:S(2)}) async-start(), calls=%async_computation.2 | async-start | bytes 1114112 | tf_op jit(solution)/shard_map/all_gather | solution.py:250
  12.1 154.4 %all-gather.11.cloned.1.call-start = ((), (), s32[]{:S(2)}) async-start(), calls=%async_computation.3 | async-start | bytes 1081344 | tf_op jit(solution)/shard_map/all_gather | solution.py:250
  27.6 6.5 %collective-permute-start = (f32[256,128]{1,0:T(8,128)S(1)}, f32[256,128]{1,0:T(8,128)S(1)}, u32[]{:S(2)}, u32[]{:S(2)}) collective-permute-start(f32[256,128]{1,0:T(8,128)S(1)} %get-tuple-element.11.refs_0_), channel_id=1, source_target_pairs={{0,2},{1,3},{2,0},{3,1},{4,6},{5,7},{6,4},{7,5},{8,10},{9,11},{10,... | collective-permute-start | bytes 393224 | tf_op jit(solution)/shard_map/ppermute | solution.py:90
  30.6 4.3 %collective-permute-start.1 = (f32[256,128]{1,0:T(8,128)S(1)}, f32[256,128]{1,0:T(8,128)S(1)}, u32[]{:S(2)}, u32[]{:S(2)}) collective-permute-start(f32[256,128]{1,0:T(8,128)S(1)} %get-tuple-element.11.refs_0_), channel_id=1, source_target_pairs={{0,1},{1,0},{2,3},{3,2},{4,5},{5,4},{6,7},{7,6},{8,9},{9,8},{10,11... | collective-permute-start | bytes 393224 | tf_op jit(solution)/shard_map/ppermute | solution.py:90
  34.1 1.5 collective-permute-start.2
  42.7 10.3 %collective-permute-start.3 = (f32[512,128]{1,0:T(8,128)S(1)}, f32[512,128]{1,0:T(8,128)S(1)}, u32[]{:S(2)}, u32[]{:S(2)}) collective-permute-start(f32[512,128]{1,0:T(8,128)S(1)} %get-tuple-element.12.refs_0_.refs_18_), channel_id=1, source_target_pairs={{0,2},{1,3},{2,0},{3,1},{4,6},{5,7},{6,4},{7,5},{8,10},{9,11},{10,... | collective-permute-start | bytes 786440 | tf_op jit(solution)/shard_map/ppermute | solution.py:90
  44.6 8.5 %collective-permute-start.4 = (f32[512,128]{1,0:T(8,128)S(1)}, f32[512,128]{1,0:T(8,128)S(1)}, u32[]{:S(2)}, u32[]{:S(2)}) collective-permute-start(f32[512,128]{1,0:T(8,128)S(1)} %get-tuple-element.12.refs_0_.refs_18_), channel_id=1, source_target_pairs={{0,1},{1,0},{2,3},{3,2},{4,5},{5,4},{6,7},{7,6},{8,9},{9,8},{10,11... | collective-permute-start | bytes 786440 | tf_op jit(solution)/shard_map/ppermute | solution.py:90
  53.0 1.5 collective-permute-start.5
  56.1 10.8 %collective-permute-start.6 = (f32[512,128]{1,0:T(8,128)S(1)}, f32[512,128]{1,0:T(8,128)S(1)}, u32[]{:S(2)}, u32[]{:S(2)}) collective-permute-start(f32[512,128]{1,0:T(8,128)S(1)} %update.3.refs_0_), channel_id=1, source_target_pairs={{0,6},{1,7},{2,4},{3,5},{4,2},{5,3},{6,0},{7,1},{8,14},{9,15},{10,... | collective-permute-start | bytes 786440 | tf_op jit(solution)/shard_map/ppermute | solution.py:90
  59.4 12.2 %collective-permute-start.7 = (f32[512,128]{1,0:T(8,128)S(1)}, f32[512,128]{1,0:T(8,128)S(1)}, u32[]{:S(2)}, u32[]{:S(2)}) collective-permute-start(f32[512,128]{1,0:T(8,128)S(1)} %update.3.refs_0_), channel_id=1, source_target_pairs={{0,4},{1,5},{2,6},{3,7},{4,0},{5,1},{6,2},{7,3},{8,12},{9,13},{10,... | collective-permute-start | bytes 786440 | tf_op jit(solution)/shard_map/ppermute | solution.py:90
  60.1 12.7 %collective-permute-start.8 = (f32[512,128]{1,0:T(8,128)S(1)}, f32[512,128]{1,0:T(8,128)S(1)}, u32[]{:S(2)}, u32[]{:S(2)}) collective-permute-start(f32[512,128]{1,0:T(8,128)S(1)} %update.3.refs_0_), channel_id=1, source_target_pairs={{0,2},{1,3},{2,0},{3,1},{4,6},{5,7},{6,4},{7,5},{8,10},{9,11},{10,... | collective-permute-start | bytes 786440 | tf_op jit(solution)/shard_map/ppermute | solution.py:90
  61.5 11.3 %collective-permute-start.9 = (f32[512,128]{1,0:T(8,128)S(1)}, f32[512,128]{1,0:T(8,128)S(1)}, u32[]{:S(2)}, u32[]{:S(2)}) collective-permute-start(f32[512,128]{1,0:T(8,128)S(1)} %update.3.refs_0_), channel_id=1, source_target_pairs={{0,1},{1,0},{2,3},{3,2},{4,5},{5,4},{6,7},{7,6},{8,9},{9,8},{10,11... | collective-permute-start | bytes 786440 | tf_op jit(solution)/shard_map/ppermute | solution.py:90
  66.9 6.0 %collective-permute-start.10 = (f32[512,128]{1,0:T(8,128)S(1)}, f32[512,128]{1,0:T(8,128)S(1)}, u32[]{:S(2)}, u32[]{:S(2)}) collective-permute-start(f32[512,128]{1,0:T(8,128)S(1)} %collective-permute-done.6.refs_1_), channel_id=1, source_target_pairs={{0,1},{1,0},{2,3},{3,2},{4,5},{5,4},{6,7},{7,6},{8,9},{9,8},{10,11... | collective-permute-start | bytes 786440 | tf_op jit(solution)/shard_map/ppermute | solution.py:90
  71.6 1.5 collective-permute-start.11
  72.8 1.5 collective-permute-start.12
  80.7 7.8 %collective-permute-start.13 = (f32[256,128]{1,0:T(8,128)S(1)}, f32[256,128]{1,0:T(8,128)S(1)}, u32[]{:S(2)}, u32[]{:S(2)}) collective-permute-start(f32[256,128]{1,0:T(8,128)S(1)} %get-tuple-element.14.refs_0_.refs_19_), channel_id=1, source_target_pairs={{0,6},{1,7},{2,4},{3,5},{4,2},{5,3},{6,0},{7,1},{8,14},{9,15},{10,... | collective-permute-start | bytes 393224 | tf_op jit(solution)/shard_map/ppermute | solution.py:90
  83.5 6.8 %collective-permute-start.14 = (f32[256,128]{1,0:T(8,128)S(1)}, f32[256,128]{1,0:T(8,128)S(1)}, u32[]{:S(2)}, u32[]{:S(2)}) collective-permute-start(f32[256,128]{1,0:T(8,128)S(1)} %get-tuple-element.14.refs_0_.refs_19_), channel_id=1, source_target_pairs={{0,4},{1,5},{2,6},{3,7},{4,0},{5,1},{6,2},{7,3},{8,12},{9,13},{10,... | collective-permute-start | bytes 393224 | tf_op jit(solution)/shard_map/ppermute | solution.py:90
  84.7 5.7 %collective-permute-start.15 = (f32[256,128]{1,0:T(8,128)S(1)}, f32[256,128]{1,0:T(8,128)S(1)}, u32[]{:S(2)}, u32[]{:S(2)}) collective-permute-start(f32[256,128]{1,0:T(8,128)S(1)} %get-tuple-element.14.refs_0_.refs_19_), channel_id=1, source_target_pairs={{0,2},{1,3},{2,0},{3,1},{4,6},{5,7},{6,4},{7,5},{8,10},{9,11},{10,... | collective-permute-start | bytes 393224 | tf_op jit(solution)/shard_map/ppermute | solution.py:90
  84.7 6.1 %collective-permute-start.16 = (f32[256,128]{1,0:T(8,128)S(1)}, f32[256,128]{1,0:T(8,128)S(1)}, u32[]{:S(2)}, u32[]{:S(2)}) collective-permute-start(f32[256,128]{1,0:T(8,128)S(1)} %get-tuple-element.14.refs_0_.refs_19_), channel_id=1, source_target_pairs={{0,1},{1,0},{2,3},{3,2},{4,5},{5,4},{6,7},{7,6},{8,9},{9,8},{10,11... | collective-permute-start | bytes 393224 | tf_op jit(solution)/shard_map/ppermute | solution.py:90
  88.5 2.3 %collective-permute-start.17 = (f32[256,128]{1,0:T(8,128)S(1)}, f32[256,128]{1,0:T(8,128)S(1)}, u32[]{:S(2)}, u32[]{:S(2)}) collective-permute-start(f32[256,128]{1,0:T(8,128)S(1)} %collective-permute-done.13.refs_1_), channel_id=1, source_target_pairs={{0,1},{1,0},{2,3},{3,2},{4,5},{5,4},{6,7},{7,6},{8,9},{9,8},{10,11... | collective-permute-start | bytes 393224 | tf_op jit(solution)/shard_map/ppermute | solution.py:90
  90.3 1.3 collective-permute-start.18
  90.3 1.5 collective-permute-start.19
  96.0 8.3 %collective-permute-start.20 = (f32[256,128]{1,0:T(8,128)S(1)}, f32[256,128]{1,0:T(8,128)S(1)}, u32[]{:S(2)}, u32[]{:S(2)}) collective-permute-start(f32[256,128]{1,0:T(8,128)S(1)} %update.4.refs_0_), channel_id=1, source_target_pairs={{0,14},{1,15},{2,12},{3,13},{4,10},{5,11},{6,8},{7,9},{8,6},{9,7},... | collective-permute-start | bytes 393224 | tf_op jit(solution)/shard_map/ppermute | solution.py:90
  99.4 9.5 %collective-permute-start.21 = (f32[256,128]{1,0:T(8,128)S(1)}, f32[256,128]{1,0:T(8,128)S(1)}, u32[]{:S(2)}, u32[]{:S(2)}) collective-permute-start(f32[256,128]{1,0:T(8,128)S(1)} %update.4.refs_0_), channel_id=1, source_target_pairs={{0,12},{1,13},{2,14},{3,15},{4,8},{5,9},{6,10},{7,11},{8,4},{9,5},... | collective-permute-start | bytes 393224 | tf_op jit(solution)/shard_map/ppermute | solution.py:90
  100.2 10.4 %collective-permute-start.22 = (f32[256,128]{1,0:T(8,128)S(1)}, f32[256,128]{1,0:T(8,128)S(1)}, u32[]{:S(2)}, u32[]{:S(2)}) collective-permute-start(f32[256,128]{1,0:T(8,128)S(1)} %update.4.refs_0_), channel_id=1, source_target_pairs={{0,10},{1,11},{2,8},{3,9},{4,14},{5,15},{6,12},{7,13},{8,2},{9,3},... | collective-permute-start | bytes 393224 | tf_op jit(solution)/shard_map/ppermute | solution.py:90
  101.4 10.9 %collective-permute-start.23 = (f32[256,128]{1,0:T(8,128)S(1)}, f32[256,128]{1,0:T(8,128)S(1)}, u32[]{:S(2)}, u32[]{:S(2)}) collective-permute-start(f32[256,128]{1,0:T(8,128)S(1)} %update.4.refs_0_), channel_id=1, source_target_pairs={{0,8},{1,9},{2,10},{3,11},{4,12},{5,13},{6,14},{7,15},{8,0},{9,1},... | collective-permute-start | bytes 393224 | tf_op jit(solution)/shard_map/ppermute | solution.py:90
  102.0 10.4 %collective-permute-start.24 = (f32[256,128]{1,0:T(8,128)S(1)}, f32[256,128]{1,0:T(8,128)S(1)}, u32[]{:S(2)}, u32[]{:S(2)}) collective-permute-start(f32[256,128]{1,0:T(8,128)S(1)} %update.4.refs_0_), channel_id=1, source_target_pairs={{0,6},{1,7},{2,4},{3,5},{4,2},{5,3},{6,0},{7,1},{8,14},{9,15},{10,... | collective-permute-start | bytes 393224 | tf_op jit(solution)/shard_map/ppermute | solution.py:90
  104.4 8.5 %collective-permute-start.25 = (f32[256,128]{1,0:T(8,128)S(1)}, f32[256,128]{1,0:T(8,128)S(1)}, u32[]{:S(2)}, u32[]{:S(2)}) collective-permute-start(f32[256,128]{1,0:T(8,128)S(1)} %update.4.refs_0_), channel_id=1, source_target_pairs={{0,4},{1,5},{2,6},{3,7},{4,0},{5,1},{6,2},{7,3},{8,12},{9,13},{10,... | collective-permute-start | bytes 393224 | tf_op jit(solution)/shard_map/ppermute | solution.py:90
  108.9 5.0 %collective-permute-start.26 = (f32[256,128]{1,0:T(8,128)S(1)}, f32[256,128]{1,0:T(8,128)S(1)}, u32[]{:S(2)}, u32[]{:S(2)}) collective-permute-start(f32[256,128]{1,0:T(8,128)S(1)} %update.4.refs_0_), channel_id=1, source_target_pairs={{0,2},{1,3},{2,0},{3,1},{4,6},{5,7},{6,4},{7,5},{8,10},{9,11},{10,... | collective-permute-start | bytes 393224 | tf_op jit(solution)/shard_map/ppermute | solution.py:90
  110.5 3.3 %collective-permute-start.27 = (f32[256,128]{1,0:T(8,128)S(1)}, f32[256,128]{1,0:T(8,128)S(1)}, u32[]{:S(2)}, u32[]{:S(2)}) collective-permute-start(f32[256,128]{1,0:T(8,128)S(1)} %update.4.refs_0_), channel_id=1, source_target_pairs={{0,1},{1,0},{2,3},{3,2},{4,5},{5,4},{6,7},{7,6},{8,9},{9,8},{10,11... | collective-permute-start | bytes 393224 | tf_op jit(solution)/shard_map/ppermute | solution.py:90
  112.3 2.1 %collective-permute-start.28 = (f32[256,128]{1,0:T(8,128)S(1)}, f32[256,128]{1,0:T(8,128)S(1)}, u32[]{:S(2)}, u32[]{:S(2)}) collective-permute-start(f32[256,128]{1,0:T(8,128)S(1)} %collective-permute-done.20.refs_1_), channel_id=1, source_target_pairs={{0,1},{1,0},{2,3},{3,2},{4,5},{5,4},{6,7},{7,6},{8,9},{9,8},{10,11... | collective-permute-start | bytes 393224 | tf_op jit(solution)/shard_map/ppermute | solution.py:90
  112.3 2.1 %collective-permute-start.29 = (f32[256,128]{1,0:T(8,128)S(1)}, f32[256,128]{1,0:T(8,128)S(1)}, u32[]{:S(2)}, u32[]{:S(2)}) collective-permute-start(f32[256,128]{1,0:T(8,128)S(1)} %collective-permute-done.21.refs_2_), channel_id=1, source_target_pairs={{0,1},{1,0},{2,3},{3,2},{4,5},{5,4},{6,7},{7,6},{8,9},{9,8},{10,11... | collective-permute-start | bytes 393224 | tf_op jit(solution)/shard_map/ppermute | solution.py:90
  112.8 2.1 %collective-permute-start.30 = (f32[256,128]{1,0:T(8,128)S(1)}, f32[256,128]{1,0:T(8,128)S(1)}, u32[]{:S(2)}, u32[]{:S(2)}) collective-permute-start(f32[256,128]{1,0:T(8,128)S(1)} %collective-permute-done.22.refs_3_), channel_id=1, source_target_pairs={{0,1},{1,0},{2,3},{3,2},{4,5},{5,4},{6,7},{7,6},{8,9},{9,8},{10,11... | collective-permute-start | bytes 393224 | tf_op jit(solution)/shard_map/ppermute | solution.py:90
  113.9 1.5 collective-permute-start.32
  114.4 1.5 collective-permute-start.34
  122.0 7.6 %collective-permute-start.35 = (f32[128,128]{1,0:T(8,128)S(1)}, f32[128,128]{1,0:T(8,128)S(1)}, u32[]{:S(2)}, u32[]{:S(2)}) collective-permute-start(f32[128,128]{1,0:T(8,128)S(1)} %get-tuple-element.16.refs_0_.refs_20_), channel_id=1, source_target_pairs={{0,14},{1,15},{2,12},{3,13},{4,10},{5,11},{6,8},{7,9},{8,6},{9,7},... | collective-permute-start | bytes 196616 | tf_op jit(solution)/shard_map/ppermute | solution.py:90
  124.5 6.3 %collective-permute-start.36 = (f32[128,128]{1,0:T(8,128)S(1)}, f32[128,128]{1,0:T(8,128)S(1)}, u32[]{:S(2)}, u32[]{:S(2)}) collective-permute-start(f32[128,128]{1,0:T(8,128)S(1)} %get-tuple-element.16.refs_0_.refs_20_), channel_id=1, source_target_pairs={{0,12},{1,13},{2,14},{3,15},{4,8},{5,9},{6,10},{7,11},{8,4},{9,5},... | collective-permute-start | bytes 196616 | tf_op jit(solution)/shard_map/ppermute | solution.py:90
  125.5 6.7 %collective-permute-start.37 = (f32[128,128]{1,0:T(8,128)S(1)}, f32[128,128]{1,0:T(8,128)S(1)}, u32[]{:S(2)}, u32[]{:S(2)}) collective-permute-start(f32[128,128]{1,0:T(8,128)S(1)} %get-tuple-element.16.refs_0_.refs_20_), channel_id=1, source_target_pairs={{0,10},{1,11},{2,8},{3,9},{4,14},{5,15},{6,12},{7,13},{8,2},{9,3},... | collective-permute-start | bytes 196616 | tf_op jit(solution)/shard_map/ppermute | solution.py:90
  127.4 5.2 %collective-permute-start.38 = (f32[128,128]{1,0:T(8,128)S(1)}, f32[128,128]{1,0:T(8,128)S(1)}, u32[]{:S(2)}, u32[]{:S(2)}) collective-permute-start(f32[128,128]{1,0:T(8,128)S(1)} %get-tuple-element.16.refs_0_.refs_20_), channel_id=1, source_target_pairs={{0,8},{1,9},{2,10},{3,11},{4,12},{5,13},{6,14},{7,15},{8,0},{9,1},... | collective-permute-start | bytes 196616 | tf_op jit(solution)/shard_map/ppermute | solution.py:90
  127.9 6.1 %collective-permute-start.39 = (f32[128,128]{1,0:T(8,128)S(1)}, f32[128,128]{1,0:T(8,128)S(1)}, u32[]{:S(2)}, u32[]{:S(2)}) collective-permute-start(f32[128,128]{1,0:T(8,128)S(1)} %get-tuple-element.16.refs_0_.refs_20_), channel_id=1, source_target_pairs={{0,6},{1,7},{2,4},{3,5},{4,2},{5,3},{6,0},{7,1},{8,14},{9,15},{10,... | collective-permute-start | bytes 196616 | tf_op jit(solution)/shard_map/ppermute | solution.py:90
  129.6 4.7 %collective-permute-start.40 = (f32[128,128]{1,0:T(8,128)S(1)}, f32[128,128]{1,0:T(8,128)S(1)}, u32[]{:S(2)}, u32[]{:S(2)}) collective-permute-start(f32[128,128]{1,0:T(8,128)S(1)} %get-tuple-element.16.refs_0_.refs_20_), channel_id=1, source_target_pairs={{0,4},{1,5},{2,6},{3,7},{4,0},{5,1},{6,2},{7,3},{8,12},{9,13},{10,... | collective-permute-start | bytes 196616 | tf_op jit(solution)/shard_map/ppermute | solution.py:90
  130.8 4.3 %collective-permute-start.41 = (f32[128,128]{1,0:T(8,128)S(1)}, f32[128,128]{1,0:T(8,128)S(1)}, u32[]{:S(2)}, u32[]{:S(2)}) collective-permute-start(f32[128,128]{1,0:T(8,128)S(1)} %get-tuple-element.16.refs_0_.refs_20_), channel_id=1, source_target_pairs={{0,2},{1,3},{2,0},{3,1},{4,6},{5,7},{6,4},{7,5},{8,10},{9,11},{10,... | collective-permute-start | bytes 196616 | tf_op jit(solution)/shard_map/ppermute | solution.py:90
  132.1 3.0 %collective-permute-start.42 = (f32[128,128]{1,0:T(8,128)S(1)}, f32[128,128]{1,0:T(8,128)S(1)}, u32[]{:S(2)}, u32[]{:S(2)}) collective-permute-start(f32[128,128]{1,0:T(8,128)S(1)} %get-tuple-element.16.refs_0_.refs_20_), channel_id=1, source_target_pairs={{0,1},{1,0},{2,3},{3,2},{4,5},{5,4},{6,7},{7,6},{8,9},{9,8},{10,11... | collective-permute-start | bytes 196616 | tf_op jit(solution)/shard_map/ppermute | solution.py:90
  132.6 3.1 %collective-permute-start.43 = (f32[128,128]{1,0:T(8,128)S(1)}, f32[128,128]{1,0:T(8,128)S(1)}, u32[]{:S(2)}, u32[]{:S(2)}) collective-permute-start(f32[128,128]{1,0:T(8,128)S(1)} %collective-permute-done.35.refs_1_), channel_id=1, source_target_pairs={{0,1},{1,0},{2,3},{3,2},{4,5},{5,4},{6,7},{7,6},{8,9},{9,8},{10,11... | collective-permute-start | bytes 196616 | tf_op jit(solution)/shard_map/ppermute | solution.py:90
  134.0 1.7 collective-permute-start.44
  134.3 1.9 %collective-permute-start.45 = (f32[128,128]{1,0:T(8,128)S(1)}, f32[128,128]{1,0:T(8,128)S(1)}, u32[]{:S(2)}, u32[]{:S(2)}) collective-permute-start(f32[128,128]{1,0:T(8,128)S(1)} %collective-permute-done.37.refs_3_), channel_id=1, source_target_pairs={{0,1},{1,0},{2,3},{3,2},{4,5},{5,4},{6,7},{7,6},{8,9},{9,8},{10,11... | collective-permute-start | bytes 196616 | tf_op jit(solution)/shard_map/ppermute | solution.py:90
  135.1 1.4 collective-permute-start.47
  140.9 8.4 %collective-permute-start.50 = (f32[128,128]{1,0:T(8,128)S(1)}, f32[128,128]{1,0:T(8,128)S(1)}, u32[]{:S(2)}, u32[]{:S(2)}) collective-permute-start(f32[128,128]{1,0:T(8,128)S(1)} %update.5), channel_id=1, source_target_pairs={{0,16},{1,17},{2,18},{3,19},{4,20},{5,21},{6,22},{7,23},{8,24},{9,... | collective-permute-start | bytes 196616 | tf_op jit(solution)/shard_map/ppermute | solution.py:90
  149.3 9.0 %collective-permute-start.51 = (f32[256,128]{1,0:T(8,128)S(1)}, f32[256,128]{1,0:T(8,128)S(1)}, u32[]{:S(2)}, u32[]{:S(2)}) collective-permute-start(f32[256,128]{1,0:T(8,128)S(1)} %pad_maximum_fusion.refs_0_), channel_id=1, source_target_pairs={{0,14},{1,15},{2,12},{3,13},{4,10},{5,11},{6,8},{7,9},{8,6},{9,7},... | collective-permute-start | bytes 393224 | tf_op jit(solution)/shard_map/ppermute | solution.py:90
  150.3 10.2 %collective-permute-start.52 = (f32[256,128]{1,0:T(8,128)S(1)}, f32[256,128]{1,0:T(8,128)S(1)}, u32[]{:S(2)}, u32[]{:S(2)}) collective-permute-start(f32[256,128]{1,0:T(8,128)S(1)} %pad_maximum_fusion.refs_0_), channel_id=1, source_target_pairs={{0,12},{1,13},{2,14},{3,15},{4,8},{5,9},{6,10},{7,11},{8,4},{9,5},... | collective-permute-start | bytes 393224 | tf_op jit(solution)/shard_map/ppermute | solution.py:90
  152.3 10.3 %collective-permute-start.53 = (f32[256,128]{1,0:T(8,128)S(1)}, f32[256,128]{1,0:T(8,128)S(1)}, u32[]{:S(2)}, u32[]{:S(2)}) collective-permute-start(f32[256,128]{1,0:T(8,128)S(1)} %pad_maximum_fusion.refs_0_), channel_id=1, source_target_pairs={{0,10},{1,11},{2,8},{3,9},{4,14},{5,15},{6,12},{7,13},{8,2},{9,3},... | collective-permute-start | bytes 393224 | tf_op jit(solution)/shard_map/ppermute | solution.py:90
  153.1 10.9 %collective-permute-start.54 = (f32[256,128]{1,0:T(8,128)S(1)}, f32[256,128]{1,0:T(8,128)S(1)}, u32[]{:S(2)}, u32[]{:S(2)}) collective-permute-start(f32[256,128]{1,0:T(8,128)S(1)} %pad_maximum_fusion.refs_0_), channel_id=1, source_target_pairs={{0,8},{1,9},{2,10},{3,11},{4,12},{5,13},{6,14},{7,15},{8,0},{9,1},... | collective-permute-start | bytes 393224 | tf_op jit(solution)/shard_map/ppermute | solution.py:90
  155.2 9.5 %collective-permute-start.55 = (f32[256,128]{1,0:T(8,128)S(1)}, f32[256,128]{1,0:T(8,128)S(1)}, u32[]{:S(2)}, u32[]{:S(2)}) collective-permute-start(f32[256,128]{1,0:T(8,128)S(1)} %pad_maximum_fusion.refs_0_), channel_id=1, source_target_pairs={{0,6},{1,7},{2,4},{3,5},{4,2},{5,3},{6,0},{7,1},{8,14},{9,15},{10,... | collective-permute-start | bytes 393224 | tf_op jit(solution)/shard_map/ppermute | solution.py:90
  158.3 6.6 %collective-permute-start.56 = (f32[256,128]{1,0:T(8,128)S(1)}, f32[256,128]{1,0:T(8,128)S(1)}, u32[]{:S(2)}, u32[]{:S(2)}) collective-permute-start(f32[256,128]{1,0:T(8,128)S(1)} %pad_maximum_fusion.refs_0_), channel_id=1, source_target_pairs={{0,4},{1,5},{2,6},{3,7},{4,0},{5,1},{6,2},{7,3},{8,12},{9,13},{10,... | collective-permute-start | bytes 393224 | tf_op jit(solution)/shard_map/ppermute | solution.py:90
  160.5 5.0 %collective-permute-start.57 = (f32[256,128]{1,0:T(8,128)S(1)}, f32[256,128]{1,0:T(8,128)S(1)}, u32[]{:S(2)}, u32[]{:S(2)}) collective-permute-start(f32[256,128]{1,0:T(8,128)S(1)} %pad_maximum_fusion.refs_0_), channel_id=1, source_target_pairs={{0,2},{1,3},{2,0},{3,1},{4,6},{5,7},{6,4},{7,5},{8,10},{9,11},{10,... | collective-permute-start | bytes 393224 | tf_op jit(solution)/shard_map/ppermute | solution.py:90
  162.7 2.8 %collective-permute-start.58 = (f32[256,128]{1,0:T(8,128)S(1)}, f32[256,128]{1,0:T(8,128)S(1)}, u32[]{:S(2)}, u32[]{:S(2)}) collective-permute-start(f32[256,128]{1,0:T(8,128)S(1)} %pad_maximum_fusion.refs_0_), channel_id=1, source_target_pairs={{0,1},{1,0},{2,3},{3,2},{4,5},{5,4},{6,7},{7,6},{8,9},{9,8},{10,11... | collective-permute-start | bytes 393224 | tf_op jit(solution)/shard_map/ppermute | solution.py:90
  163.9 2.1 %collective-permute-start.59 = (f32[256,128]{1,0:T(8,128)S(1)}, f32[256,128]{1,0:T(8,128)S(1)}, u32[]{:S(2)}, u32[]{:S(2)}) collective-permute-start(f32[256,128]{1,0:T(8,128)S(1)} %collective-permute-done.51.refs_1_), channel_id=1, source_target_pairs={{0,1},{1,0},{2,3},{3,2},{4,5},{5,4},{6,7},{7,6},{8,9},{9,8},{10,11... | collective-permute-start | bytes 393224 | tf_op jit(solution)/shard_map/ppermute | solution.py:90
  164.7 1.4 collective-permute-start.60
  164.9 1.6 collective-permute-start.61
  165.5 1.5 collective-permute-start.63
  166.0 1.3 collective-permute-start.64
  166.1 1.5 collective-permute-start.65
  (25 other events, 148.7 us)
Sparse Core Ops, SparseCore 0:
  10.1 19.4 all-gather.4
  31.5 23.9 all-gather.6
  57.1 32.3 all-gather.8
  92.2 59.7 all-gather.10

commit v2 on v1

v2 whole, which is shorter than its diff:
```python
import functools

import jax
import jax.numpy as jnp
from jax import lax
from jax.experimental import pallas as pl
from jax.experimental.pallas import tpu as pltpu
from jax.sharding import PartitionSpec as P

AXES = ("leaf", "front")
B = 128
BF16 = jnp.bfloat16
F32 = jnp.float32
ANY = pl.BlockSpec(memory_space=pl.ANY)
VMEM = pl.BlockSpec(memory_space=pltpu.VMEM)
HBM = pl.BlockSpec(memory_space=pltpu.HBM)
SMEM = pl.BlockSpec(memory_space=pltpu.SMEM)
MIB = 2**20


def in_hbm(x):
    return pltpu.with_memory_space_constraint(x, pltpu.HBM)


def in_vmem(x):
    return pltpu.with_memory_space_constraint(x, pltpu.VMEM)


def halves(x):
    high = x.astype(BF16)
    return high, (x - high.astype(F32)).astype(BF16)


def tall(x):
    return jnp.concatenate(halves(x), 0)


def wide(x):
    return jnp.concatenate(halves(x), 1)


def product(left, right):
    both = jnp.dot(left, right, preferred_element_type=F32)
    rows, cols = left.shape[0] // 2, right.shape[1] // 2
    return both[:rows, :cols] + both[:rows, cols:] + both[rows:, :cols]


def subtree_kernel(
    bounds, pattern_in, rhs_in, dinv_in, off_in, upd_in, y_out, w, *scratch
):
    pattern, rhs, dinv, off, upd, y, coef, lead, solved, sems, end_sems = scratch
    rounds = len(bounds) - 1

    def loads(r):
        low, high = bounds[r : r + 2]
        above = max(low - 1, 0)
        return [
            pltpu.make_async_copy(dinv_in.at[low:high], dinv.at[low:high], sems.at[r, 0]),
            pltpu.make_async_copy(
                rhs_in.at[low * B : high * B], rhs.at[low * B : high * B], sems.at[r, 1]
            ),
            pltpu.make_async_copy(
                off_in.at[above : high - 1], off.at[above : high - 1], sems.at[r, 2]
            ),
        ]

    def store(r):
        rows = slice(bounds[r] * B, bounds[r + 1] * B)
        return pltpu.make_async_copy(y.at[rows], y_out.at[rows], sems.at[r, 3])

    pattern_copy = pltpu.make_async_copy(pattern_in, pattern, end_sems.at[0])
    upd_copy = pltpu.make_async_copy(upd_in, upd, end_sems.at[1])
    pattern_copy.start()
    for r in range(rounds):
        for copy in loads(r):
            copy.start()
    upd_copy.start()

    def put(i, value):
        rows = slice(i * B, (i + 1) * B)
        y[rows, :] = value
        solved[rows, :] = wide(value)

    def prepare(i):
        right = jnp.concatenate([off[i - 1, 0], off[i - 1, 1], rhs[i * B : (i + 1) * B, :]], 1)
        out = product(tall(dinv[i]), wide(right))
        lead[i] = out[:, 2 * B :]
        coef[i] = tall(-out[:, : 2 * B])

    def step(i):
        first = pl.multiple_of(pattern[0, i - 1] * B, B)
        second = pl.multiple_of(pattern[1, i - 1] * B, B)
        known = jnp.concatenate([solved[pl.ds(first, B), :], solved[pl.ds(second, B), :]], 0)
        put(i, lead[i] + product(coef[i], known))

    pattern_copy.wait()
    for r in range(rounds):
        for copy in loads(r):
            copy.wait()
        if r == 0:
            put(0, product(tall(dinv[0]), wide(rhs[:B, :])))
        low, high = max(bounds[r], 1), bounds[r + 1]
        prepare(low)
        for i in range(low, high):
            if i + 1 < high:
                prepare(i + 1)
            step(i)
        store(r).start()
    upd_copy.wait()
    w[...] = -product(tall(upd[...]), solved[...])
    for r in range(rounds):
        store(r).wait()


def solve_subtree(rhs, dinv, off, pattern, upd):
    count = dinv.shape[0]
    bounds = [0, count // 6, count // 2, count]
    return pl.pallas_call(
        functools.partial(subtree_kernel, bounds),
        out_shape=(
            jax.ShapeDtypeStruct(rhs.shape, F32),
            jax.ShapeDtypeStruct((upd.shape[0], rhs.shape[1]), F32),
        ),
        in_specs=[HBM] * 5,
        out_specs=(HBM, VMEM),
        scratch_shapes=[
            pltpu.SMEM(pattern.shape, jnp.int32),
            pltpu.VMEM(rhs.shape, F32),
            pltpu.VMEM(dinv.shape, F32),
            pltpu.VMEM(off.shape, F32),
            pltpu.VMEM(upd.shape, F32),
            pltpu.VMEM(rhs.shape, F32),
            pltpu.VMEM((count, 2 * B, 2 * B), BF16),
            pltpu.VMEM((count, B, B), F32),
            pltpu.VMEM((count * B, 2 * B), BF16),
            pltpu.SemaphoreType.DMA((len(bounds) - 1, 4)),
            pltpu.SemaphoreType.DMA((2,)),
        ],
        compiler_params=pltpu.CompilerParams(vmem_limit_bytes=32 * MIB),
        cost_estimate=pl.CostEstimate(flops=10**6, bytes_accessed=10**5, transcendentals=0),
        name="subtree",
    )(*[in_hbm(x) for x in (pattern, rhs, dinv, off, upd)])


def exchange(x, mask):
    size = lax.axis_size("leaf") * lax.axis_size("front")
    return lax.ppermute(x, AXES, [(source, source ^ mask) for source in range(size)])


def spread(x, group, through=lambda x: x):
    masks = [0]
    apart = group // 2
    while apart >= 16:
        far = exchange(x, apart)
        x = through(x)
        x = jnp.concatenate([x, far], 0)
        masks = masks + [mask ^ apart for mask in masks]
        apart //= 2
        through = lambda value: value
    low = 2 * apart
    arrays = [(mask, exchange(x, mask)) for mask in range(low - 2, 0, -2)]
    if low > 4:
        arrays[0] = (low - 2, through(arrays[0][1]))
        arrays.append((0, x))
    else:
        arrays.append((0, through(x)))
    arrays += [(mask ^ 1, exchange(array, 1)) for mask, array in arrays]
    return [(array, [mask ^ high for high in masks]) for mask, array in arrays]


def factor_kernel(block, factor, own, out, own_out, held, sems):
    rows = held.shape[0]
    first, step = block[0] * block[1], held.shape[0] // sems.shape[0]
    loads = [
        pltpu.make_async_copy(
            factor.at[first + at : first + at + step], held.at[at : at + step], sems.at[at // step]
        )
        for at in range(0, rows, step)
    ]
    for load in loads:
        load.start()
    own_out[...] = own[...]
    for n, load in enumerate(loads):
        load.wait()
        high, low = halves(held[n * step : (n + 1) * step, :])
        out[n * step : (n + 1) * step, :] = high
        out[rows + n * step : rows + (n + 1) * step, :] = low


def prepare_factor(factor, block, own):
    rows, columns = block[1], factor.shape[1]
    return pl.pallas_call(
        functools.partial(factor_kernel, block),
        out_shape=(
            jax.ShapeDtypeStruct((2 * rows, columns), BF16),
            jax.ShapeDtypeStruct(own.shape, F32),
        ),
        in_specs=[HBM, VMEM],
        out_specs=(VMEM, VMEM),
        scratch_shapes=[
            pltpu.VMEM((rows, columns), F32),
            pltpu.SemaphoreType.DMA((max(1, min(4, rows // 16)),)),
        ],
        compiler_params=pltpu.CompilerParams(vmem_limit_bytes=16 * MIB),
        cost_estimate=pl.CostEstimate(
            flops=0, bytes_accessed=8 * rows * columns, transcendentals=0
        ),
        name="factor",
    )(in_hbm(factor), own)


def pivot_kernel(masks, shape, me, maps, *refs):
    count = len(masks)
    pieces, refs = refs[:count], refs[count:]
    own_h, refs = refs[: shape["h_count"]], refs[shape["h_count"] :]
    factor, refs = refs[0], refs[1:]
    earlier, rest = refs[: shape["earlier"]], refs[shape["earlier"] :]
    front = shape["front"]
    p_size, child_rows, span = shape["p_size"], shape["child_rows"], shape["child_span"]
    upd_rows = shape["upd_rows"]
    device = me[0]
    frontal, right = rest[-2:]
    h_rows = p_size // shape["group"]
    for n, start, mask in shape["h_parts"]:
        rank = jnp.bitwise_and(jnp.bitwise_xor(device, mask), shape["group"] - 1)
        row = rank * h_rows
        part = own_h[n][start : start + h_rows, :]
        if h_rows >= B:
            frontal[pl.ds(row // B, h_rows // B)] = part.reshape(h_rows // B, B, -1)
        else:
            inner = pl.multiple_of(lax.rem(row, B), h_rows)
            frontal[row // B, pl.ds(inner, h_rows), :] = part
    if upd_rows:
        frontal[p_size // B :, :, :] = jnp.zeros_like(frontal[p_size // B :, :, :])
    if shape["earlier"]:
        done = 0
        for array in earlier:
            rest[0][done : done + array.shape[0], :] = array[...]
            done += array.shape[0]
    step = min(child_rows, B)
    for piece, piece_masks in zip(pieces, masks, strict=True):
        for part, mask in enumerate(piece_masks):
            source = jnp.bitwise_xor(device, mask)
            if span:
                leaf = source // front
                row_of_map = shape["map_offset"] + leaf // span
                offset = (lax.rem(leaf, span) * front + lax.rem(source, front)) * child_rows
            else:
                row_of_map, offset = source, 0
            for at in range(0, child_rows, step):
                row = offset + at
                target = maps[row // B, row_of_map]
                inner = pl.multiple_of(lax.rem(row, B), step)
                here = part * child_rows + at
                if step == B:
                    frontal[target] += piece[here : here + step, :]
                else:
                    frontal[target, pl.ds(inner, step), :] += piece[here : here + step, :]
    right[...] = wide(frontal[: p_size // B].reshape(p_size, -1))
    z = product(factor[...], right[...])
    if shape["earlier"]:
        rest[0][done : done + z.shape[0], :] = z
    else:
        rest[0][...] = z
    if upd_rows:
        rank = jnp.bitwise_and(device, shape["group"] - 1)
        row = rank * upd_rows
        if upd_rows >= B:
            side = frontal[pl.ds(p_size // B + row // B, upd_rows // B)]
            rest[1][...] = side.reshape(upd_rows, -1)
        else:
            inner = pl.multiple_of(lax.rem(row, B), upd_rows)
            rest[1][...] = frontal[p_size // B + row // B, pl.ds(inner, upd_rows), :]


def solve_pivots(me, maps, pieces, h, factor, earlier, **shape):
    rows = factor.shape[0] // 2
    columns = pieces[0][0].shape[1]
    p_size = factor.shape[1]
    upd_rows = shape["upd_rows"]
    shape |= {
        "p_size": p_size,
        "earlier": len(earlier),
        "h_count": len(h[0]),
        "h_parts": h[1],
    }
    total = rows + sum(array.shape[0] for array in earlier)
    outs = [jax.ShapeDtypeStruct((total, columns), F32)]
    if upd_rows:
        outs.append(jax.ShapeDtypeStruct((upd_rows, columns), F32))
    frontal_rows = p_size + upd_rows * shape["group"]
    operands = [array for array, _ in pieces] + h[0] + [factor, *earlier]
    return pl.pallas_call(
        functools.partial(pivot_kernel, [masks for _, masks in pieces], shape),
        out_shape=tuple(outs),
        in_specs=[SMEM, SMEM] + [VMEM] * len(operands),
        out_specs=tuple(VMEM for _ in outs),
        scratch_shapes=[
            pltpu.VMEM((frontal_rows // B, B, columns), F32),
            pltpu.VMEM((p_size, 2 * columns), BF16),
        ],
        compiler_params=pltpu.CompilerParams(vmem_limit_bytes=24 * MIB),
        cost_estimate=pl.CostEstimate(
            flops=2 * rows * p_size * columns * 3, bytes_accessed=8 * 10**6, transcendentals=0
        ),
        name="pivots",
    )(me, maps, *operands)


def update_kernel(masks, group, me, *refs):
    count = len(masks)
    pieces = refs[:count]
    side, factor, w, right = refs[count:]
    rank = jnp.bitwise_and(me[0], group - 1)
    for piece, piece_masks in zip(pieces, masks, strict=True):
        rows = piece.shape[0] // len(piece_masks)
        for part, mask in enumerate(piece_masks):
            source = jnp.bitwise_xor(rank, mask)
            where = pl.ds(pl.multiple_of(source * rows, 16), rows)
            right[where, :] = wide(piece[part * rows : (part + 1) * rows, :])
    w[...] = side[...] - product(factor[...], right[...])


def solve_update(me, pieces, side, factor, group):
    rows, columns = side.shape
    p_size = factor.shape[1]
    return pl.pallas_call(
        functools.partial(update_kernel, [masks for _, masks in pieces], group),
        out_shape=jax.ShapeDtypeStruct((rows, columns), F32),
        in_specs=[SMEM] + [VMEM] * (len(pieces) + 2),
        out_specs=VMEM,
        scratch_shapes=[pltpu.VMEM((p_size, 2 * columns), BF16)],
        compiler_params=pltpu.CompilerParams(vmem_limit_bytes=24 * MIB),
        cost_estimate=pl.CostEstimate(
            flops=2 * rows * p_size * columns * 3, bytes_accessed=8 * 10**6, transcendentals=0
        ),
        name="update",
    )(me, *[array for array, _ in pieces], side, factor)


def join_kernel(plans, after, *refs):
    del after
    outs = refs[len(refs) - len(plans) :]
    for out, parts in zip(outs, plans, strict=True):
        at = 0
        for n, start, stop in parts:
            out[at : at + stop - start, :] = refs[n][start:stop, :]
            at += stop - start


def join_rows(after, arrays, plans):
    totals = [sum(stop - start for _, start, stop in parts) for parts in plans]
    return pl.pallas_call(
        functools.partial(join_kernel, plans),
        out_shape=tuple(
            jax.ShapeDtypeStruct((total, arrays[0].shape[1]), F32) for total in totals
        ),
        in_specs=[ANY] + [VMEM] * len(arrays),
        out_specs=tuple(VMEM for _ in totals),
        compiler_params=pltpu.CompilerParams(vmem_limit_bytes=8 * MIB),
        cost_estimate=pl.CostEstimate(flops=0, bytes_accessed=10**6, transcendentals=0),
        name="join",
    )(after, *arrays)


class Rhs:
    def __init__(self, front_rhs, p_size, groups):
        self.rows = [p_size // group for group in groups]
        self.total = front_rhs.shape[0]
        self.masks = [0, 2]
        self.held = [front_rhs, exchange(front_rhs, 2)]
        self.level = 0

    def next_level(self, after):
        rows, group = self.rows[self.level], 2 * len(self.masks)
        span = sum(self.rows[self.level :])
        parts = [
            (n, at * span) for n, array in enumerate(self.held) for at in range(array.shape[0] // span)
        ]
        plans = [[(n, at, at + rows) for n, at in parts]]
        last = self.level + 1 == len(self.rows)
        if not last:
            plans.append([(n, at + rows, at + span) for n, at in parts])
        mine, *rest = join_rows(after, self.held, plans)
        other = exchange(mine, 1)
        place = [(0, at * rows, mask) for at, mask in enumerate(self.masks)]
        place += [(1, at * rows, mask ^ 1) for at, mask in enumerate(self.masks)]
        if not last:
            self.held = [rest[0], exchange(rest[0], group)]
            self.masks = self.masks + [mask ^ group for mask in self.masks]
        self.level += 1
        return [mine, other], place


def per_device(
    sub_rhs,
    sub_dinv,
    sub_off,
    sub_pattern,
    sub_update,
    sub_map,
    front_rhs,
    piv_inverse,
    upd_factor,
    front_map,
):
    front_size = lax.axis_size("front")
    leaf_size = lax.axis_size("leaf")
    level_count = leaf_size.bit_length()
    p_size = piv_inverse.shape[1]
    u_size = upd_factor.shape[0] * front_size * leaf_size // (2 * (leaf_size - 1))
    me = (lax.axis_index("leaf") * front_size + lax.axis_index("front")).reshape(1)

    size = front_size * leaf_size
    groups = [front_size * 2**level for level in range(level_count)]
    columns = sub_rhs.shape[1]
    sizes = [p_size // group for group in groups]
    rhs = Rhs(front_rhs, p_size, groups)

    flat, update = solve_subtree(sub_rhs, sub_dinv, sub_off, sub_pattern.T, sub_update)
    kept = []

    def keep(factor, block):
        def through(x):
            factor_rows, x = prepare_factor(factor, block, x)
            kept[:] = [factor_rows]
            return x

        return through

    pieces = spread(update, front_size, keep(piv_inverse, (0, sizes[0])))
    factor = kept[0]
    h = [rhs.next_level(update)]
    maps, map_offset, child_span = sub_map.T, 0, 0
    earlier = []
    for level in range(1, level_count + 1):
        group = groups[level - 1]
        last = level == level_count
        out = solve_pivots(
            me,
            maps,
            pieces,
            h[level - 1],
            factor,
            earlier if last else [],
            front=front_size,
            child_rows=update.shape[0],
            child_span=child_span,
            map_offset=map_offset,
            upd_rows=0 if last else u_size // group,
            group=group,
        )
        if last:
            return flat, out[0]
        z, side = out
        earlier.append(z)
        if len(h) < level_count:
            h.append(rhs.next_level(z))
        z_pieces = spread(z, group, keep(upd_factor, (2**level - 2, u_size // group)))
        update = solve_update(me, z_pieces, side, kept[0], group)
        pieces = spread(update, 2 * group, keep(piv_inverse, (2 ** (level + 1) - 2, sizes[level])))
        factor = kept[0]
        if len(h) < level_count:
            h.append(rhs.next_level(update))
        map_offset = 0 if level == 1 else map_offset + leaf_size // child_span
        child_span = 2 ** (level - 1)
        maps = front_map.T


def solution(mesh):
    split = P(AXES)
    return jax.shard_map(
        per_device,
        mesh=mesh,
        in_specs=(split, split, split, split, split, P(), split, split, split, P()),
        out_specs=(split, split),
        check_vma=False,
    )
```

time: 182 us -> 146 us (0.80)
  local copies, waits for them, and re-layouts: 38.5 us -> 6.15 us
  Pallas kernels: 19.8 us -> 33.8 us
  waiting for transfers between devices: 59.5 us -> 46.5 us
  between operations: 13.9 us -> 0.93 us
  starting transfers between devices: 49.2 us -> 57.9 us
    unnamed x40 -> x16, local copies, waits for them, and re-layouts: 32.4 us -> 6.14 us
    pallas_call x1 -> x12, Pallas kernels: 8.1 us -> 22 us  [the longest x7 12.3 us: prepare_factor(): pl.pallas_call(functools.partial(factor_kernel, block), out_shape=(jax.Sh...]
    ppermute x66 -> x74, waiting for transfers between devices: 59.4 us -> 46.5 us  [exchange(): lax.ppermute(x, AXES, [(source, source ^ mask) for source in range(size)])]
    ppermute x66 -> x74, starting transfers between devices: 49 us -> 57.9 us  [exchange(): lax.ppermute(x, AXES, [(source, source ^ mask) for source in range(size)])]
    slice x4 -> x0, local copies, waits for them, and re-layouts: 6.09 us -> none  [per_device(): mine = front_rhs[offset:offset + rows]]
  transfers between devices with their start and end apart: 70 -> 74, of which waited for: 43 -> 37; matrix products, arithmetic and copies ran while one was open for 3% -> 0% of each run, Pallas kernels for 10% -> 22%
where the time goes in v2:
time: 146 us; the launch traced here: 145 us
  starting transfers between devices  57.9 us (40%)
  waiting for transfers between devices  46.5 us (32%)
  Pallas kernels  33.8 us (23%)
  local copies, waits for them, and re-layouts  6.15 us (4%)
    ppermute x74, starting transfers between devices, exchange(): lax.ppermute(x, AXES, [(source, source ^ mask) for source in range(size)])  57.9 us
    ppermute x74, waiting for transfers between devices, exchange(): lax.ppermute(x, AXES, [(source, source ^ mask) for source in range(size)])  46.5 us
    pallas_call x7, Pallas kernels, prepare_factor(): pl.pallas_call(functools.partial(factor_kernel, block), out_shape=(jax.Sh...  12.3 us
    pallas_call x4, Pallas kernels, solve_pivots(): pl.pallas_call(functools.partial(pivot_kernel, [masks for _, masks in pie...  8.83 us
    pallas_call x1, Pallas kernels, solve_subtree(): pl.pallas_call(functools.partial(subtree_kernel, bounds), out_shape=(jax....  8.48 us
    unnamed x16, local copies, waits for them, and re-layouts  6.14 us
    pallas_call x3, Pallas kernels, solve_update(): pl.pallas_call(functools.partial(update_kernel, [masks for _, masks in pi...  2.98 us
  transfers between devices with their start and end apart: 74, of which 37 were waited for; matrix products, arithmetic and copies ran while one was open for 0% of the time, Pallas kernels for 22%

profile of v2, /device:TPU:0, one launch (start us, length us, event | category | flops | bytes accessed | tf_op | source)
XLA Modules:
  0.0 145.2 jit_solution(12478663289474184600)
XLA Ops:
  0.6 3.0 %collective-permute-start.3 = (f32[960,128]{1,0:T(8,128)}, f32[960,128]{1,0:T(8,128)S(1)}, u32[]{:S(2)}, u32[]{:S(2)}) collective-permute-start(f32[960,128]{1,0:T(8,128)} %refs_0_.1), channel_id=1, source_target_pairs={{0,2},{1,3},{2,0},{3,1},{4,6},{5,7},{6,4},{7,5},{8,10},{9,11},{10,... | collective-permute-start | bytes 1474568 | tf_op jit(solution)/shard_map/ppermute | solution.py:147
  3.6 8.5 %subtree.1 = (f32[3072,128]{1,0:T(8,128)}, f32[256,128]{1,0:T(8,128)S(1)}) custom-call(s32[2,23]{1,0:T(2,128)} %bitcast.8, f32[3072,128]{1,0:T(8,128)} %rhs_in.1, f32[24,128,128]{2,1,0:T(8,128)} %dinv_in.1, f32[23,2,128,128]{3,2,1,0:T(8,128)} %off_in.1, f32[256,3072]{1,0:T(8,128)} %upd_in.1), custom_call_target="tpu_custom_call" | custom-call | flops 1000000 | bytes 100000 | tf_op jit(solution)/shard_map/subtree/pallas_call | solution.py:118
  12.1 2.9 %collective-permute-done.3.refs_1_ = f32[960,128]{1,0:T(8,128)S(1)} collective-permute-done((f32[960,128]{1,0:T(8,128)}, f32[960,128]{1,0:T(8,128)S(1)}, u32[]{:S(2)}, u32[]{:S(2)}) %collective-permute-start.3) | collective-permute-done | bytes 491552 | tf_op jit(solution)/shard_map/ppermute | solution.py:147
  15.2 1.8 %collective-permute-start = (f32[256,128]{1,0:T(8,128)S(1)}, f32[256,128]{1,0:T(8,128)S(1)}, u32[]{:S(2)}, u32[]{:S(2)}) collective-permute-start(f32[256,128]{1,0:T(8,128)S(1)} %get-tuple-element.31.own.after), channel_id=1, source_target_pairs={{0,2},{1,3},{2,0},{3,1},{4,6},{5,7},{6,4},{7,5},{8,10},{9,11},{10,... | collective-permute-start | bytes 393224 | tf_op jit(solution)/shard_map/ppermute | solution.py:147
  17.0 2.3 %factor.14 = (bf16[1024,2048]{1,0:T(8,128)(2,1)S(1)}, f32[256,128]{1,0:T(8,128)S(1)}) custom-call(f32[960,2048]{1,0:T(8,128)} %factor.27, f32[256,128]{1,0:T(8,128)S(1)} %get-tuple-element.31.own.after), custom_call_target="tpu_custom_call" | custom-call | bytes 8388608 | tf_op jit(solution)/shard_map/factor/pallas_call | solution.py:192
  19.4 2.0 %copy-done = bf16[1024,2048]{1,0:T(8,128)(2,1)} copy-done((bf16[1024,2048]{1,0:T(8,128)(2,1)}, bf16[1024,2048]{1,0:T(8,128)(2,1)S(1)}, u32[]{:S(2)}) %copy-start) | copy-done | bytes 4194328
  21.9 1.5 %collective-permute-start.15 = (f32[896,128]{1,0:T(8,128)S(1)}, f32[896,128]{1,0:T(8,128)S(1)}, u32[]{:S(2)}, u32[]{:S(2)}) collective-permute-start(f32[896,128]{1,0:T(8,128)S(1)} %get-tuple-element.40.refs_0_), channel_id=1, source_target_pairs={{0,4},{1,5},{2,6},{3,7},{4,0},{5,1},{6,2},{7,3},{8,12},{9,13},{10,... | collective-permute-start | bytes 1376264 | tf_op jit(solution)/shard_map/ppermute | solution.py:147
  23.5 2.2 %copy-done.1 = bf16[1024,2048]{1,0:T(8,128)(2,1)S(1)} copy-done((bf16[1024,2048]{1,0:T(8,128)(2,1)S(1)}, bf16[1024,2048]{1,0:T(8,128)(2,1)}, u32[]{:S(2)}) %copy-start.1) | copy-done | bytes 4194328
  25.7 2.0 %pivots.4 = (f32[512,128]{1,0:T(8,128)S(1)}, f32[512,128]{1,0:T(8,128)S(1)}) custom-call(s32[1]{0:T(128)} %bitcast.1.me, s32[2,32]{1,0:T(2,128)S(1)} %bitcast.7, f32[256,128]{1,0:T(8,128)S(1)} %collective-permute-done.refs_0_, f32[256,128]{1,0:T(8,128)S(1)} %get-tuple-element.32.refs_1_, f32[256,128]{1,0:T(8,128)S(1)} %collective-permute-done.1.refs_2_, ...), custom_call_target="tpu_custom_call" | custom-call | flops 805306368 | bytes 8000000 | tf_op jit(solution)/shard_map/pivots/pallas_call | solution.py:293
  27.7 1.0 collective-permute-start.5
  28.7 2.3 %factor.16 = (bf16[1024,2048]{1,0:T(8,128)(2,1)S(1)}, f32[512,128]{1,0:T(8,128)S(1)}) custom-call(f32[896,2048]{1,0:T(8,128)} %factor.25, f32[512,128]{1,0:T(8,128)S(1)} %get-tuple-element.35.own.after.refs_19_), custom_call_target="tpu_custom_call" | custom-call | bytes 8388608 | tf_op jit(solution)/shard_map/factor/pallas_call | solution.py:192
  31.1 4.7 %collective-permute-done.5.refs_0_ = f32[512,128]{1,0:T(8,128)S(1)} collective-permute-done((f32[512,128]{1,0:T(8,128)S(1)}, f32[512,128]{1,0:T(8,128)S(1)}, u32[]{:S(2)}, u32[]{:S(2)}) %collective-permute-start.5) | collective-permute-done | bytes 262176 | tf_op jit(solution)/shard_map/ppermute | solution.py:147
  36.5 0.9 collective-permute-done.6.refs_2_
  37.4 1.5 %update.3.refs_3_.after = f32[512,128]{1,0:T(8,128)S(1)} custom-call(s32[1]{0:T(128)} %bitcast.1.me, f32[512,128]{1,0:T(8,128)S(1)} %collective-permute-done.5.refs_0_, f32[512,128]{1,0:T(8,128)S(1)} %get-tuple-element.36.refs_1_, f32[512,128]{1,0:T(8,128)S(1)} %collective-permute-done.6.refs_2_, f32[512,128]{1,0:T(8,128)S(1)} %collective-permute-done.7.refs_3_, ...), custom_call_target="tpu_custom_call" | custom-call | flops 805306368 | bytes 8000000 | tf_op jit(solution)/shard_map/update/pallas_call | solution.py:327
  38.9 2.1 %collective-permute-start.8 = (f32[512,128]{1,0:T(8,128)S(1)}, f32[512,128]{1,0:T(8,128)S(1)}, u32[]{:S(2)}, u32[]{:S(2)}) collective-permute-start(f32[512,128]{1,0:T(8,128)S(1)} %update.3.refs_3_.after), channel_id=1, source_target_pairs={{0,6},{1,7},{2,4},{3,5},{4,2},{5,3},{6,0},{7,1},{8,14},{9,15},{10,... | collective-permute-start | bytes 786440 | tf_op jit(solution)/shard_map/ppermute | solution.py:147
  40.9 0.8 collective-permute-start.9
  42.4 1.6 %collective-permute-start.39 = (f32[768,128]{1,0:T(8,128)S(1)}, f32[768,128]{1,0:T(8,128)}, u32[]{:S(2)}, u32[]{:S(2)}) collective-permute-start(f32[768,128]{1,0:T(8,128)S(1)} %get-tuple-element.48.refs_0_), channel_id=1, source_target_pairs={{0,8},{1,9},{2,10},{3,11},{4,12},{5,13},{6,14},{7,15},{8,0},{9,1},... | collective-permute-start | bytes 1179656 | tf_op jit(solution)/shard_map/ppermute | solution.py:147
  44.0 5.0 %collective-permute-done.8.own = f32[512,128]{1,0:T(8,128)S(1)} collective-permute-done((f32[512,128]{1,0:T(8,128)S(1)}, f32[512,128]{1,0:T(8,128)S(1)}, u32[]{:S(2)}, u32[]{:S(2)}) %collective-permute-start.8) | collective-permute-done | bytes 262176 | tf_op jit(solution)/shard_map/ppermute | solution.py:147
  49.0 2.3 %factor.18 = (bf16[512,2048]{1,0:T(8,128)(2,1)S(1)}, f32[512,128]{1,0:T(8,128)}) custom-call(f32[960,2048]{1,0:T(8,128)} %factor.27, f32[512,128]{1,0:T(8,128)S(1)} %collective-permute-done.8.own), custom_call_target="tpu_custom_call" | custom-call | bytes 4194304 | tf_op jit(solution)/shard_map/factor/pallas_call | solution.py:192
  51.3 0.8 copy-done.2
  52.6 1.3 collective-permute-done.9.refs_1_
  54.5 1.3 collective-permute-done.12.refs_5_
  56.2 1.0 copy-done.3
  57.2 2.8 %pivots.5 = (f32[256,128]{1,0:T(8,128)S(1)}, f32[256,128]{1,0:T(8,128)S(1)}) custom-call(s32[1]{0:T(128)} %bitcast.1.me, s32[16,14]{1,0:T(8,128)S(1)} %bitcast.4, f32[512,128]{1,0:T(8,128)} %get-tuple-element.39.refs_0_, f32[512,128]{1,0:T(8,128)} %collective-permute-done.9.refs_1_, f32[512,128]{1,0:T(8,128)} %collective-permute-done.10.refs_2_, ...), custom_call_target="tpu_custom_call" | custom-call | flops 402653184 | bytes 8000000 | tf_op jit(solution)/shard_map/pivots/pallas_call | solution.py:293
  60.0 1.8 %collective-permute-start.17 = (f32[256,128]{1,0:T(8,128)S(1)}, f32[256,128]{1,0:T(8,128)S(1)}, u32[]{:S(2)}, u32[]{:S(2)}) collective-permute-start(f32[256,128]{1,0:T(8,128)S(1)} %get-tuple-element.43.refs_3_.after.refs_20_), channel_id=1, source_target_pairs={{0,6},{1,7},{2,4},{3,5},{4,2},{5,3},{6,0},{7,1},{8,14},{9,15},{10,... | collective-permute-start | bytes 393224 | tf_op jit(solution)/shard_map/ppermute | solution.py:147
  61.8 1.0 collective-permute-start.18
  63.5 1.0 join.6
  65.2 2.1 %collective-permute-done.17.own = f32[256,128]{1,0:T(8,128)S(1)} collective-permute-done((f32[256,128]{1,0:T(8,128)S(1)}, f32[256,128]{1,0:T(8,128)S(1)}, u32[]{:S(2)}, u32[]{:S(2)}) %collective-permute-start.17) | collective-permute-done | bytes 131104 | tf_op jit(solution)/shard_map/ppermute | solution.py:147
  67.3 1.6 %factor.20 = (bf16[512,2048]{1,0:T(8,128)(2,1)S(1)}, f32[256,128]{1,0:T(8,128)S(1)}) custom-call(f32[896,2048]{1,0:T(8,128)} %factor.25, f32[256,128]{1,0:T(8,128)S(1)} %collective-permute-done.17.own), custom_call_target="tpu_custom_call" | custom-call | bytes 4194304 | tf_op jit(solution)/shard_map/factor/pallas_call | solution.py:192
  69.8 2.6 %collective-permute-start.72 = (f32[512,128]{1,0:T(8,128)S(1)}, f32[512,128]{1,0:T(8,128)S(1)}, u32[]{:S(2)}, u32[]{:S(2)}) collective-permute-start(f32[512,128]{1,0:T(8,128)S(1)} %get-tuple-element.56.refs_0_), channel_id=1, source_target_pairs={{0,16},{1,17},{2,18},{3,19},{4,20},{5,21},{6,22},{7,23},{8,24},{9,... | collective-permute-start | bytes 786440 | tf_op jit(solution)/shard_map/ppermute | solution.py:147
  72.4 0.9 update.4.refs_7_
  73.3 2.8 %collective-permute-start.24 = (f32[256,128]{1,0:T(8,128)S(1)}, f32[256,128]{1,0:T(8,128)S(1)}, u32[]{:S(2)}, u32[]{:S(2)}) collective-permute-start(f32[256,128]{1,0:T(8,128)S(1)} %update.4.refs_7_), channel_id=1, source_target_pairs={{0,14},{1,15},{2,12},{3,13},{4,10},{5,11},{6,8},{7,9},{8,6},{9,7},... | collective-permute-start | bytes 393224 | tf_op jit(solution)/shard_map/ppermute | solution.py:147
  76.1 0.9 collective-permute-start.25
  77.0 1.7 %collective-permute-start.26 = (f32[256,128]{1,0:T(8,128)S(1)}, f32[256,128]{1,0:T(8,128)S(1)}, u32[]{:S(2)}, u32[]{:S(2)}) collective-permute-start(f32[256,128]{1,0:T(8,128)S(1)} %update.4.refs_7_), channel_id=1, source_target_pairs={{0,10},{1,11},{2,8},{3,9},{4,14},{5,15},{6,12},{7,13},{8,2},{9,3},... | collective-permute-start | bytes 393224 | tf_op jit(solution)/shard_map/ppermute | solution.py:147
  78.8 6.1 %collective-permute-done.72.refs_1_ = f32[512,128]{1,0:T(8,128)S(1)} collective-permute-done((f32[512,128]{1,0:T(8,128)S(1)}, f32[512,128]{1,0:T(8,128)S(1)}, u32[]{:S(2)}, u32[]{:S(2)}) %collective-permute-start.72) | collective-permute-done | bytes 262176 | tf_op jit(solution)/shard_map/ppermute | solution.py:147
  85.5 2.5 %collective-permute-start.28 = (f32[256,128]{1,0:T(8,128)S(1)}, f32[256,128]{1,0:T(8,128)S(1)}, u32[]{:S(2)}, u32[]{:S(2)}) collective-permute-start(f32[256,128]{1,0:T(8,128)S(1)} %update.4.refs_7_), channel_id=1, source_target_pairs={{0,6},{1,7},{2,4},{3,5},{4,2},{5,3},{6,0},{7,1},{8,14},{9,15},{10,... | collective-permute-start | bytes 393224 | tf_op jit(solution)/shard_map/ppermute | solution.py:147
  87.9 1.3 factor.22
  89.2 1.0 collective-permute-start.29
  90.6 1.0 collective-permute-done.26.refs_2_
  91.6 1.2 collective-permute-done.27.refs_3_
  93.6 2.4 %collective-permute-done.29.refs_5_ = f32[256,128]{1,0:T(8,128)S(1)} collective-permute-done((f32[256,128]{1,0:T(8,128)S(1)}, f32[256,128]{1,0:T(8,128)S(1)}, u32[]{:S(2)}, u32[]{:S(2)}) %collective-permute-start.29) | collective-permute-done | bytes 131104 | tf_op jit(solution)/shard_map/ppermute | solution.py:147
  98.4 1.6 %pivots.6 = (f32[128,128]{1,0:T(8,128)S(1)}, f32[128,128]{1,0:T(8,128)S(1)}) custom-call(s32[1]{0:T(128)} %bitcast.1.me, s32[16,14]{1,0:T(8,128)S(1)} %bitcast.5, f32[256,128]{1,0:T(8,128)S(1)} %get-tuple-element.47.refs_0_, f32[256,128]{1,0:T(8,128)S(1)} %collective-permute-done.25.refs_1_, f32[256,128]{1,0:T(8,128)S(1)} %collective-permute-done.26.refs_2_, ...), custom_call_target="tpu_custom_call" | custom-call | flops 201326592 | bytes 8000000 | tf_op jit(solution)/shard_map/pivots/pallas_call | solution.py:293
  100.0 1.1 collective-permute-start.41
  101.1 2.3 %collective-permute-start.42 = (f32[128,128]{1,0:T(8,128)S(1)}, f32[128,128]{1,0:T(8,128)S(1)}, u32[]{:S(2)}, u32[]{:S(2)}) collective-permute-start(f32[128,128]{1,0:T(8,128)S(1)} %get-tuple-element.51.refs_7_.refs_21_), channel_id=1, source_target_pairs={{0,12},{1,13},{2,14},{3,15},{4,8},{5,9},{6,10},{7,11},{8,4},{9,5},... | collective-permute-start | bytes 196616 | tf_op jit(solution)/shard_map/ppermute | solution.py:147
  103.4 1.0 collective-permute-start.43
  104.4 1.5 %collective-permute-start.44 = (f32[128,128]{1,0:T(8,128)S(1)}, f32[128,128]{1,0:T(8,128)S(1)}, u32[]{:S(2)}, u32[]{:S(2)}) collective-permute-start(f32[128,128]{1,0:T(8,128)S(1)} %get-tuple-element.51.refs_7_.refs_21_), channel_id=1, source_target_pairs={{0,8},{1,9},{2,10},{3,11},{4,12},{5,13},{6,14},{7,15},{8,0},{9,1},... | collective-permute-start | bytes 196616 | tf_op jit(solution)/shard_map/ppermute | solution.py:147
  105.9 1.4 collective-permute-done.41.own
  107.3 1.1 collective-permute-start.45
  108.4 1.0 collective-permute-start.46
  109.4 1.4 collective-permute-start.47
  110.8 1.3 factor.24
  116.8 1.2 factor.26
  117.9 2.6 %collective-permute-start.56 = (f32[128,128]{1,0:T(8,128)S(1)}, f32[128,128]{1,0:T(8,128)S(1)}, u32[]{:S(2)}, u32[]{:S(2)}) collective-permute-start(f32[128,128]{1,0:T(8,128)S(1)} %update.5.own), channel_id=1, source_target_pairs={{0,16},{1,17},{2,18},{3,19},{4,20},{5,21},{6,22},{7,23},{8,24},{9,... | collective-permute-start | bytes 196616 | tf_op jit(solution)/shard_map/ppermute | solution.py:147
  120.5 4.0 %collective-permute-done.56 = f32[128,128]{1,0:T(8,128)S(1)} collective-permute-done((f32[128,128]{1,0:T(8,128)S(1)}, f32[128,128]{1,0:T(8,128)S(1)}, u32[]{:S(2)}, u32[]{:S(2)}) %collective-permute-start.56) | collective-permute-done | bytes 65568 | tf_op jit(solution)/shard_map/ppermute | solution.py:147
  124.6 1.3 collective-permute-start.57
  125.8 2.4 %collective-permute-start.58 = (f32[256,128]{1,0:T(8,128)S(1)}, f32[256,128]{1,0:T(8,128)S(1)}, u32[]{:S(2)}, u32[]{:S(2)}) collective-permute-start(f32[256,128]{1,0:T(8,128)S(1)} %constant_dynamic-update-slice_fusion.refs_7_), channel_id=1, source_target_pairs={{0,12},{1,13},{2,14},{3,15},{4,8},{5,9},{6,10},{7,11},{8,4},{9,5},... | collective-permute-start | bytes 393224 | tf_op jit(solution)/shard_map/ppermute | solution.py:147
  128.9 1.5 %collective-permute-start.60 = (f32[256,128]{1,0:T(8,128)S(1)}, f32[256,128]{1,0:T(8,128)S(1)}, u32[]{:S(2)}, u32[]{:S(2)}) collective-permute-start(f32[256,128]{1,0:T(8,128)S(1)} %constant_dynamic-update-slice_fusion.refs_7_), channel_id=1, source_target_pairs={{0,8},{1,9},{2,10},{3,11},{4,12},{5,13},{6,14},{7,15},{8,0},{9,1},... | collective-permute-start | bytes 393224 | tf_op jit(solution)/shard_map/ppermute | solution.py:147
  130.4 1.7 %collective-permute-start.61 = (f32[256,128]{1,0:T(8,128)S(1)}, f32[256,128]{1,0:T(8,128)S(1)}, u32[]{:S(2)}, u32[]{:S(2)}) collective-permute-start(f32[256,128]{1,0:T(8,128)S(1)} %constant_dynamic-update-slice_fusion.refs_7_), channel_id=1, source_target_pairs={{0,6},{1,7},{2,4},{3,5},{4,2},{5,3},{6,0},{7,1},{8,14},{9,15},{10,... | collective-permute-start | bytes 393224 | tf_op jit(solution)/shard_map/ppermute | solution.py:147
  132.7 1.6 %collective-permute-start.62 = (f32[256,128]{1,0:T(8,128)S(1)}, f32[256,128]{1,0:T(8,128)S(1)}, u32[]{:S(2)}, u32[]{:S(2)}) collective-permute-start(f32[256,128]{1,0:T(8,128)S(1)} %constant_dynamic-update-slice_fusion.refs_7_), channel_id=1, source_target_pairs={{0,4},{1,5},{2,6},{3,7},{4,0},{5,1},{6,2},{7,3},{8,12},{9,13},{10,... | collective-permute-start | bytes 393224 | tf_op jit(solution)/shard_map/ppermute | solution.py:147
  134.4 1.4 collective-permute-done.58.refs_1_
  136.4 1.4 collective-permute-done.59.refs_2_
  137.7 1.4 collective-permute-done.60.refs_3_
  139.8 1.0 collective-permute-done.63.refs_6_
  142.8 2.4 %pivots.7 = f32[960,128]{1,0:T(8,128)} custom-call(s32[1]{0:T(128)} %bitcast.1.me, s32[16,14]{1,0:T(8,128)S(1)} %bitcast.6, f32[256,128]{1,0:T(8,128)S(1)} %collective-permute-done.57.refs_0_, f32[256,128]{1,0:T(8,128)S(1)} %collective-permute-done.58.refs_1_, f32[256,128]{1,0:T(8,128)S(1)} %collective-permute-done.59.refs_2_, ...), custom_call_target="tpu_custom_call" | custom-call | flops 100663296 | bytes 8000000 | tf_op jit(solution)/shard_map/pivots/pallas_call | solution.py:293
  (120 shorter events, 19.0 us)
Async XLA Ops:
  0.6 14.4 %collective-permute-start.3 = (f32[960,128]{1,0:T(8,128)}, f32[960,128]{1,0:T(8,128)S(1)}, u32[]{:S(2)}, u32[]{:S(2)}) collective-permute-start(f32[960,128]{1,0:T(8,128)} %refs_0_.1), channel_id=1, source_target_pairs={{0,2},{1,3},{2,0},{3,1},{4,6},{5,7},{6,4},{7,5},{8,10},{9,11},{10,... | collective-permute-start | bytes 1474568 | tf_op jit(solution)/shard_map/ppermute | solution.py:147
  15.1 8.3 %collective-permute-start.4 = (f32[1024,128]{1,0:T(8,128)S(1)}, f32[1024,128]{1,0:T(8,128)S(1)}, u32[]{:S(2)}, u32[]{:S(2)}) collective-permute-start(f32[1024,128]{1,0:T(8,128)S(1)} %get-tuple-element.33.refs_4_), channel_id=1, source_target_pairs={{0,1},{1,0},{2,3},{3,2},{4,5},{5,4},{6,7},{7,6},{8,9},{9,8},{10,11... | collective-permute-start | bytes 1572872 | tf_op jit(solution)/shard_map/ppermute | solution.py:147
  15.2 6.3 %collective-permute-start = (f32[256,128]{1,0:T(8,128)S(1)}, f32[256,128]{1,0:T(8,128)S(1)}, u32[]{:S(2)}, u32[]{:S(2)}) collective-permute-start(f32[256,128]{1,0:T(8,128)S(1)} %get-tuple-element.31.own.after), channel_id=1, source_target_pairs={{0,2},{1,3},{2,0},{3,1},{4,6},{5,7},{6,4},{7,5},{8,10},{9,11},{10,... | collective-permute-start | bytes 393224 | tf_op jit(solution)/shard_map/ppermute | solution.py:147
  21.4 2.0 %collective-permute-start.2 = (f32[256,128]{1,0:T(8,128)S(1)}, f32[256,128]{1,0:T(8,128)S(1)}, u32[]{:S(2)}, u32[]{:S(2)}) collective-permute-start(f32[256,128]{1,0:T(8,128)S(1)} %get-tuple-element.32.refs_1_), channel_id=1, source_target_pairs={{0,1},{1,0},{2,3},{3,2},{4,5},{5,4},{6,7},{7,6},{8,9},{9,8},{10,11... | collective-permute-start | bytes 393224 | tf_op jit(solution)/shard_map/ppermute | solution.py:147
  21.6 1.9 %collective-permute-start.1 = (f32[256,128]{1,0:T(8,128)S(1)}, f32[256,128]{1,0:T(8,128)S(1)}, u32[]{:S(2)}, u32[]{:S(2)}) collective-permute-start(f32[256,128]{1,0:T(8,128)S(1)} %collective-permute-done.refs_0_), channel_id=1, source_target_pairs={{0,1},{1,0},{2,3},{3,2},{4,5},{5,4},{6,7},{7,6},{8,9},{9,8},{10,11... | collective-permute-start | bytes 393224 | tf_op jit(solution)/shard_map/ppermute | solution.py:147
  21.9 13.9 %collective-permute-start.15 = (f32[896,128]{1,0:T(8,128)S(1)}, f32[896,128]{1,0:T(8,128)S(1)}, u32[]{:S(2)}, u32[]{:S(2)}) collective-permute-start(f32[896,128]{1,0:T(8,128)S(1)} %get-tuple-element.40.refs_0_), channel_id=1, source_target_pairs={{0,4},{1,5},{2,6},{3,7},{4,0},{5,1},{6,2},{7,3},{8,12},{9,13},{10,... | collective-permute-start | bytes 1376264 | tf_op jit(solution)/shard_map/ppermute | solution.py:147
  27.7 8.2 %collective-permute-start.5 = (f32[512,128]{1,0:T(8,128)S(1)}, f32[512,128]{1,0:T(8,128)S(1)}, u32[]{:S(2)}, u32[]{:S(2)}) collective-permute-start(f32[512,128]{1,0:T(8,128)S(1)} %get-tuple-element.35.own.after.refs_19_), channel_id=1, source_target_pairs={{0,2},{1,3},{2,0},{3,1},{4,6},{5,7},{6,4},{7,5},{8,10},{9,11},{10,... | collective-permute-start | bytes 786440 | tf_op jit(solution)/shard_map/ppermute | solution.py:147
  31.1 5.4 %collective-permute-start.7 = (f32[512,128]{1,0:T(8,128)S(1)}, f32[512,128]{1,0:T(8,128)S(1)}, u32[]{:S(2)}, u32[]{:S(2)}) collective-permute-start(f32[512,128]{1,0:T(8,128)S(1)} %get-tuple-element.36.refs_1_), channel_id=1, source_target_pairs={{0,1},{1,0},{2,3},{3,2},{4,5},{5,4},{6,7},{7,6},{8,9},{9,8},{10,11... | collective-permute-start | bytes 786440 | tf_op jit(solution)/shard_map/ppermute | solution.py:147
  35.8 1.5 %collective-permute-start.6 = (f32[512,128]{1,0:T(8,128)S(1)}, f32[512,128]{1,0:T(8,128)S(1)}, u32[]{:S(2)}, u32[]{:S(2)}) collective-permute-start(f32[512,128]{1,0:T(8,128)S(1)} %collective-permute-done.5.refs_0_), channel_id=1, source_target_pairs={{0,1},{1,0},{2,3},{3,2},{4,5},{5,4},{6,7},{7,6},{8,9},{9,8},{10,11... | collective-permute-start | bytes 786440 | tf_op jit(solution)/shard_map/ppermute | solution.py:147
  35.9 15.4 %collective-permute-start.16 = (f32[1024,128]{1,0:T(8,128)S(1)}, f32[1024,128]{1,0:T(8,128)S(1)}, u32[]{:S(2)}, u32[]{:S(2)}) collective-permute-start(f32[1024,128]{1,0:T(8,128)S(1)} %get-tuple-element.41.refs_8_), channel_id=1, source_target_pairs={{0,1},{1,0},{2,3},{3,2},{4,5},{5,4},{6,7},{7,6},{8,9},{9,8},{10,11... | collective-permute-start | bytes 1572872 | tf_op jit(solution)/shard_map/ppermute | solution.py:147
  38.9 10.2 %collective-permute-start.8 = (f32[512,128]{1,0:T(8,128)S(1)}, f32[512,128]{1,0:T(8,128)S(1)}, u32[]{:S(2)}, u32[]{:S(2)}) collective-permute-start(f32[512,128]{1,0:T(8,128)S(1)} %update.3.refs_3_.after), channel_id=1, source_target_pairs={{0,6},{1,7},{2,4},{3,5},{4,2},{5,3},{6,0},{7,1},{8,14},{9,15},{10,... | collective-permute-start | bytes 786440 | tf_op jit(solution)/shard_map/ppermute | solution.py:147
  40.9 13.0 %collective-permute-start.9 = (f32[512,128]{1,0:T(8,128)S(1)}, f32[512,128]{1,0:T(8,128)}, u32[]{:S(2)}, u32[]{:S(2)}) collective-permute-start(f32[512,128]{1,0:T(8,128)S(1)} %update.3.refs_3_.after), channel_id=1, source_target_pairs={{0,4},{1,5},{2,6},{3,7},{4,0},{5,1},{6,2},{7,3},{8,12},{9,13},{10,... | collective-permute-start | bytes 786440 | tf_op jit(solution)/shard_map/ppermute | solution.py:147
  41.7 12.2 %collective-permute-start.10 = (f32[512,128]{1,0:T(8,128)S(1)}, f32[512,128]{1,0:T(8,128)}, u32[]{:S(2)}, u32[]{:S(2)}) collective-permute-start(f32[512,128]{1,0:T(8,128)S(1)} %update.3.refs_3_.after), channel_id=1, source_target_pairs={{0,2},{1,3},{2,0},{3,1},{4,6},{5,7},{6,4},{7,5},{8,10},{9,11},{10,... | collective-permute-start | bytes 786440 | tf_op jit(solution)/shard_map/ppermute | solution.py:147
  42.4 21.1 %collective-permute-start.39 = (f32[768,128]{1,0:T(8,128)S(1)}, f32[768,128]{1,0:T(8,128)}, u32[]{:S(2)}, u32[]{:S(2)}) collective-permute-start(f32[768,128]{1,0:T(8,128)S(1)} %get-tuple-element.48.refs_0_), channel_id=1, source_target_pairs={{0,8},{1,9},{2,10},{3,11},{4,12},{5,13},{6,14},{7,15},{8,0},{9,1},... | collective-permute-start | bytes 1179656 | tf_op jit(solution)/shard_map/ppermute | solution.py:147
  49.0 5.5 %collective-permute-start.14 = (f32[512,128]{1,0:T(8,128)S(1)}, f32[512,128]{1,0:T(8,128)}, u32[]{:S(2)}, u32[]{:S(2)}) collective-permute-start(f32[512,128]{1,0:T(8,128)S(1)} %update.3.refs_3_.after), channel_id=1, source_target_pairs={{0,1},{1,0},{2,3},{3,2},{4,5},{5,4},{6,7},{7,6},{8,9},{9,8},{10,11... | collective-permute-start | bytes 786440 | tf_op jit(solution)/shard_map/ppermute | solution.py:147
  52.1 2.4 %collective-permute-start.11 = (f32[512,128]{1,0:T(8,128)}, f32[512,128]{1,0:T(8,128)}, u32[]{:S(2)}, u32[]{:S(2)}) collective-permute-start(f32[512,128]{1,0:T(8,128)} %get-tuple-element.39.refs_0_), channel_id=1, source_target_pairs={{0,1},{1,0},{2,3},{3,2},{4,5},{5,4},{6,7},{7,6},{8,9},{9,8},{10,11... | collective-permute-start | bytes 786440 | tf_op jit(solution)/shard_map/ppermute | solution.py:147
  53.9 1.9 %collective-permute-start.12 = (f32[512,128]{1,0:T(8,128)}, f32[512,128]{1,0:T(8,128)}, u32[]{:S(2)}, u32[]{:S(2)}) collective-permute-start(f32[512,128]{1,0:T(8,128)} %collective-permute-done.9.refs_1_), channel_id=1, source_target_pairs={{0,1},{1,0},{2,3},{3,2},{4,5},{5,4},{6,7},{7,6},{8,9},{9,8},{10,11... | collective-permute-start | bytes 786440 | tf_op jit(solution)/shard_map/ppermute | solution.py:147
  53.9 2.2 %collective-permute-start.13 = (f32[512,128]{1,0:T(8,128)}, f32[512,128]{1,0:T(8,128)}, u32[]{:S(2)}, u32[]{:S(2)}) collective-permute-start(f32[512,128]{1,0:T(8,128)} %collective-permute-done.10.refs_2_), channel_id=1, source_target_pairs={{0,1},{1,0},{2,3},{3,2},{4,5},{5,4},{6,7},{7,6},{8,9},{9,8},{10,11... | collective-permute-start | bytes 786440 | tf_op jit(solution)/shard_map/ppermute | solution.py:147
  60.0 7.3 %collective-permute-start.17 = (f32[256,128]{1,0:T(8,128)S(1)}, f32[256,128]{1,0:T(8,128)S(1)}, u32[]{:S(2)}, u32[]{:S(2)}) collective-permute-start(f32[256,128]{1,0:T(8,128)S(1)} %get-tuple-element.43.refs_3_.after.refs_20_), channel_id=1, source_target_pairs={{0,6},{1,7},{2,4},{3,5},{4,2},{5,3},{6,0},{7,1},{8,14},{9,15},{10,... | collective-permute-start | bytes 393224 | tf_op jit(solution)/shard_map/ppermute | solution.py:147
  61.8 7.5 %collective-permute-start.18 = (f32[256,128]{1,0:T(8,128)S(1)}, f32[256,128]{1,0:T(8,128)S(1)}, u32[]{:S(2)}, u32[]{:S(2)}) collective-permute-start(f32[256,128]{1,0:T(8,128)S(1)} %get-tuple-element.43.refs_3_.after.refs_20_), channel_id=1, source_target_pairs={{0,4},{1,5},{2,6},{3,7},{4,0},{5,1},{6,2},{7,3},{8,12},{9,13},{10,... | collective-permute-start | bytes 393224 | tf_op jit(solution)/shard_map/ppermute | solution.py:147
  62.8 6.7 %collective-permute-start.19 = (f32[256,128]{1,0:T(8,128)S(1)}, f32[256,128]{1,0:T(8,128)S(1)}, u32[]{:S(2)}, u32[]{:S(2)}) collective-permute-start(f32[256,128]{1,0:T(8,128)S(1)} %get-tuple-element.43.refs_3_.after.refs_20_), channel_id=1, source_target_pairs={{0,2},{1,3},{2,0},{3,1},{4,6},{5,7},{6,4},{7,5},{8,10},{9,11},{10,... | collective-permute-start | bytes 393224 | tf_op jit(solution)/shard_map/ppermute | solution.py:147
  64.6 24.6 %collective-permute-start.40 = (f32[1024,128]{1,0:T(8,128)S(1)}, f32[1024,128]{1,0:T(8,128)S(1)}, u32[]{:S(2)}, u32[]{:S(2)}) collective-permute-start(f32[1024,128]{1,0:T(8,128)S(1)} %get-tuple-element.49.refs_16_), channel_id=1, source_target_pairs={{0,1},{1,0},{2,3},{3,2},{4,5},{5,4},{6,7},{7,6},{8,9},{9,8},{10,11... | collective-permute-start | bytes 1572872 | tf_op jit(solution)/shard_map/ppermute | solution.py:147
  64.7 5.1 %collective-permute-start.23 = (f32[256,128]{1,0:T(8,128)S(1)}, f32[256,128]{1,0:T(8,128)S(1)}, u32[]{:S(2)}, u32[]{:S(2)}) collective-permute-start(f32[256,128]{1,0:T(8,128)S(1)} %get-tuple-element.43.refs_3_.after.refs_20_), channel_id=1, source_target_pairs={{0,1},{1,0},{2,3},{3,2},{4,5},{5,4},{6,7},{7,6},{8,9},{9,8},{10,11... | collective-permute-start | bytes 393224 | tf_op jit(solution)/shard_map/ppermute | solution.py:147
  68.9 3.5 %collective-permute-start.20 = (f32[256,128]{1,0:T(8,128)S(1)}, f32[256,128]{1,0:T(8,128)S(1)}, u32[]{:S(2)}, u32[]{:S(2)}) collective-permute-start(f32[256,128]{1,0:T(8,128)S(1)} %get-tuple-element.44.refs_0_), channel_id=1, source_target_pairs={{0,1},{1,0},{2,3},{3,2},{4,5},{5,4},{6,7},{7,6},{8,9},{9,8},{10,11... | collective-permute-start | bytes 393224 | tf_op jit(solution)/shard_map/ppermute | solution.py:147
  69.3 3.1 %collective-permute-start.21 = (f32[256,128]{1,0:T(8,128)S(1)}, f32[256,128]{1,0:T(8,128)S(1)}, u32[]{:S(2)}, u32[]{:S(2)}) collective-permute-start(f32[256,128]{1,0:T(8,128)S(1)} %collective-permute-done.18.refs_1_), channel_id=1, source_target_pairs={{0,1},{1,0},{2,3},{3,2},{4,5},{5,4},{6,7},{7,6},{8,9},{9,8},{10,11... | collective-permute-start | bytes 393224 | tf_op jit(solution)/shard_map/ppermute | solution.py:147
  69.5 2.9 %collective-permute-start.22 = (f32[256,128]{1,0:T(8,128)S(1)}, f32[256,128]{1,0:T(8,128)S(1)}, u32[]{:S(2)}, u32[]{:S(2)}) collective-permute-start(f32[256,128]{1,0:T(8,128)S(1)} %collective-permute-done.19.refs_2_), channel_id=1, source_target_pairs={{0,1},{1,0},{2,3},{3,2},{4,5},{5,4},{6,7},{7,6},{8,9},{9,8},{10,11... | collective-permute-start | bytes 393224 | tf_op jit(solution)/shard_map/ppermute | solution.py:147
  69.8 15.1 %collective-permute-start.72 = (f32[512,128]{1,0:T(8,128)S(1)}, f32[512,128]{1,0:T(8,128)S(1)}, u32[]{:S(2)}, u32[]{:S(2)}) collective-permute-start(f32[512,128]{1,0:T(8,128)S(1)} %get-tuple-element.56.refs_0_), channel_id=1, source_target_pairs={{0,16},{1,17},{2,18},{3,19},{4,20},{5,21},{6,22},{7,23},{8,24},{9,... | collective-permute-start | bytes 786440 | tf_op jit(solution)/shard_map/ppermute | solution.py:147
  73.3 12.2 %collective-permute-start.24 = (f32[256,128]{1,0:T(8,128)S(1)}, f32[256,128]{1,0:T(8,128)S(1)}, u32[]{:S(2)}, u32[]{:S(2)}) collective-permute-start(f32[256,128]{1,0:T(8,128)S(1)} %update.4.refs_7_), channel_id=1, source_target_pairs={{0,14},{1,15},{2,12},{3,13},{4,10},{5,11},{6,8},{7,9},{8,6},{9,7},... | collective-permute-start | bytes 393224 | tf_op jit(solution)/shard_map/ppermute | solution.py:147
  76.1 14.1 %collective-permute-start.25 = (f32[256,128]{1,0:T(8,128)S(1)}, f32[256,128]{1,0:T(8,128)S(1)}, u32[]{:S(2)}, u32[]{:S(2)}) collective-permute-start(f32[256,128]{1,0:T(8,128)S(1)} %update.4.refs_7_), channel_id=1, source_target_pairs={{0,12},{1,13},{2,14},{3,15},{4,8},{5,9},{6,10},{7,11},{8,4},{9,5},... | collective-permute-start | bytes 393224 | tf_op jit(solution)/shard_map/ppermute | solution.py:147
  77.0 14.6 %collective-permute-start.26 = (f32[256,128]{1,0:T(8,128)S(1)}, f32[256,128]{1,0:T(8,128)S(1)}, u32[]{:S(2)}, u32[]{:S(2)}) collective-permute-start(f32[256,128]{1,0:T(8,128)S(1)} %update.4.refs_7_), channel_id=1, source_target_pairs={{0,10},{1,11},{2,8},{3,9},{4,14},{5,15},{6,12},{7,13},{8,2},{9,3},... | collective-permute-start | bytes 393224 | tf_op jit(solution)/shard_map/ppermute | solution.py:147
  84.8 8.0 %collective-permute-start.27 = (f32[256,128]{1,0:T(8,128)S(1)}, f32[256,128]{1,0:T(8,128)S(1)}, u32[]{:S(2)}, u32[]{:S(2)}) collective-permute-start(f32[256,128]{1,0:T(8,128)S(1)} %update.4.refs_7_), channel_id=1, source_target_pairs={{0,8},{1,9},{2,10},{3,11},{4,12},{5,13},{6,14},{7,15},{8,0},{9,1},... | collective-permute-start | bytes 393224 | tf_op jit(solution)/shard_map/ppermute | solution.py:147
  85.5 8.1 %collective-permute-start.28 = (f32[256,128]{1,0:T(8,128)S(1)}, f32[256,128]{1,0:T(8,128)S(1)}, u32[]{:S(2)}, u32[]{:S(2)}) collective-permute-start(f32[256,128]{1,0:T(8,128)S(1)} %update.4.refs_7_), channel_id=1, source_target_pairs={{0,6},{1,7},{2,4},{3,5},{4,2},{5,3},{6,0},{7,1},{8,14},{9,15},{10,... | collective-permute-start | bytes 393224 | tf_op jit(solution)/shard_map/ppermute | solution.py:147
  89.2 6.8 %collective-permute-start.29 = (f32[256,128]{1,0:T(8,128)S(1)}, f32[256,128]{1,0:T(8,128)S(1)}, u32[]{:S(2)}, u32[]{:S(2)}) collective-permute-start(f32[256,128]{1,0:T(8,128)S(1)} %update.4.refs_7_), channel_id=1, source_target_pairs={{0,4},{1,5},{2,6},{3,7},{4,0},{5,1},{6,2},{7,3},{8,12},{9,13},{10,... | collective-permute-start | bytes 393224 | tf_op jit(solution)/shard_map/ppermute | solution.py:147
  90.2 6.1 %collective-permute-start.30 = (f32[256,128]{1,0:T(8,128)S(1)}, f32[256,128]{1,0:T(8,128)S(1)}, u32[]{:S(2)}, u32[]{:S(2)}) collective-permute-start(f32[256,128]{1,0:T(8,128)S(1)} %update.4.refs_7_), channel_id=1, source_target_pairs={{0,2},{1,3},{2,0},{3,1},{4,6},{5,7},{6,4},{7,5},{8,10},{9,11},{10,... | collective-permute-start | bytes 393224 | tf_op jit(solution)/shard_map/ppermute | solution.py:147
  91.6 4.9 %collective-permute-start.38 = (f32[256,128]{1,0:T(8,128)S(1)}, f32[256,128]{1,0:T(8,128)S(1)}, u32[]{:S(2)}, u32[]{:S(2)}) collective-permute-start(f32[256,128]{1,0:T(8,128)S(1)} %update.4.refs_7_), channel_id=1, source_target_pairs={{0,1},{1,0},{2,3},{3,2},{4,5},{5,4},{6,7},{7,6},{8,9},{9,8},{10,11... | collective-permute-start | bytes 393224 | tf_op jit(solution)/shard_map/ppermute | solution.py:147
  92.9 3.9 %collective-permute-start.31 = (f32[256,128]{1,0:T(8,128)S(1)}, f32[256,128]{1,0:T(8,128)S(1)}, u32[]{:S(2)}, u32[]{:S(2)}) collective-permute-start(f32[256,128]{1,0:T(8,128)S(1)} %get-tuple-element.47.refs_0_), channel_id=1, source_target_pairs={{0,1},{1,0},{2,3},{3,2},{4,5},{5,4},{6,7},{7,6},{8,9},{9,8},{10,11... | collective-permute-start | bytes 393224 | tf_op jit(solution)/shard_map/ppermute | solution.py:147
  93.6 3.5 %collective-permute-start.32 = (f32[256,128]{1,0:T(8,128)S(1)}, f32[256,128]{1,0:T(8,128)S(1)}, u32[]{:S(2)}, u32[]{:S(2)}) collective-permute-start(f32[256,128]{1,0:T(8,128)S(1)} %collective-permute-done.25.refs_1_), channel_id=1, source_target_pairs={{0,1},{1,0},{2,3},{3,2},{4,5},{5,4},{6,7},{7,6},{8,9},{9,8},{10,11... | collective-permute-start | bytes 393224 | tf_op jit(solution)/shard_map/ppermute | solution.py:147
  96.0 1.4 collective-permute-start.33
  96.3 1.4 collective-permute-start.34
  97.4 33.0 %collective-permute-start.73 = (f32[1024,128]{1,0:T(8,128)S(1)}, f32[1024,128]{1,0:T(8,128)S(1)}, u32[]{:S(2)}, u32[]{:S(2)}) collective-permute-start(f32[1024,128]{1,0:T(8,128)S(1)} %join.7.refs_16_), channel_id=1, source_target_pairs={{0,1},{1,0},{2,3},{3,2},{4,5},{5,4},{6,7},{7,6},{8,9},{9,8},{10,11... | collective-permute-start | bytes 1572872 | tf_op jit(solution)/shard_map/ppermute | solution.py:147
  100.0 7.3 %collective-permute-start.41 = (f32[128,128]{1,0:T(8,128)S(1)}, f32[128,128]{1,0:T(8,128)S(1)}, u32[]{:S(2)}, u32[]{:S(2)}) collective-permute-start(f32[128,128]{1,0:T(8,128)S(1)} %get-tuple-element.51.refs_7_.refs_21_), channel_id=1, source_target_pairs={{0,14},{1,15},{2,12},{3,13},{4,10},{5,11},{6,8},{7,9},{8,6},{9,7},... | collective-permute-start | bytes 196616 | tf_op jit(solution)/shard_map/ppermute | solution.py:147
  101.1 7.2 %collective-permute-start.42 = (f32[128,128]{1,0:T(8,128)S(1)}, f32[128,128]{1,0:T(8,128)S(1)}, u32[]{:S(2)}, u32[]{:S(2)}) collective-permute-start(f32[128,128]{1,0:T(8,128)S(1)} %get-tuple-element.51.refs_7_.refs_21_), channel_id=1, source_target_pairs={{0,12},{1,13},{2,14},{3,15},{4,8},{5,9},{6,10},{7,11},{8,4},{9,5},... | collective-permute-start | bytes 196616 | tf_op jit(solution)/shard_map/ppermute | solution.py:147
  103.4 6.0 %collective-permute-start.43 = (f32[128,128]{1,0:T(8,128)S(1)}, f32[128,128]{1,0:T(8,128)S(1)}, u32[]{:S(2)}, u32[]{:S(2)}) collective-permute-start(f32[128,128]{1,0:T(8,128)S(1)} %get-tuple-element.51.refs_7_.refs_21_), channel_id=1, source_target_pairs={{0,10},{1,11},{2,8},{3,9},{4,14},{5,15},{6,12},{7,13},{8,2},{9,3},... | collective-permute-start | bytes 196616 | tf_op jit(solution)/shard_map/ppermute | solution.py:147
  104.4 7.6 %collective-permute-start.44 = (f32[128,128]{1,0:T(8,128)S(1)}, f32[128,128]{1,0:T(8,128)S(1)}, u32[]{:S(2)}, u32[]{:S(2)}) collective-permute-start(f32[128,128]{1,0:T(8,128)S(1)} %get-tuple-element.51.refs_7_.refs_21_), channel_id=1, source_target_pairs={{0,8},{1,9},{2,10},{3,11},{4,12},{5,13},{6,14},{7,15},{8,0},{9,1},... | collective-permute-start | bytes 196616 | tf_op jit(solution)/shard_map/ppermute | solution.py:147
  107.3 5.2 %collective-permute-start.45 = (f32[128,128]{1,0:T(8,128)S(1)}, f32[128,128]{1,0:T(8,128)S(1)}, u32[]{:S(2)}, u32[]{:S(2)}) collective-permute-start(f32[128,128]{1,0:T(8,128)S(1)} %get-tuple-element.51.refs_7_.refs_21_), channel_id=1, source_target_pairs={{0,6},{1,7},{2,4},{3,5},{4,2},{5,3},{6,0},{7,1},{8,14},{9,15},{10,... | collective-permute-start | bytes 196616 | tf_op jit(solution)/shard_map/ppermute | solution.py:147
  108.4 4.8 %collective-permute-start.46 = (f32[128,128]{1,0:T(8,128)S(1)}, f32[128,128]{1,0:T(8,128)S(1)}, u32[]{:S(2)}, u32[]{:S(2)}) collective-permute-start(f32[128,128]{1,0:T(8,128)S(1)} %get-tuple-element.51.refs_7_.refs_21_), channel_id=1, source_target_pairs={{0,4},{1,5},{2,6},{3,7},{4,0},{5,1},{6,2},{7,3},{8,12},{9,13},{10,... | collective-permute-start | bytes 196616 | tf_op jit(solution)/shard_map/ppermute | solution.py:147
  109.4 4.3 %collective-permute-start.47 = (f32[128,128]{1,0:T(8,128)S(1)}, f32[128,128]{1,0:T(8,128)S(1)}, u32[]{:S(2)}, u32[]{:S(2)}) collective-permute-start(f32[128,128]{1,0:T(8,128)S(1)} %get-tuple-element.51.refs_7_.refs_21_), channel_id=1, source_target_pairs={{0,2},{1,3},{2,0},{3,1},{4,6},{5,7},{6,4},{7,5},{8,10},{9,11},{10,... | collective-permute-start | bytes 196616 | tf_op jit(solution)/shard_map/ppermute | solution.py:147
  112.1 1.6 %collective-permute-start.55 = (f32[128,128]{1,0:T(8,128)S(1)}, f32[128,128]{1,0:T(8,128)S(1)}, u32[]{:S(2)}, u32[]{:S(2)}) collective-permute-start(f32[128,128]{1,0:T(8,128)S(1)} %get-tuple-element.51.refs_7_.refs_21_), channel_id=1, source_target_pairs={{0,1},{1,0},{2,3},{3,2},{4,5},{5,4},{6,7},{7,6},{8,9},{9,8},{10,11... | collective-permute-start | bytes 196616 | tf_op jit(solution)/shard_map/ppermute | solution.py:147
  112.5 1.7 %collective-permute-start.48 = (f32[128,128]{1,0:T(8,128)S(1)}, f32[128,128]{1,0:T(8,128)S(1)}, u32[]{:S(2)}, u32[]{:S(2)}) collective-permute-start(f32[128,128]{1,0:T(8,128)S(1)} %get-tuple-element.52.refs_0_), channel_id=1, source_target_pairs={{0,1},{1,0},{2,3},{3,2},{4,5},{5,4},{6,7},{7,6},{8,9},{9,8},{10,11... | collective-permute-start | bytes 196616 | tf_op jit(solution)/shard_map/ppermute | solution.py:147
  113.7 1.4 collective-permute-start.51
  117.9 6.6 %collective-permute-start.56 = (f32[128,128]{1,0:T(8,128)S(1)}, f32[128,128]{1,0:T(8,128)S(1)}, u32[]{:S(2)}, u32[]{:S(2)}) collective-permute-start(f32[128,128]{1,0:T(8,128)S(1)} %update.5.own), channel_id=1, source_target_pairs={{0,16},{1,17},{2,18},{3,19},{4,20},{5,21},{6,22},{7,23},{8,24},{9,... | collective-permute-start | bytes 196616 | tf_op jit(solution)/shard_map/ppermute | solution.py:147
  124.6 8.2 %collective-permute-start.57 = (f32[256,128]{1,0:T(8,128)S(1)}, f32[256,128]{1,0:T(8,128)S(1)}, u32[]{:S(2)}, u32[]{:S(2)}) collective-permute-start(f32[256,128]{1,0:T(8,128)S(1)} %constant_dynamic-update-slice_fusion.refs_7_), channel_id=1, source_target_pairs={{0,14},{1,15},{2,12},{3,13},{4,10},{5,11},{6,8},{7,9},{8,6},{9,7},... | collective-permute-start | bytes 393224 | tf_op jit(solution)/shard_map/ppermute | solution.py:147
  125.8 10.0 %collective-permute-start.58 = (f32[256,128]{1,0:T(8,128)S(1)}, f32[256,128]{1,0:T(8,128)S(1)}, u32[]{:S(2)}, u32[]{:S(2)}) collective-permute-start(f32[256,128]{1,0:T(8,128)S(1)} %constant_dynamic-update-slice_fusion.refs_7_), channel_id=1, source_target_pairs={{0,12},{1,13},{2,14},{3,15},{4,8},{5,9},{6,10},{7,11},{8,4},{9,5},... | collective-permute-start | bytes 393224 | tf_op jit(solution)/shard_map/ppermute | solution.py:147
  128.2 9.5 %collective-permute-start.59 = (f32[256,128]{1,0:T(8,128)S(1)}, f32[256,128]{1,0:T(8,128)S(1)}, u32[]{:S(2)}, u32[]{:S(2)}) collective-permute-start(f32[256,128]{1,0:T(8,128)S(1)} %constant_dynamic-update-slice_fusion.refs_7_), channel_id=1, source_target_pairs={{0,10},{1,11},{2,8},{3,9},{4,14},{5,15},{6,12},{7,13},{8,2},{9,3},... | collective-permute-start | bytes 393224 | tf_op jit(solution)/shard_map/ppermute | solution.py:147
  128.9 10.3 %collective-permute-start.60 = (f32[256,128]{1,0:T(8,128)S(1)}, f32[256,128]{1,0:T(8,128)S(1)}, u32[]{:S(2)}, u32[]{:S(2)}) collective-permute-start(f32[256,128]{1,0:T(8,128)S(1)} %constant_dynamic-update-slice_fusion.refs_7_), channel_id=1, source_target_pairs={{0,8},{1,9},{2,10},{3,11},{4,12},{5,13},{6,14},{7,15},{8,0},{9,1},... | collective-permute-start | bytes 393224 | tf_op jit(solution)/shard_map/ppermute | solution.py:147
  130.4 8.8 %collective-permute-start.61 = (f32[256,128]{1,0:T(8,128)S(1)}, f32[256,128]{1,0:T(8,128)S(1)}, u32[]{:S(2)}, u32[]{:S(2)}) collective-permute-start(f32[256,128]{1,0:T(8,128)S(1)} %constant_dynamic-update-slice_fusion.refs_7_), channel_id=1, source_target_pairs={{0,6},{1,7},{2,4},{3,5},{4,2},{5,3},{6,0},{7,1},{8,14},{9,15},{10,... | collective-permute-start | bytes 393224 | tf_op jit(solution)/shard_map/ppermute | solution.py:147
  132.7 6.9 %collective-permute-start.62 = (f32[256,128]{1,0:T(8,128)S(1)}, f32[256,128]{1,0:T(8,128)S(1)}, u32[]{:S(2)}, u32[]{:S(2)}) collective-permute-start(f32[256,128]{1,0:T(8,128)S(1)} %constant_dynamic-update-slice_fusion.refs_7_), channel_id=1, source_target_pairs={{0,4},{1,5},{2,6},{3,7},{4,0},{5,1},{6,2},{7,3},{8,12},{9,13},{10,... | collective-permute-start | bytes 393224 | tf_op jit(solution)/shard_map/ppermute | solution.py:147
  135.8 5.0 %collective-permute-start.63 = (f32[256,128]{1,0:T(8,128)S(1)}, f32[256,128]{1,0:T(8,128)S(1)}, u32[]{:S(2)}, u32[]{:S(2)}) collective-permute-start(f32[256,128]{1,0:T(8,128)S(1)} %constant_dynamic-update-slice_fusion.refs_7_), channel_id=1, source_target_pairs={{0,2},{1,3},{2,0},{3,1},{4,6},{5,7},{6,4},{7,5},{8,10},{9,11},{10,... | collective-permute-start | bytes 393224 | tf_op jit(solution)/shard_map/ppermute | solution.py:147
  137.7 3.0 %collective-permute-start.71 = (f32[256,128]{1,0:T(8,128)S(1)}, f32[256,128]{1,0:T(8,128)S(1)}, u32[]{:S(2)}, u32[]{:S(2)}) collective-permute-start(f32[256,128]{1,0:T(8,128)S(1)} %constant_dynamic-update-slice_fusion.refs_7_), channel_id=1, source_target_pairs={{0,1},{1,0},{2,3},{3,2},{4,5},{5,4},{6,7},{7,6},{8,9},{9,8},{10,11... | collective-permute-start | bytes 393224 | tf_op jit(solution)/shard_map/ppermute | solution.py:147
  139.2 2.1 %collective-permute-start.64 = (f32[256,128]{1,0:T(8,128)S(1)}, f32[256,128]{1,0:T(8,128)S(1)}, u32[]{:S(2)}, u32[]{:S(2)}) collective-permute-start(f32[256,128]{1,0:T(8,128)S(1)} %collective-permute-done.57.refs_0_), channel_id=1, source_target_pairs={{0,1},{1,0},{2,3},{3,2},{4,5},{5,4},{6,7},{7,6},{8,9},{9,8},{10,11... | collective-permute-start | bytes 393224 | tf_op jit(solution)/shard_map/ppermute | solution.py:147
  139.2 2.2 %collective-permute-start.65 = (f32[256,128]{1,0:T(8,128)S(1)}, f32[256,128]{1,0:T(8,128)S(1)}, u32[]{:S(2)}, u32[]{:S(2)}) collective-permute-start(f32[256,128]{1,0:T(8,128)S(1)} %collective-permute-done.58.refs_1_), channel_id=1, source_target_pairs={{0,1},{1,0},{2,3},{3,2},{4,5},{5,4},{6,7},{7,6},{8,9},{9,8},{10,11... | collective-permute-start | bytes 393224 | tf_op jit(solution)/shard_map/ppermute | solution.py:147
  139.7 2.1 %collective-permute-start.66 = (f32[256,128]{1,0:T(8,128)S(1)}, f32[256,128]{1,0:T(8,128)S(1)}, u32[]{:S(2)}, u32[]{:S(2)}) collective-permute-start(f32[256,128]{1,0:T(8,128)S(1)} %collective-permute-done.59.refs_2_), channel_id=1, source_target_pairs={{0,1},{1,0},{2,3},{3,2},{4,5},{5,4},{6,7},{7,6},{8,9},{9,8},{10,11... | collective-permute-start | bytes 393224 | tf_op jit(solution)/shard_map/ppermute | solution.py:147
  140.8 1.5 %collective-permute-start.68 = (f32[256,128]{1,0:T(8,128)S(1)}, f32[256,128]{1,0:T(8,128)S(1)}, u32[]{:S(2)}, u32[]{:S(2)}) collective-permute-start(f32[256,128]{1,0:T(8,128)S(1)} %collective-permute-done.61.refs_4_), channel_id=1, source_target_pairs={{0,1},{1,0},{2,3},{3,2},{4,5},{5,4},{6,7},{7,6},{8,9},{9,8},{10,11... | collective-permute-start | bytes 393224 | tf_op jit(solution)/shard_map/ppermute | solution.py:147
  141.3 1.5 %collective-permute-start.70 = (f32[256,128]{1,0:T(8,128)S(1)}, f32[256,128]{1,0:T(8,128)S(1)}, u32[]{:S(2)}, u32[]{:S(2)}) collective-permute-start(f32[256,128]{1,0:T(8,128)S(1)} %collective-permute-done.63.refs_6_), channel_id=1, source_target_pairs={{0,1},{1,0},{2,3},{3,2},{4,5},{5,4},{6,7},{7,6},{8,9},{9,8},{10,11... | collective-permute-start | bytes 393224 | tf_op jit(solution)/shard_map/ppermute | solution.py:147
  (17 other events, 50.8 us)

commit v3 on v2

--- a/solution.py
+++ b/solution.py
@@ -147,23 +147,21 @@
     return lax.ppermute(x, AXES, [(source, source ^ mask) for source in range(size)])
 
 
-def spread(x, group, through=lambda x: x):
+def spread(x, group, *throughs):
     masks = [0]
     apart = group // 2
     while apart >= 16:
-        far = exchange(x, apart)
-        x = through(x)
-        x = jnp.concatenate([x, far], 0)
+        x = jnp.concatenate([x, exchange(x, apart)], 0)
         masks = masks + [mask ^ apart for mask in masks]
         apart //= 2
-        through = lambda value: value
     low = 2 * apart
     arrays = [(mask, exchange(x, mask)) for mask in range(low - 2, 0, -2)]
     if low > 4:
-        arrays[0] = (low - 2, through(arrays[0][1]))
+        for n, through in enumerate(throughs):
+            arrays[n] = (arrays[n][0], through(arrays[n][1]))
         arrays.append((0, x))
     else:
-        arrays.append((0, through(x)))
+        arrays.append((0, throughs[0](x)))
     arrays += [(mask ^ 1, exchange(array, 1)) for mask, array in arrays]
     return [(array, [mask ^ high for high in masks]) for mask, array in arrays]
 
@@ -214,7 +212,8 @@
     pieces, refs = refs[:count], refs[count:]
     own_h, refs = refs[: shape["h_count"]], refs[shape["h_count"] :]
     factor, refs = refs[0], refs[1:]
-    earlier, rest = refs[: shape["earlier"]], refs[shape["earlier"] :]
+    earlier, refs = refs[: shape["earlier"]], refs[shape["earlier"] :]
+    rides, rest = refs[: shape["rides"]], refs[shape["rides"] + shape["ahead"] :]
     front = shape["front"]
     p_size, child_rows, span = shape["p_size"], shape["child_rows"], shape["child_span"]
     upd_rows = shape["upd_rows"]
@@ -234,9 +233,10 @@
         frontal[p_size // B :, :, :] = jnp.zeros_like(frontal[p_size // B :, :, :])
     if shape["earlier"]:
         done = 0
-        for array in earlier:
-            rest[0][done : done + array.shape[0], :] = array[...]
-            done += array.shape[0]
+        for n, array in enumerate(earlier):
+            rows = p_size // (front * 2**n)
+            rest[0][done : done + rows, :] = array[:rows, :]
+            done += rows
     step = min(child_rows, B)
     for piece, piece_masks in zip(pieces, masks, strict=True):
         for part, mask in enumerate(piece_masks):
@@ -258,7 +258,10 @@
                     frontal[target, pl.ds(inner, step), :] += piece[here : here + step, :]
     right[...] = wide(frontal[: p_size // B].reshape(p_size, -1))
     z = product(factor[...], right[...])
-    if shape["earlier"]:
+    if shape["rides"]:
+        rest[0][: z.shape[0], :] = z
+        rest[0][z.shape[0] :, :] = rides[0][...]
+    elif shape["earlier"]:
         rest[0][done : done + z.shape[0], :] = z
     else:
         rest[0][...] = z
@@ -273,7 +276,7 @@
             rest[1][...] = frontal[p_size // B + row // B, pl.ds(inner, upd_rows), :]
 
 
-def solve_pivots(me, maps, pieces, h, factor, earlier, **shape):
+def solve_pivots(me, maps, pieces, h, factor, earlier, rides, ahead, **shape):
     rows = factor.shape[0] // 2
     columns = pieces[0][0].shape[1]
     p_size = factor.shape[1]
@@ -281,19 +284,22 @@
     shape |= {
         "p_size": p_size,
         "earlier": len(earlier),
+        "rides": len(rides),
+        "ahead": len(ahead),
         "h_count": len(h[0]),
         "h_parts": h[1],
     }
-    total = rows + sum(array.shape[0] for array in earlier)
+    total = sum(p_size // (shape["front"] * 2**n) for n in range(len(earlier)))
+    total += rows + sum(array.shape[0] for array in rides)
     outs = [jax.ShapeDtypeStruct((total, columns), F32)]
     if upd_rows:
         outs.append(jax.ShapeDtypeStruct((upd_rows, columns), F32))
     frontal_rows = p_size + upd_rows * shape["group"]
-    operands = [array for array, _ in pieces] + h[0] + [factor, *earlier]
+    operands = [array for array, _ in pieces] + h[0] + [factor, *earlier, *rides, *ahead]
     return pl.pallas_call(
         functools.partial(pivot_kernel, [masks for _, masks in pieces], shape),
         out_shape=tuple(outs),
-        in_specs=[SMEM, SMEM] + [VMEM] * len(operands),
+        in_specs=[SMEM, SMEM] + [VMEM] * (len(operands) - len(ahead)) + [ANY] * len(ahead),
         out_specs=tuple(VMEM for _ in outs),
         scratch_shapes=[
             pltpu.VMEM((frontal_rows // B, B, columns), F32),
@@ -312,12 +318,13 @@
     pieces = refs[:count]
     side, factor, w, right = refs[count:]
     rank = jnp.bitwise_and(me[0], group - 1)
+    used = right.shape[0] // group
     for piece, piece_masks in zip(pieces, masks, strict=True):
         rows = piece.shape[0] // len(piece_masks)
         for part, mask in enumerate(piece_masks):
             source = jnp.bitwise_xor(rank, mask)
-            where = pl.ds(pl.multiple_of(source * rows, 16), rows)
-            right[where, :] = wide(piece[part * rows : (part + 1) * rows, :])
+            where = pl.ds(pl.multiple_of(source * used, 16), used)
+            right[where, :] = wide(piece[part * rows : part * rows + used, :])
     w[...] = side[...] - product(factor[...], right[...])
 
 
@@ -366,30 +373,38 @@
 class Rhs:
     def __init__(self, front_rhs, p_size, groups):
         self.rows = [p_size // group for group in groups]
-        self.total = front_rhs.shape[0]
         self.masks = [0, 2]
         self.held = [front_rhs, exchange(front_rhs, 2)]
-        self.level = 0
+        self.spans = [front_rhs.shape[0]] * 2
+        self.first = 0
+        self.done = []
+        root = front_rhs[front_rhs.shape[0] - self.rows[-1] :]
+        self.root = [root, exchange(root, groups[-1] // 2)]
+
+    def pair_root(self, after):
+        plan = [(n, 0, self.rows[-1]) for n in range(2)]
+        (self.root_pair,) = join_rows(after, self.root, [plan])
 
     def next_level(self, after):
-        rows, group = self.rows[self.level], 2 * len(self.masks)
-        span = sum(self.rows[self.level :])
+        level = len(self.done)
+        rows, group = self.rows[level], 2 * len(self.masks)
+        rest = sum(self.rows[level + 1 : -1])
         parts = [
-            (n, at * span) for n, array in enumerate(self.held) for at in range(array.shape[0] // span)
+            (n, at + self.first)
+            for n, (array, span) in enumerate(zip(self.held, self.spans, strict=True))
+            for at in range(0, array.shape[0], span)
         ]
         plans = [[(n, at, at + rows) for n, at in parts]]
-        last = self.level + 1 == len(self.rows)
-        if not last:
-            plans.append([(n, at + rows, at + span) for n, at in parts])
-        mine, *rest = join_rows(after, self.held, plans)
-        other = exchange(mine, 1)
+        if rest:
+            plans.append([(n, at + rows, at + rows + rest) for n, at in parts])
+        out = join_rows(after, self.held, plans)
         place = [(0, at * rows, mask) for at, mask in enumerate(self.masks)]
         place += [(1, at * rows, mask ^ 1) for at, mask in enumerate(self.masks)]
-        if not last:
-            self.held = [rest[0], exchange(rest[0], group)]
+        self.done.append(([out[0], exchange(out[0], 1)], place))
+        if rest:
+            self.held = [out[1], exchange(out[1], group)]
+            self.spans = [rest, rest]
             self.masks = self.masks + [mask ^ group for mask in self.masks]
-        self.level += 1
-        return [mine, other], place
 
 
 def per_device(
@@ -418,19 +433,18 @@
     rhs = Rhs(front_rhs, p_size, groups)
 
     flat, update = solve_subtree(sub_rhs, sub_dinv, sub_off, sub_pattern.T, sub_update)
-    kept = []
-
-    def keep(factor, block):
+    kept = {}
+
+    def keep(name, factor, block):
         def through(x):
             factor_rows, x = prepare_factor(factor, block, x)
-            kept[:] = [factor_rows]
+            kept[name] = factor_rows
             return x
 
         return through
 
-    pieces = spread(update, front_size, keep(piv_inverse, (0, sizes[0])))
-    factor = kept[0]
-    h = [rhs.next_level(update)]
+    pieces = spread(update, front_size, keep("pivots", piv_inverse, (0, sizes[0])))
+    rhs.next_level(update)
     maps, map_offset, child_span = sub_map.T, 0, 0
     earlier = []
     for level in range(1, level_count + 1):
@@ -440,9 +454,11 @@
             me,
             maps,
             pieces,
-            h[level - 1],
-            factor,
+            rhs.done[level - 1],
+            kept["pivots"],
             earlier if last else [],
+            [rhs.root_pair] if level == level_count - 1 else [],
+            [rhs.root_pair] if level == 2 else [],
             front=front_size,
             child_rows=update.shape[0],
             child_span=child_span,
@@ -454,14 +470,28 @@
             return flat, out[0]
         z, side = out
         earlier.append(z)
-        if len(h) < level_count:
-            h.append(rhs.next_level(z))
-        z_pieces = spread(z, group, keep(upd_factor, (2**level - 2, u_size // group)))
-        update = solve_update(me, z_pieces, side, kept[0], group)
-        pieces = spread(update, 2 * group, keep(piv_inverse, (2 ** (level + 1) - 2, sizes[level])))
-        factor = kept[0]
-        if len(h) < level_count:
-            h.append(rhs.next_level(update))
+        if level > 1 and len(rhs.done) < level_count - 1:
+            rhs.next_level(z)
+        throughs = [keep("update", upd_factor, (2**level - 2, u_size // group))]
+        following = [keep("pivots", piv_inverse, (2 ** (level + 1) - 2, sizes[level]))]
+        if level == level_count - 1:
+            throughs, following = throughs + following, []
+        z_pieces = spread(z, group, *throughs)
+        update = solve_update(me, z_pieces, side, kept["update"], group)
+        pieces = spread(update, 2 * group, *following)
+        if level == 1:
+            rhs.pair_root(update)
+        if level == 1:
+            rhs.next_level(update)
+        if level == level_count - 1:
+            parts = []
+            for n, (array, masks) in enumerate(z_pieces):
+                rows = array.shape[0] // len(masks)
+                for at, mask in enumerate(masks):
+                    row = at * rows + sizes[level - 1]
+                    parts.append((n, row, mask))
+                    parts.append((n, row + sizes[level], mask ^ group))
+            rhs.done.append(([array for array, _ in z_pieces], parts))
         map_offset = 0 if level == 1 else map_offset + leaf_size // child_span
         child_span = 2 ** (level - 1)
         maps = front_map.T

time: 146 us -> 143 us (0.979)
  waiting for transfers between devices: 46.5 us -> 44.2 us
    ppermute x74 -> x73, waiting for transfers between devices: 46.5 us -> 44.2 us  [exchange(): lax.ppermute(x, AXES, [(source, source ^ mask) for source in range(size)])]
    ppermute x74 -> x73, starting transfers between devices: 57.9 us -> 57.3 us  [exchange(): lax.ppermute(x, AXES, [(source, source ^ mask) for source in range(size)])]
    unnamed x16 -> x15, local copies, waits for them, and re-layouts: 6.14 us -> 5.95 us
  transfers between devices with their start and end apart: 74 -> 73, of which waited for: 37 -> 40; matrix products, arithmetic and copies ran while one was open for 0% -> 0% of each run, Pallas kernels for 22% -> 19%
where the time goes in v3:
time: 143 us
  starting transfers between devices  57.3 us (40%)
  waiting for transfers between devices  44.2 us (31%)
  Pallas kernels  34.5 us (24%)
  local copies, waits for them, and re-layouts  5.95 us (4%)
    ppermute x73, starting transfers between devices, exchange(): lax.ppermute(x, AXES, [(source, source ^ mask) for source in range(size)])  57.3 us
    ppermute x73, waiting for transfers between devices, exchange(): lax.ppermute(x, AXES, [(source, source ^ mask) for source in range(size)])  44.2 us
    pallas_call x7, Pallas kernels, prepare_factor(): pl.pallas_call(functools.partial(factor_kernel, block), out_shape=(jax.Sh...  12.3 us
    pallas_call x4, Pallas kernels, solve_pivots(): pl.pallas_call(functools.partial(pivot_kernel, [masks for _, masks in pie...  8.85 us
    pallas_call x1, Pallas kernels, solve_subtree(): pl.pallas_call(functools.partial(subtree_kernel, bounds), out_shape=(jax....  8.48 us
    unnamed x15, local copies, waits for them, and re-layouts  5.95 us
    pallas_call x3, Pallas kernels, solve_update(): pl.pallas_call(functools.partial(update_kernel, [masks for _, masks in pi...  2.98 us
  transfers between devices with their start and end apart: 73, of which 40 were waited for; matrix products, arithmetic and copies ran while one was open for 0% of the time, Pallas kernels for 19%

profile of v3, /device:TPU:0, one launch (start us, length us, event | category | flops | bytes accessed | tf_op | source)
XLA Modules:
  0.0 142.8 jit_solution(7019806813025495464)
XLA Ops:
  0.6 3.0 %collective-permute-start.3 = (f32[960,128]{1,0:T(8,128)}, f32[960,128]{1,0:T(8,128)S(1)}, u32[]{:S(2)}, u32[]{:S(2)}) collective-permute-start(f32[960,128]{1,0:T(8,128)} %refs_0_.1), channel_id=1, source_target_pairs={{0,2},{1,3},{2,0},{3,1},{4,6},{5,7},{6,4},{7,5},{8,10},{9,11},{10,... | collective-permute-start | bytes 1474568 | tf_op jit(solution)/shard_map/ppermute | solution.py:147
  3.6 8.5 %subtree.1 = (f32[3072,128]{1,0:T(8,128)}, f32[256,128]{1,0:T(8,128)S(1)}) custom-call(s32[2,23]{1,0:T(2,128)} %bitcast.8, f32[3072,128]{1,0:T(8,128)} %rhs_in.1, f32[24,128,128]{2,1,0:T(8,128)} %dinv_in.1, f32[23,2,128,128]{3,2,1,0:T(8,128)} %off_in.1, f32[256,3072]{1,0:T(8,128)} %upd_in.1), custom_call_target="tpu_custom_call" | custom-call | flops 1000000 | bytes 100000 | tf_op jit(solution)/shard_map/subtree/pallas_call | solution.py:118
  12.1 2.9 %collective-permute-done.3.refs_1_ = f32[960,128]{1,0:T(8,128)S(1)} collective-permute-done((f32[960,128]{1,0:T(8,128)}, f32[960,128]{1,0:T(8,128)S(1)}, u32[]{:S(2)}, u32[]{:S(2)}) %collective-permute-start.3) | collective-permute-done | bytes 491552 | tf_op jit(solution)/shard_map/ppermute | solution.py:147
  15.2 1.8 %collective-permute-start = (f32[256,128]{1,0:T(8,128)S(1)}, f32[256,128]{1,0:T(8,128)S(1)}, u32[]{:S(2)}, u32[]{:S(2)}) collective-permute-start(f32[256,128]{1,0:T(8,128)S(1)} %get-tuple-element.29.own.after), channel_id=1, source_target_pairs={{0,2},{1,3},{2,0},{3,1},{4,6},{5,7},{6,4},{7,5},{8,10},{9,11},{10,... | collective-permute-start | bytes 393224 | tf_op jit(solution)/shard_map/ppermute | solution.py:147
  17.0 2.3 %factor.14 = (bf16[1024,2048]{1,0:T(8,128)(2,1)S(1)}, f32[256,128]{1,0:T(8,128)S(1)}) custom-call(f32[960,2048]{1,0:T(8,128)} %factor.27, f32[256,128]{1,0:T(8,128)S(1)} %get-tuple-element.29.own.after), custom_call_target="tpu_custom_call" | custom-call | bytes 8388608 | tf_op jit(solution)/shard_map/factor/pallas_call | solution.py:190
  19.4 2.0 %copy-done = bf16[1024,2048]{1,0:T(8,128)(2,1)} copy-done((bf16[1024,2048]{1,0:T(8,128)(2,1)}, bf16[1024,2048]{1,0:T(8,128)(2,1)S(1)}, u32[]{:S(2)}) %copy-start) | copy-done | bytes 4194328
  23.0 2.2 %copy-done.1 = bf16[1024,2048]{1,0:T(8,128)(2,1)S(1)} copy-done((bf16[1024,2048]{1,0:T(8,128)(2,1)S(1)}, bf16[1024,2048]{1,0:T(8,128)(2,1)}, u32[]{:S(2)}) %copy-start.1) | copy-done | bytes 4194328
  25.1 2.0 %pivots.4 = (f32[512,128]{1,0:T(8,128)S(1)}, f32[512,128]{1,0:T(8,128)S(1)}) custom-call(s32[1]{0:T(128)} %bitcast.1.me, s32[2,32]{1,0:T(2,128)S(1)} %bitcast.7, f32[256,128]{1,0:T(8,128)S(1)} %collective-permute-done.refs_0_, f32[256,128]{1,0:T(8,128)S(1)} %get-tuple-element.30.refs_1_, f32[256,128]{1,0:T(8,128)S(1)} %collective-permute-done.1.refs_2_, ...), custom_call_target="tpu_custom_call" | custom-call | flops 805306368 | bytes 8000000 | tf_op jit(solution)/shard_map/pivots/pallas_call | solution.py:299
  27.2 1.3 collective-permute-start.5
  28.5 1.5 %collective-permute-start.15 = (f32[768,128]{1,0:T(8,128)S(1)}, f32[768,128]{1,0:T(8,128)S(1)}, u32[]{:S(2)}, u32[]{:S(2)}) collective-permute-start(f32[768,128]{1,0:T(8,128)S(1)} %get-tuple-element.38.refs_0_), channel_id=1, source_target_pairs={{0,4},{1,5},{2,6},{3,7},{4,0},{5,1},{6,2},{7,3},{8,12},{9,13},{10,... | collective-permute-start | bytes 1179656 | tf_op jit(solution)/shard_map/ppermute | solution.py:147
  30.0 2.3 %factor.16 = (bf16[1024,2048]{1,0:T(8,128)(2,1)S(1)}, f32[512,128]{1,0:T(8,128)S(1)}) custom-call(f32[896,2048]{1,0:T(8,128)} %factor.25, f32[512,128]{1,0:T(8,128)S(1)} %get-tuple-element.33.own.refs_33_), custom_call_target="tpu_custom_call" | custom-call | bytes 8388608 | tf_op jit(solution)/shard_map/factor/pallas_call | solution.py:190
  32.5 3.3 %collective-permute-done.5.refs_0_ = f32[512,128]{1,0:T(8,128)S(1)} collective-permute-done((f32[512,128]{1,0:T(8,128)S(1)}, f32[512,128]{1,0:T(8,128)S(1)}, u32[]{:S(2)}, u32[]{:S(2)}) %collective-permute-start.5) | collective-permute-done | bytes 262176 | tf_op jit(solution)/shard_map/ppermute | solution.py:147
  35.8 1.5 %collective-permute-done.6.refs_2_ = f32[512,128]{1,0:T(8,128)S(1)} collective-permute-done((f32[512,128]{1,0:T(8,128)S(1)}, f32[512,128]{1,0:T(8,128)S(1)}, u32[]{:S(2)}, u32[]{:S(2)}) %collective-permute-start.6) | collective-permute-done | bytes 262176 | tf_op jit(solution)/shard_map/ppermute | solution.py:147
  37.3 1.5 %update.3.after.refs_3_ = f32[512,128]{1,0:T(8,128)S(1)} custom-call(s32[1]{0:T(128)} %bitcast.1.me, f32[512,128]{1,0:T(8,128)S(1)} %collective-permute-done.5.refs_0_, f32[512,128]{1,0:T(8,128)S(1)} %get-tuple-element.34.refs_1_, f32[512,128]{1,0:T(8,128)S(1)} %collective-permute-done.6.refs_2_, f32[512,128]{1,0:T(8,128)S(1)} %collective-permute-done.7.refs_3_, ...), custom_call_target="tpu_custom_call" | custom-call | flops 805306368 | bytes 8000000 | tf_op jit(solution)/shard_map/update/pallas_call | solution.py:334
  38.8 2.1 %collective-permute-start.8 = (f32[512,128]{1,0:T(8,128)S(1)}, f32[512,128]{1,0:T(8,128)S(1)}, u32[]{:S(2)}, u32[]{:S(2)}) collective-permute-start(f32[512,128]{1,0:T(8,128)S(1)} %update.3.after.refs_3_), channel_id=1, source_target_pairs={{0,6},{1,7},{2,4},{3,5},{4,2},{5,3},{6,0},{7,1},{8,14},{9,15},{10,... | collective-permute-start | bytes 786440 | tf_op jit(solution)/shard_map/ppermute | solution.py:147
  41.4 0.9 collective-permute-start.10
  43.7 5.3 %collective-permute-done.8.own = f32[512,128]{1,0:T(8,128)S(1)} collective-permute-done((f32[512,128]{1,0:T(8,128)S(1)}, f32[512,128]{1,0:T(8,128)S(1)}, u32[]{:S(2)}, u32[]{:S(2)}) %collective-permute-start.8) | collective-permute-done | bytes 262176 | tf_op jit(solution)/shard_map/ppermute | solution.py:147
  49.0 2.6 %collective-permute-start.17 = (f32[64,128]{1,0:T(8,128)S(1)}, f32[64,128]{1,0:T(8,128)S(1)}, u32[]{:S(2)}, u32[]{:S(2)}) collective-permute-start(f32[64,128]{1,0:T(8,128)S(1)} %slice.3.refs_0_), channel_id=1, source_target_pairs={{0,16},{1,17},{2,18},{3,19},{4,20},{5,21},{6,22},{7,23},{8,24},{9,... | collective-permute-start | bytes 98312 | tf_op jit(solution)/shard_map/ppermute | solution.py:147
  51.6 2.3 %factor.18 = (bf16[512,2048]{1,0:T(8,128)(2,1)S(1)}, f32[512,128]{1,0:T(8,128)}) custom-call(f32[960,2048]{1,0:T(8,128)} %factor.27, f32[512,128]{1,0:T(8,128)S(1)} %collective-permute-done.8.own), custom_call_target="tpu_custom_call" | custom-call | bytes 4194304 | tf_op jit(solution)/shard_map/factor/pallas_call | solution.py:190
  55.2 1.6 %collective-permute-start.40 = (f32[512,128]{1,0:T(8,128)}, f32[512,128]{1,0:T(8,128)}, u32[]{:S(2)}, u32[]{:S(2)}) collective-permute-start(f32[512,128]{1,0:T(8,128)} %get-tuple-element.46.refs_0_), channel_id=1, source_target_pairs={{0,8},{1,9},{2,10},{3,11},{4,12},{5,13},{6,14},{7,15},{8,0},{9,1},... | collective-permute-start | bytes 786440 | tf_op jit(solution)/shard_map/ppermute | solution.py:147
  56.9 0.9 copy-done.4
  57.9 2.8 %pivots.5 = (f32[256,128]{1,0:T(8,128)S(1)}, f32[256,128]{1,0:T(8,128)S(1)}) custom-call(s32[1]{0:T(128)} %bitcast.1.me, s32[16,14]{1,0:T(8,128)S(1)} %bitcast.4, f32[512,128]{1,0:T(8,128)} %get-tuple-element.37.refs_0_, f32[512,128]{1,0:T(8,128)S(1)} %collective-permute-done.9.refs_1_, f32[512,128]{1,0:T(8,128)} %collective-permute-done.10.refs_2_, ...), custom_call_target="tpu_custom_call" | custom-call | flops 402653184 | bytes 8000000 | tf_op jit(solution)/shard_map/pivots/pallas_call | solution.py:299
  60.6 2.1 %collective-permute-start.18 = (f32[256,128]{1,0:T(8,128)S(1)}, f32[256,128]{1,0:T(8,128)S(1)}, u32[]{:S(2)}, u32[]{:S(2)}) collective-permute-start(f32[256,128]{1,0:T(8,128)S(1)} %get-tuple-element.41.refs_3_.after.refs_34_), channel_id=1, source_target_pairs={{0,6},{1,7},{2,4},{3,5},{4,2},{5,3},{6,0},{7,1},{8,14},{9,15},{10,... | collective-permute-start | bytes 393224 | tf_op jit(solution)/shard_map/ppermute | solution.py:147
  63.3 0.9 collective-permute-start.20
  64.2 3.7 %collective-permute-done.18.own = f32[256,128]{1,0:T(8,128)S(1)} collective-permute-done((f32[256,128]{1,0:T(8,128)S(1)}, f32[256,128]{1,0:T(8,128)S(1)}, u32[]{:S(2)}, u32[]{:S(2)}) %collective-permute-start.18) | collective-permute-done | bytes 131104 | tf_op jit(solution)/shard_map/ppermute | solution.py:147
  67.9 1.6 %factor.20 = (bf16[512,2048]{1,0:T(8,128)(2,1)S(1)}, f32[256,128]{1,0:T(8,128)S(1)}) custom-call(f32[896,2048]{1,0:T(8,128)} %factor.25, f32[256,128]{1,0:T(8,128)S(1)} %collective-permute-done.18.own), custom_call_target="tpu_custom_call" | custom-call | bytes 4194304 | tf_op jit(solution)/shard_map/factor/pallas_call | solution.py:190
  70.5 1.1 join.7.refs_16_
  71.8 0.9 update.4.refs_7_
  72.7 2.9 %collective-permute-start.25 = (f32[256,128]{1,0:T(8,128)S(1)}, f32[256,128]{1,0:T(8,128)S(1)}, u32[]{:S(2)}, u32[]{:S(2)}) collective-permute-start(f32[256,128]{1,0:T(8,128)S(1)} %update.4.refs_7_), channel_id=1, source_target_pairs={{0,14},{1,15},{2,12},{3,13},{4,10},{5,11},{6,8},{7,9},{8,6},{9,7},... | collective-permute-start | bytes 393224 | tf_op jit(solution)/shard_map/ppermute | solution.py:147
  76.3 1.5 %collective-permute-start.27 = (f32[256,128]{1,0:T(8,128)S(1)}, f32[256,128]{1,0:T(8,128)S(1)}, u32[]{:S(2)}, u32[]{:S(2)}) collective-permute-start(f32[256,128]{1,0:T(8,128)S(1)} %update.4.refs_7_), channel_id=1, source_target_pairs={{0,10},{1,11},{2,8},{3,9},{4,14},{5,15},{6,12},{7,13},{8,2},{9,3},... | collective-permute-start | bytes 393224 | tf_op jit(solution)/shard_map/ppermute | solution.py:147
  77.8 0.9 collective-permute-start.28
  78.6 2.6 %collective-permute-done.25.own = f32[256,128]{1,0:T(8,128)S(1)} collective-permute-done((f32[256,128]{1,0:T(8,128)S(1)}, f32[256,128]{1,0:T(8,128)S(1)}, u32[]{:S(2)}, u32[]{:S(2)}) %collective-permute-start.25) | collective-permute-done | bytes 131104 | tf_op jit(solution)/shard_map/ppermute | solution.py:147
  81.2 2.4 %collective-permute-start.29 = (f32[256,128]{1,0:T(8,128)S(1)}, f32[256,128]{1,0:T(8,128)S(1)}, u32[]{:S(2)}, u32[]{:S(2)}) collective-permute-start(f32[256,128]{1,0:T(8,128)S(1)} %update.4.refs_7_), channel_id=1, source_target_pairs={{0,6},{1,7},{2,4},{3,5},{4,2},{5,3},{6,0},{7,1},{8,14},{9,15},{10,... | collective-permute-start | bytes 393224 | tf_op jit(solution)/shard_map/ppermute | solution.py:147
  83.7 1.5 %collective-permute-start.30 = (f32[256,128]{1,0:T(8,128)S(1)}, f32[256,128]{1,0:T(8,128)S(1)}, u32[]{:S(2)}, u32[]{:S(2)}) collective-permute-start(f32[256,128]{1,0:T(8,128)S(1)} %update.4.refs_7_), channel_id=1, source_target_pairs={{0,4},{1,5},{2,6},{3,7},{4,0},{5,1},{6,2},{7,3},{8,12},{9,13},{10,... | collective-permute-start | bytes 393224 | tf_op jit(solution)/shard_map/ppermute | solution.py:147
  85.2 1.8 %collective-permute-done.27.refs_2_ = f32[256,128]{1,0:T(8,128)S(1)} collective-permute-done((f32[256,128]{1,0:T(8,128)S(1)}, f32[256,128]{1,0:T(8,128)S(1)}, u32[]{:S(2)}, u32[]{:S(2)}) %collective-permute-start.27) | collective-permute-done | bytes 131104 | tf_op jit(solution)/shard_map/ppermute | solution.py:147
  87.0 1.1 collective-permute-start.31
  88.6 1.3 factor.22
  90.5 1.5 %collective-permute-done.31.refs_6_ = f32[256,128]{1,0:T(8,128)S(1)} collective-permute-done((f32[256,128]{1,0:T(8,128)S(1)}, f32[256,128]{1,0:T(8,128)S(1)}, u32[]{:S(2)}, u32[]{:S(2)}) %collective-permute-start.31) | collective-permute-done | bytes 131104 | tf_op jit(solution)/shard_map/ppermute | solution.py:147
  94.4 1.6 %pivots.6 = (f32[256,128]{1,0:T(8,128)S(1)}, f32[128,128]{1,0:T(8,128)S(1)}) custom-call(s32[1]{0:T(128)} %bitcast.1.me, s32[16,14]{1,0:T(8,128)S(1)} %bitcast.5, f32[256,128]{1,0:T(8,128)S(1)} %get-tuple-element.45.refs_0_, f32[256,128]{1,0:T(8,128)S(1)} %collective-permute-done.26.refs_1_, f32[256,128]{1,0:T(8,128)S(1)} %collective-permute-done.27.refs_2_, ...), custom_call_target="tpu_custom_call" | custom-call | flops 201326592 | bytes 8000000 | tf_op jit(solution)/shard_map/pivots/pallas_call | solution.py:299
  96.0 1.7 %collective-permute-start.42 = (f32[256,128]{1,0:T(8,128)S(1)}, f32[256,128]{1,0:T(8,128)S(1)}, u32[]{:S(2)}, u32[]{:S(2)}) collective-permute-start(f32[256,128]{1,0:T(8,128)S(1)} %get-tuple-element.48.refs_7_.refs_23_.refs_35_), channel_id=1, source_target_pairs={{0,14},{1,15},{2,12},{3,13},{4,10},{5,11},{6,8},{7,9},{8,6},{9,7},... | collective-permute-start | bytes 393224 | tf_op jit(solution)/shard_map/ppermute | solution.py:147
  97.7 1.8 %collective-permute-start.43 = (f32[256,128]{1,0:T(8,128)S(1)}, f32[256,128]{1,0:T(8,128)S(1)}, u32[]{:S(2)}, u32[]{:S(2)}) collective-permute-start(f32[256,128]{1,0:T(8,128)S(1)} %get-tuple-element.48.refs_7_.refs_23_.refs_35_), channel_id=1, source_target_pairs={{0,12},{1,13},{2,14},{3,15},{4,8},{5,9},{6,10},{7,11},{8,4},{9,5},... | collective-permute-start | bytes 393224 | tf_op jit(solution)/shard_map/ppermute | solution.py:147
  99.5 1.6 %collective-permute-start.44 = (f32[256,128]{1,0:T(8,128)S(1)}, f32[256,128]{1,0:T(8,128)S(1)}, u32[]{:S(2)}, u32[]{:S(2)}) collective-permute-start(f32[256,128]{1,0:T(8,128)S(1)} %get-tuple-element.48.refs_7_.refs_23_.refs_35_), channel_id=1, source_target_pairs={{0,10},{1,11},{2,8},{3,9},{4,14},{5,15},{6,12},{7,13},{8,2},{9,3},... | collective-permute-start | bytes 393224 | tf_op jit(solution)/shard_map/ppermute | solution.py:147
  101.1 0.8 collective-permute-start.45
  101.9 1.0 collective-permute-start.46
  102.9 1.7 %collective-permute-done.42.own = f32[256,128]{1,0:T(8,128)S(1)} collective-permute-done((f32[256,128]{1,0:T(8,128)S(1)}, f32[256,128]{1,0:T(8,128)S(1)}, u32[]{:S(2)}, u32[]{:S(2)}) %collective-permute-start.42) | collective-permute-done | bytes 131104 | tf_op jit(solution)/shard_map/ppermute | solution.py:147
  105.2 1.3 factor.24
  106.5 1.4 collective-permute-done.43.own
  107.9 1.0 collective-permute-start.48
  108.9 1.1 factor.26
  111.9 1.0 collective-permute-done.48.refs_6_.refs_22_
  115.5 2.8 %collective-permute-start.57 = (f32[128,128]{1,0:T(8,128)S(1)}, f32[128,128]{1,0:T(8,128)S(1)}, u32[]{:S(2)}, u32[]{:S(2)}) collective-permute-start(f32[128,128]{1,0:T(8,128)S(1)} %update.5), channel_id=1, source_target_pairs={{0,16},{1,17},{2,18},{3,19},{4,20},{5,21},{6,22},{7,23},{8,24},{9,... | collective-permute-start | bytes 196616 | tf_op jit(solution)/shard_map/ppermute | solution.py:147
  118.3 4.0 %collective-permute-done.57 = f32[128,128]{1,0:T(8,128)S(1)} collective-permute-done((f32[128,128]{1,0:T(8,128)S(1)}, f32[128,128]{1,0:T(8,128)S(1)}, u32[]{:S(2)}, u32[]{:S(2)}) %collective-permute-start.57) | collective-permute-done | bytes 65568 | tf_op jit(solution)/shard_map/ppermute | solution.py:147
  122.3 1.5 %collective-permute-start.58 = (f32[256,128]{1,0:T(8,128)S(1)}, f32[256,128]{1,0:T(8,128)S(1)}, u32[]{:S(2)}, u32[]{:S(2)}) collective-permute-start(f32[256,128]{1,0:T(8,128)S(1)} %pad_maximum_fusion.refs_7_), channel_id=1, source_target_pairs={{0,14},{1,15},{2,12},{3,13},{4,10},{5,11},{6,8},{7,9},{8,6},{9,7},... | collective-permute-start | bytes 393224 | tf_op jit(solution)/shard_map/ppermute | solution.py:147
  123.7 2.0 %collective-permute-start.59 = (f32[256,128]{1,0:T(8,128)S(1)}, f32[256,128]{1,0:T(8,128)S(1)}, u32[]{:S(2)}, u32[]{:S(2)}) collective-permute-start(f32[256,128]{1,0:T(8,128)S(1)} %pad_maximum_fusion.refs_7_), channel_id=1, source_target_pairs={{0,12},{1,13},{2,14},{3,15},{4,8},{5,9},{6,10},{7,11},{8,4},{9,5},... | collective-permute-start | bytes 393224 | tf_op jit(solution)/shard_map/ppermute | solution.py:147
  125.7 0.9 collective-permute-start.60
  126.6 1.6 %collective-permute-start.61 = (f32[256,128]{1,0:T(8,128)S(1)}, f32[256,128]{1,0:T(8,128)S(1)}, u32[]{:S(2)}, u32[]{:S(2)}) collective-permute-start(f32[256,128]{1,0:T(8,128)S(1)} %pad_maximum_fusion.refs_7_), channel_id=1, source_target_pairs={{0,8},{1,9},{2,10},{3,11},{4,12},{5,13},{6,14},{7,15},{8,0},{9,1},... | collective-permute-start | bytes 393224 | tf_op jit(solution)/shard_map/ppermute | solution.py:147
  128.2 1.5 %collective-permute-start.62 = (f32[256,128]{1,0:T(8,128)S(1)}, f32[256,128]{1,0:T(8,128)S(1)}, u32[]{:S(2)}, u32[]{:S(2)}) collective-permute-start(f32[256,128]{1,0:T(8,128)S(1)} %pad_maximum_fusion.refs_7_), channel_id=1, source_target_pairs={{0,6},{1,7},{2,4},{3,5},{4,2},{5,3},{6,0},{7,1},{8,14},{9,15},{10,... | collective-permute-start | bytes 393224 | tf_op jit(solution)/shard_map/ppermute | solution.py:147
  129.7 1.4 %collective-permute-done.58.refs_0_ = f32[256,128]{1,0:T(8,128)S(1)} collective-permute-done((f32[256,128]{1,0:T(8,128)S(1)}, f32[256,128]{1,0:T(8,128)S(1)}, u32[]{:S(2)}, u32[]{:S(2)}) %collective-permute-start.58) | collective-permute-done | bytes 131104 | tf_op jit(solution)/shard_map/ppermute | solution.py:147
  131.2 1.0 collective-permute-start.63
  132.1 1.3 collective-permute-done.59.refs_1_
  133.4 1.0 collective-permute-start.64
  134.4 1.3 collective-permute-done.60.refs_2_
  135.7 1.0 collective-permute-done.61.refs_3_
  140.4 2.4 %pivots.7 = f32[960,128]{1,0:T(8,128)} custom-call(s32[1]{0:T(128)} %bitcast.1.me, s32[16,14]{1,0:T(8,128)S(1)} %bitcast.6, f32[256,128]{1,0:T(8,128)S(1)} %collective-permute-done.58.refs_0_, f32[256,128]{1,0:T(8,128)S(1)} %collective-permute-done.59.refs_1_, f32[256,128]{1,0:T(8,128)S(1)} %collective-permute-done.60.refs_2_, ...), custom_call_target="tpu_custom_call" | custom-call | flops 100663296 | bytes 8000000 | tf_op jit(solution)/shard_map/pivots/pallas_call | solution.py:299
  (118 shorter events, 19.8 us)
Async XLA Ops:
  0.6 14.4 %collective-permute-start.3 = (f32[960,128]{1,0:T(8,128)}, f32[960,128]{1,0:T(8,128)S(1)}, u32[]{:S(2)}, u32[]{:S(2)}) collective-permute-start(f32[960,128]{1,0:T(8,128)} %refs_0_.1), channel_id=1, source_target_pairs={{0,2},{1,3},{2,0},{3,1},{4,6},{5,7},{6,4},{7,5},{8,10},{9,11},{10,... | collective-permute-start | bytes 1474568 | tf_op jit(solution)/shard_map/ppermute | solution.py:147
  15.1 7.8 %collective-permute-start.4 = (f32[1024,128]{1,0:T(8,128)S(1)}, f32[1024,128]{1,0:T(8,128)S(1)}, u32[]{:S(2)}, u32[]{:S(2)}) collective-permute-start(f32[1024,128]{1,0:T(8,128)S(1)} %get-tuple-element.31.refs_4_), channel_id=1, source_target_pairs={{0,1},{1,0},{2,3},{3,2},{4,5},{5,4},{6,7},{7,6},{8,9},{9,8},{10,11... | collective-permute-start | bytes 1572872 | tf_op jit(solution)/shard_map/ppermute | solution.py:147
  15.2 6.4 %collective-permute-start = (f32[256,128]{1,0:T(8,128)S(1)}, f32[256,128]{1,0:T(8,128)S(1)}, u32[]{:S(2)}, u32[]{:S(2)}) collective-permute-start(f32[256,128]{1,0:T(8,128)S(1)} %get-tuple-element.29.own.after), channel_id=1, source_target_pairs={{0,2},{1,3},{2,0},{3,1},{4,6},{5,7},{6,4},{7,5},{8,10},{9,11},{10,... | collective-permute-start | bytes 393224 | tf_op jit(solution)/shard_map/ppermute | solution.py:147
  27.2 8.6 %collective-permute-start.5 = (f32[512,128]{1,0:T(8,128)S(1)}, f32[512,128]{1,0:T(8,128)S(1)}, u32[]{:S(2)}, u32[]{:S(2)}) collective-permute-start(f32[512,128]{1,0:T(8,128)S(1)} %get-tuple-element.33.own.refs_33_), channel_id=1, source_target_pairs={{0,2},{1,3},{2,0},{3,1},{4,6},{5,7},{6,4},{7,5},{8,10},{9,11},{10,... | collective-permute-start | bytes 786440 | tf_op jit(solution)/shard_map/ppermute | solution.py:147
  28.5 13.8 %collective-permute-start.15 = (f32[768,128]{1,0:T(8,128)S(1)}, f32[768,128]{1,0:T(8,128)S(1)}, u32[]{:S(2)}, u32[]{:S(2)}) collective-permute-start(f32[768,128]{1,0:T(8,128)S(1)} %get-tuple-element.38.refs_0_), channel_id=1, source_target_pairs={{0,4},{1,5},{2,6},{3,7},{4,0},{5,1},{6,2},{7,3},{8,12},{9,13},{10,... | collective-permute-start | bytes 1179656 | tf_op jit(solution)/shard_map/ppermute | solution.py:147
  32.4 3.4 %collective-permute-start.7 = (f32[512,128]{1,0:T(8,128)S(1)}, f32[512,128]{1,0:T(8,128)S(1)}, u32[]{:S(2)}, u32[]{:S(2)}) collective-permute-start(f32[512,128]{1,0:T(8,128)S(1)} %get-tuple-element.34.refs_1_), channel_id=1, source_target_pairs={{0,1},{1,0},{2,3},{3,2},{4,5},{5,4},{6,7},{7,6},{8,9},{9,8},{10,11... | collective-permute-start | bytes 786440 | tf_op jit(solution)/shard_map/ppermute | solution.py:147
  35.8 1.5 %collective-permute-start.6 = (f32[512,128]{1,0:T(8,128)S(1)}, f32[512,128]{1,0:T(8,128)S(1)}, u32[]{:S(2)}, u32[]{:S(2)}) collective-permute-start(f32[512,128]{1,0:T(8,128)S(1)} %collective-permute-done.5.refs_0_), channel_id=1, source_target_pairs={{0,1},{1,0},{2,3},{3,2},{4,5},{5,4},{6,7},{7,6},{8,9},{9,8},{10,11... | collective-permute-start | bytes 786440 | tf_op jit(solution)/shard_map/ppermute | solution.py:147
  38.8 10.2 %collective-permute-start.8 = (f32[512,128]{1,0:T(8,128)S(1)}, f32[512,128]{1,0:T(8,128)S(1)}, u32[]{:S(2)}, u32[]{:S(2)}) collective-permute-start(f32[512,128]{1,0:T(8,128)S(1)} %update.3.after.refs_3_), channel_id=1, source_target_pairs={{0,6},{1,7},{2,4},{3,5},{4,2},{5,3},{6,0},{7,1},{8,14},{9,15},{10,... | collective-permute-start | bytes 786440 | tf_op jit(solution)/shard_map/ppermute | solution.py:147
  40.9 13.0 %collective-permute-start.9 = (f32[512,128]{1,0:T(8,128)S(1)}, f32[512,128]{1,0:T(8,128)S(1)}, u32[]{:S(2)}, u32[]{:S(2)}) collective-permute-start(f32[512,128]{1,0:T(8,128)S(1)} %update.3.after.refs_3_), channel_id=1, source_target_pairs={{0,4},{1,5},{2,6},{3,7},{4,0},{5,1},{6,2},{7,3},{8,12},{9,13},{10,... | collective-permute-start | bytes 786440 | tf_op jit(solution)/shard_map/ppermute | solution.py:147
  41.4 13.0 %collective-permute-start.10 = (f32[512,128]{1,0:T(8,128)S(1)}, f32[512,128]{1,0:T(8,128)}, u32[]{:S(2)}, u32[]{:S(2)}) collective-permute-start(f32[512,128]{1,0:T(8,128)S(1)} %update.3.after.refs_3_), channel_id=1, source_target_pairs={{0,2},{1,3},{2,0},{3,1},{4,6},{5,7},{6,4},{7,5},{8,10},{9,11},{10,... | collective-permute-start | bytes 786440 | tf_op jit(solution)/shard_map/ppermute | solution.py:147
  43.1 13.8 %collective-permute-start.16 = (f32[1024,128]{1,0:T(8,128)S(1)}, f32[1024,128]{1,0:T(8,128)}, u32[]{:S(2)}, u32[]{:S(2)}) collective-permute-start(f32[1024,128]{1,0:T(8,128)S(1)} %get-tuple-element.39.refs_8_), channel_id=1, source_target_pairs={{0,1},{1,0},{2,3},{3,2},{4,5},{5,4},{6,7},{7,6},{8,9},{9,8},{10,11... | collective-permute-start | bytes 1572872 | tf_op jit(solution)/shard_map/ppermute | solution.py:147
  43.1 11.4 %collective-permute-start.14 = (f32[512,128]{1,0:T(8,128)S(1)}, f32[512,128]{1,0:T(8,128)S(1)}, u32[]{:S(2)}, u32[]{:S(2)}) collective-permute-start(f32[512,128]{1,0:T(8,128)S(1)} %update.3.after.refs_3_), channel_id=1, source_target_pairs={{0,1},{1,0},{2,3},{3,2},{4,5},{5,4},{6,7},{7,6},{8,9},{9,8},{10,11... | collective-permute-start | bytes 786440 | tf_op jit(solution)/shard_map/ppermute | solution.py:147
  49.0 4.9 %collective-permute-start.17 = (f32[64,128]{1,0:T(8,128)S(1)}, f32[64,128]{1,0:T(8,128)S(1)}, u32[]{:S(2)}, u32[]{:S(2)}) collective-permute-start(f32[64,128]{1,0:T(8,128)S(1)} %slice.3.refs_0_), channel_id=1, source_target_pairs={{0,16},{1,17},{2,18},{3,19},{4,20},{5,21},{6,22},{7,23},{8,24},{9,... | collective-permute-start | bytes 98312 | tf_op jit(solution)/shard_map/ppermute | solution.py:147
  53.8 3.0 %collective-permute-start.11 = (f32[512,128]{1,0:T(8,128)}, f32[512,128]{1,0:T(8,128)}, u32[]{:S(2)}, u32[]{:S(2)}) collective-permute-start(f32[512,128]{1,0:T(8,128)} %get-tuple-element.37.refs_0_), channel_id=1, source_target_pairs={{0,1},{1,0},{2,3},{3,2},{4,5},{5,4},{6,7},{7,6},{8,9},{9,8},{10,11... | collective-permute-start | bytes 786440 | tf_op jit(solution)/shard_map/ppermute | solution.py:147
  53.9 3.0 %collective-permute-start.12 = (f32[512,128]{1,0:T(8,128)S(1)}, f32[512,128]{1,0:T(8,128)}, u32[]{:S(2)}, u32[]{:S(2)}) collective-permute-start(f32[512,128]{1,0:T(8,128)S(1)} %collective-permute-done.9.refs_1_), channel_id=1, source_target_pairs={{0,1},{1,0},{2,3},{3,2},{4,5},{5,4},{6,7},{7,6},{8,9},{9,8},{10,11... | collective-permute-start | bytes 786440 | tf_op jit(solution)/shard_map/ppermute | solution.py:147
  54.4 2.5 %collective-permute-start.13 = (f32[512,128]{1,0:T(8,128)}, f32[512,128]{1,0:T(8,128)}, u32[]{:S(2)}, u32[]{:S(2)}) collective-permute-start(f32[512,128]{1,0:T(8,128)} %collective-permute-done.10.refs_2_), channel_id=1, source_target_pairs={{0,1},{1,0},{2,3},{3,2},{4,5},{5,4},{6,7},{7,6},{8,9},{9,8},{10,11... | collective-permute-start | bytes 786440 | tf_op jit(solution)/shard_map/ppermute | solution.py:147
  55.2 15.3 %collective-permute-start.40 = (f32[512,128]{1,0:T(8,128)}, f32[512,128]{1,0:T(8,128)}, u32[]{:S(2)}, u32[]{:S(2)}) collective-permute-start(f32[512,128]{1,0:T(8,128)} %get-tuple-element.46.refs_0_), channel_id=1, source_target_pairs={{0,8},{1,9},{2,10},{3,11},{4,12},{5,13},{6,14},{7,15},{8,0},{9,1},... | collective-permute-start | bytes 786440 | tf_op jit(solution)/shard_map/ppermute | solution.py:147
  60.6 7.2 %collective-permute-start.18 = (f32[256,128]{1,0:T(8,128)S(1)}, f32[256,128]{1,0:T(8,128)S(1)}, u32[]{:S(2)}, u32[]{:S(2)}) collective-permute-start(f32[256,128]{1,0:T(8,128)S(1)} %get-tuple-element.41.refs_3_.after.refs_34_), channel_id=1, source_target_pairs={{0,6},{1,7},{2,4},{3,5},{4,2},{5,3},{6,0},{7,1},{8,14},{9,15},{10,... | collective-permute-start | bytes 393224 | tf_op jit(solution)/shard_map/ppermute | solution.py:147
  62.8 7.2 %collective-permute-start.19 = (f32[256,128]{1,0:T(8,128)S(1)}, f32[256,128]{1,0:T(8,128)S(1)}, u32[]{:S(2)}, u32[]{:S(2)}) collective-permute-start(f32[256,128]{1,0:T(8,128)S(1)} %get-tuple-element.41.refs_3_.after.refs_34_), channel_id=1, source_target_pairs={{0,4},{1,5},{2,6},{3,7},{4,0},{5,1},{6,2},{7,3},{8,12},{9,13},{10,... | collective-permute-start | bytes 393224 | tf_op jit(solution)/shard_map/ppermute | solution.py:147
  63.3 6.8 %collective-permute-start.20 = (f32[256,128]{1,0:T(8,128)S(1)}, f32[256,128]{1,0:T(8,128)S(1)}, u32[]{:S(2)}, u32[]{:S(2)}) collective-permute-start(f32[256,128]{1,0:T(8,128)S(1)} %get-tuple-element.41.refs_3_.after.refs_34_), channel_id=1, source_target_pairs={{0,2},{1,3},{2,0},{3,1},{4,6},{5,7},{6,4},{7,5},{8,10},{9,11},{10,... | collective-permute-start | bytes 393224 | tf_op jit(solution)/shard_map/ppermute | solution.py:147
  64.2 7.5 %collective-permute-start.24 = (f32[256,128]{1,0:T(8,128)S(1)}, f32[256,128]{1,0:T(8,128)S(1)}, u32[]{:S(2)}, u32[]{:S(2)}) collective-permute-start(f32[256,128]{1,0:T(8,128)S(1)} %get-tuple-element.41.refs_3_.after.refs_34_), channel_id=1, source_target_pairs={{0,1},{1,0},{2,3},{3,2},{4,5},{5,4},{6,7},{7,6},{8,9},{9,8},{10,11... | collective-permute-start | bytes 393224 | tf_op jit(solution)/shard_map/ppermute | solution.py:147
  69.5 2.2 %collective-permute-start.21 = (f32[256,128]{1,0:T(8,128)S(1)}, f32[256,128]{1,0:T(8,128)S(1)}, u32[]{:S(2)}, u32[]{:S(2)}) collective-permute-start(f32[256,128]{1,0:T(8,128)S(1)} %get-tuple-element.42.refs_0_), channel_id=1, source_target_pairs={{0,1},{1,0},{2,3},{3,2},{4,5},{5,4},{6,7},{7,6},{8,9},{9,8},{10,11... | collective-permute-start | bytes 393224 | tf_op jit(solution)/shard_map/ppermute | solution.py:147
  70.0 1.8 %collective-permute-start.22 = (f32[256,128]{1,0:T(8,128)S(1)}, f32[256,128]{1,0:T(8,128)S(1)}, u32[]{:S(2)}, u32[]{:S(2)}) collective-permute-start(f32[256,128]{1,0:T(8,128)S(1)} %collective-permute-done.19.refs_1_), channel_id=1, source_target_pairs={{0,1},{1,0},{2,3},{3,2},{4,5},{5,4},{6,7},{7,6},{8,9},{9,8},{10,11... | collective-permute-start | bytes 393224 | tf_op jit(solution)/shard_map/ppermute | solution.py:147
  70.1 1.7 %collective-permute-start.23 = (f32[256,128]{1,0:T(8,128)S(1)}, f32[256,128]{1,0:T(8,128)S(1)}, u32[]{:S(2)}, u32[]{:S(2)}) collective-permute-start(f32[256,128]{1,0:T(8,128)S(1)} %collective-permute-done.20.refs_2_), channel_id=1, source_target_pairs={{0,1},{1,0},{2,3},{3,2},{4,5},{5,4},{6,7},{7,6},{8,9},{9,8},{10,11... | collective-permute-start | bytes 393224 | tf_op jit(solution)/shard_map/ppermute | solution.py:147
  71.6 21.0 %collective-permute-start.41 = (f32[1024,128]{1,0:T(8,128)S(1)}, f32[1024,128]{1,0:T(8,128)S(1)}, u32[]{:S(2)}, u32[]{:S(2)}) collective-permute-start(f32[1024,128]{1,0:T(8,128)S(1)} %join.7.refs_16_), channel_id=1, source_target_pairs={{0,1},{1,0},{2,3},{3,2},{4,5},{5,4},{6,7},{7,6},{8,9},{9,8},{10,11... | collective-permute-start | bytes 1572872 | tf_op jit(solution)/shard_map/ppermute | solution.py:147
  72.7 8.6 %collective-permute-start.25 = (f32[256,128]{1,0:T(8,128)S(1)}, f32[256,128]{1,0:T(8,128)S(1)}, u32[]{:S(2)}, u32[]{:S(2)}) collective-permute-start(f32[256,128]{1,0:T(8,128)S(1)} %update.4.refs_7_), channel_id=1, source_target_pairs={{0,14},{1,15},{2,12},{3,13},{4,10},{5,11},{6,8},{7,9},{8,6},{9,7},... | collective-permute-start | bytes 393224 | tf_op jit(solution)/shard_map/ppermute | solution.py:147
  75.6 8.1 %collective-permute-start.26 = (f32[256,128]{1,0:T(8,128)S(1)}, f32[256,128]{1,0:T(8,128)S(1)}, u32[]{:S(2)}, u32[]{:S(2)}) collective-permute-start(f32[256,128]{1,0:T(8,128)S(1)} %update.4.refs_7_), channel_id=1, source_target_pairs={{0,12},{1,13},{2,14},{3,15},{4,8},{5,9},{6,10},{7,11},{8,4},{9,5},... | collective-permute-start | bytes 393224 | tf_op jit(solution)/shard_map/ppermute | solution.py:147
  76.3 10.7 %collective-permute-start.27 = (f32[256,128]{1,0:T(8,128)S(1)}, f32[256,128]{1,0:T(8,128)S(1)}, u32[]{:S(2)}, u32[]{:S(2)}) collective-permute-start(f32[256,128]{1,0:T(8,128)S(1)} %update.4.refs_7_), channel_id=1, source_target_pairs={{0,10},{1,11},{2,8},{3,9},{4,14},{5,15},{6,12},{7,13},{8,2},{9,3},... | collective-permute-start | bytes 393224 | tf_op jit(solution)/shard_map/ppermute | solution.py:147
  77.8 10.8 %collective-permute-start.28 = (f32[256,128]{1,0:T(8,128)S(1)}, f32[256,128]{1,0:T(8,128)S(1)}, u32[]{:S(2)}, u32[]{:S(2)}) collective-permute-start(f32[256,128]{1,0:T(8,128)S(1)} %update.4.refs_7_), channel_id=1, source_target_pairs={{0,8},{1,9},{2,10},{3,11},{4,12},{5,13},{6,14},{7,15},{8,0},{9,1},... | collective-permute-start | bytes 393224 | tf_op jit(solution)/shard_map/ppermute | solution.py:147
  81.2 8.6 %collective-permute-start.29 = (f32[256,128]{1,0:T(8,128)S(1)}, f32[256,128]{1,0:T(8,128)S(1)}, u32[]{:S(2)}, u32[]{:S(2)}) collective-permute-start(f32[256,128]{1,0:T(8,128)S(1)} %update.4.refs_7_), channel_id=1, source_target_pairs={{0,6},{1,7},{2,4},{3,5},{4,2},{5,3},{6,0},{7,1},{8,14},{9,15},{10,... | collective-permute-start | bytes 393224 | tf_op jit(solution)/shard_map/ppermute | solution.py:147
  83.7 6.7 %collective-permute-start.30 = (f32[256,128]{1,0:T(8,128)S(1)}, f32[256,128]{1,0:T(8,128)S(1)}, u32[]{:S(2)}, u32[]{:S(2)}) collective-permute-start(f32[256,128]{1,0:T(8,128)S(1)} %update.4.refs_7_), channel_id=1, source_target_pairs={{0,4},{1,5},{2,6},{3,7},{4,0},{5,1},{6,2},{7,3},{8,12},{9,13},{10,... | collective-permute-start | bytes 393224 | tf_op jit(solution)/shard_map/ppermute | solution.py:147
  87.0 5.0 %collective-permute-start.31 = (f32[256,128]{1,0:T(8,128)S(1)}, f32[256,128]{1,0:T(8,128)S(1)}, u32[]{:S(2)}, u32[]{:S(2)}) collective-permute-start(f32[256,128]{1,0:T(8,128)S(1)} %update.4.refs_7_), channel_id=1, source_target_pairs={{0,2},{1,3},{2,0},{3,1},{4,6},{5,7},{6,4},{7,5},{8,10},{9,11},{10,... | collective-permute-start | bytes 393224 | tf_op jit(solution)/shard_map/ppermute | solution.py:147
  88.6 3.4 %collective-permute-start.39 = (f32[256,128]{1,0:T(8,128)S(1)}, f32[256,128]{1,0:T(8,128)S(1)}, u32[]{:S(2)}, u32[]{:S(2)}) collective-permute-start(f32[256,128]{1,0:T(8,128)S(1)} %update.4.refs_7_), channel_id=1, source_target_pairs={{0,1},{1,0},{2,3},{3,2},{4,5},{5,4},{6,7},{7,6},{8,9},{9,8},{10,11... | collective-permute-start | bytes 393224 | tf_op jit(solution)/shard_map/ppermute | solution.py:147
  89.8 2.7 %collective-permute-start.32 = (f32[256,128]{1,0:T(8,128)S(1)}, f32[256,128]{1,0:T(8,128)S(1)}, u32[]{:S(2)}, u32[]{:S(2)}) collective-permute-start(f32[256,128]{1,0:T(8,128)S(1)} %get-tuple-element.45.refs_0_), channel_id=1, source_target_pairs={{0,1},{1,0},{2,3},{3,2},{4,5},{5,4},{6,7},{7,6},{8,9},{9,8},{10,11... | collective-permute-start | bytes 393224 | tf_op jit(solution)/shard_map/ppermute | solution.py:147
  90.4 2.6 %collective-permute-start.33 = (f32[256,128]{1,0:T(8,128)S(1)}, f32[256,128]{1,0:T(8,128)S(1)}, u32[]{:S(2)}, u32[]{:S(2)}) collective-permute-start(f32[256,128]{1,0:T(8,128)S(1)} %collective-permute-done.26.refs_1_), channel_id=1, source_target_pairs={{0,1},{1,0},{2,3},{3,2},{4,5},{5,4},{6,7},{7,6},{8,9},{9,8},{10,11... | collective-permute-start | bytes 393224 | tf_op jit(solution)/shard_map/ppermute | solution.py:147
  92.0 1.5 %collective-permute-start.35 = (f32[256,128]{1,0:T(8,128)S(1)}, f32[256,128]{1,0:T(8,128)S(1)}, u32[]{:S(2)}, u32[]{:S(2)}) collective-permute-start(f32[256,128]{1,0:T(8,128)S(1)} %collective-permute-done.28.refs_3_), channel_id=1, source_target_pairs={{0,1},{1,0},{2,3},{3,2},{4,5},{5,4},{6,7},{7,6},{8,9},{9,8},{10,11... | collective-permute-start | bytes 393224 | tf_op jit(solution)/shard_map/ppermute | solution.py:147
  92.6 1.5 %collective-permute-start.37 = (f32[256,128]{1,0:T(8,128)S(1)}, f32[256,128]{1,0:T(8,128)S(1)}, u32[]{:S(2)}, u32[]{:S(2)}) collective-permute-start(f32[256,128]{1,0:T(8,128)S(1)} %collective-permute-done.30.refs_5_), channel_id=1, source_target_pairs={{0,1},{1,0},{2,3},{3,2},{4,5},{5,4},{6,7},{7,6},{8,9},{9,8},{10,11... | collective-permute-start | bytes 393224 | tf_op jit(solution)/shard_map/ppermute | solution.py:147
  96.0 8.6 %collective-permute-start.42 = (f32[256,128]{1,0:T(8,128)S(1)}, f32[256,128]{1,0:T(8,128)S(1)}, u32[]{:S(2)}, u32[]{:S(2)}) collective-permute-start(f32[256,128]{1,0:T(8,128)S(1)} %get-tuple-element.48.refs_7_.refs_23_.refs_35_), channel_id=1, source_target_pairs={{0,14},{1,15},{2,12},{3,13},{4,10},{5,11},{6,8},{7,9},{8,6},{9,7},... | collective-permute-start | bytes 393224 | tf_op jit(solution)/shard_map/ppermute | solution.py:147
  97.7 10.2 %collective-permute-start.43 = (f32[256,128]{1,0:T(8,128)S(1)}, f32[256,128]{1,0:T(8,128)S(1)}, u32[]{:S(2)}, u32[]{:S(2)}) collective-permute-start(f32[256,128]{1,0:T(8,128)S(1)} %get-tuple-element.48.refs_7_.refs_23_.refs_35_), channel_id=1, source_target_pairs={{0,12},{1,13},{2,14},{3,15},{4,8},{5,9},{6,10},{7,11},{8,4},{9,5},... | collective-permute-start | bytes 393224 | tf_op jit(solution)/shard_map/ppermute | solution.py:147
  99.5 10.6 %collective-permute-start.44 = (f32[256,128]{1,0:T(8,128)S(1)}, f32[256,128]{1,0:T(8,128)S(1)}, u32[]{:S(2)}, u32[]{:S(2)}) collective-permute-start(f32[256,128]{1,0:T(8,128)S(1)} %get-tuple-element.48.refs_7_.refs_23_.refs_35_), channel_id=1, source_target_pairs={{0,10},{1,11},{2,8},{3,9},{4,14},{5,15},{6,12},{7,13},{8,2},{9,3},... | collective-permute-start | bytes 393224 | tf_op jit(solution)/shard_map/ppermute | solution.py:147
  101.1 9.8 %collective-permute-start.45 = (f32[256,128]{1,0:T(8,128)S(1)}, f32[256,128]{1,0:T(8,128)S(1)}, u32[]{:S(2)}, u32[]{:S(2)}) collective-permute-start(f32[256,128]{1,0:T(8,128)S(1)} %get-tuple-element.48.refs_7_.refs_23_.refs_35_), channel_id=1, source_target_pairs={{0,8},{1,9},{2,10},{3,11},{4,12},{5,13},{6,14},{7,15},{8,0},{9,1},... | collective-permute-start | bytes 393224 | tf_op jit(solution)/shard_map/ppermute | solution.py:147
  101.9 9.4 %collective-permute-start.46 = (f32[256,128]{1,0:T(8,128)S(1)}, f32[256,128]{1,0:T(8,128)S(1)}, u32[]{:S(2)}, u32[]{:S(2)}) collective-permute-start(f32[256,128]{1,0:T(8,128)S(1)} %get-tuple-element.48.refs_7_.refs_23_.refs_35_), channel_id=1, source_target_pairs={{0,6},{1,7},{2,4},{3,5},{4,2},{5,3},{6,0},{7,1},{8,14},{9,15},{10,... | collective-permute-start | bytes 393224 | tf_op jit(solution)/shard_map/ppermute | solution.py:147
  104.6 7.3 %collective-permute-start.47 = (f32[256,128]{1,0:T(8,128)S(1)}, f32[256,128]{1,0:T(8,128)S(1)}, u32[]{:S(2)}, u32[]{:S(2)}) collective-permute-start(f32[256,128]{1,0:T(8,128)S(1)} %get-tuple-element.48.refs_7_.refs_23_.refs_35_), channel_id=1, source_target_pairs={{0,4},{1,5},{2,6},{3,7},{4,0},{5,1},{6,2},{7,3},{8,12},{9,13},{10,... | collective-permute-start | bytes 393224 | tf_op jit(solution)/shard_map/ppermute | solution.py:147
  107.9 5.0 %collective-permute-start.48 = (f32[256,128]{1,0:T(8,128)S(1)}, f32[256,128]{1,0:T(8,128)S(1)}, u32[]{:S(2)}, u32[]{:S(2)}) collective-permute-start(f32[256,128]{1,0:T(8,128)S(1)} %get-tuple-element.48.refs_7_.refs_23_.refs_35_), channel_id=1, source_target_pairs={{0,2},{1,3},{2,0},{3,1},{4,6},{5,7},{6,4},{7,5},{8,10},{9,11},{10,... | collective-permute-start | bytes 393224 | tf_op jit(solution)/shard_map/ppermute | solution.py:147
  110.1 2.8 %collective-permute-start.56 = (f32[256,128]{1,0:T(8,128)S(1)}, f32[256,128]{1,0:T(8,128)S(1)}, u32[]{:S(2)}, u32[]{:S(2)}) collective-permute-start(f32[256,128]{1,0:T(8,128)S(1)} %get-tuple-element.48.refs_7_.refs_23_.refs_35_), channel_id=1, source_target_pairs={{0,1},{1,0},{2,3},{3,2},{4,5},{5,4},{6,7},{7,6},{8,9},{9,8},{10,11... | collective-permute-start | bytes 393224 | tf_op jit(solution)/shard_map/ppermute | solution.py:147
  110.9 2.5 %collective-permute-start.49 = (f32[256,128]{1,0:T(8,128)S(1)}, f32[256,128]{1,0:T(8,128)S(1)}, u32[]{:S(2)}, u32[]{:S(2)}) collective-permute-start(f32[256,128]{1,0:T(8,128)S(1)} %get-tuple-element.49.refs_0_.refs_16_), channel_id=1, source_target_pairs={{0,1},{1,0},{2,3},{3,2},{4,5},{5,4},{6,7},{7,6},{8,9},{9,8},{10,11... | collective-permute-start | bytes 393224 | tf_op jit(solution)/shard_map/ppermute | solution.py:147
  111.4 2.1 %collective-permute-start.50 = (f32[256,128]{1,0:T(8,128)S(1)}, f32[256,128]{1,0:T(8,128)S(1)}, u32[]{:S(2)}, u32[]{:S(2)}) collective-permute-start(f32[256,128]{1,0:T(8,128)S(1)} %get-tuple-element.50.refs_1_.refs_17_), channel_id=1, source_target_pairs={{0,1},{1,0},{2,3},{3,2},{4,5},{5,4},{6,7},{7,6},{8,9},{9,8},{10,11... | collective-permute-start | bytes 393224 | tf_op jit(solution)/shard_map/ppermute | solution.py:147
  111.9 2.0 %collective-permute-start.51 = (f32[256,128]{1,0:T(8,128)S(1)}, f32[256,128]{1,0:T(8,128)S(1)}, u32[]{:S(2)}, u32[]{:S(2)}) collective-permute-start(f32[256,128]{1,0:T(8,128)S(1)} %collective-permute-done.44.refs_2_.refs_18_), channel_id=1, source_target_pairs={{0,1},{1,0},{2,3},{3,2},{4,5},{5,4},{6,7},{7,6},{8,9},{9,8},{10,11... | collective-permute-start | bytes 393224 | tf_op jit(solution)/shard_map/ppermute | solution.py:147
  112.9 1.5 %collective-permute-start.53 = (f32[256,128]{1,0:T(8,128)S(1)}, f32[256,128]{1,0:T(8,128)S(1)}, u32[]{:S(2)}, u32[]{:S(2)}) collective-permute-start(f32[256,128]{1,0:T(8,128)S(1)} %collective-permute-done.46.refs_4_.refs_20_), channel_id=1, source_target_pairs={{0,1},{1,0},{2,3},{3,2},{4,5},{5,4},{6,7},{7,6},{8,9},{9,8},{10,11... | collective-permute-start | bytes 393224 | tf_op jit(solution)/shard_map/ppermute | solution.py:147
  113.5 1.5 %collective-permute-start.55 = (f32[256,128]{1,0:T(8,128)S(1)}, f32[256,128]{1,0:T(8,128)S(1)}, u32[]{:S(2)}, u32[]{:S(2)}) collective-permute-start(f32[256,128]{1,0:T(8,128)S(1)} %collective-permute-done.48.refs_6_.refs_22_), channel_id=1, source_target_pairs={{0,1},{1,0},{2,3},{3,2},{4,5},{5,4},{6,7},{7,6},{8,9},{9,8},{10,11... | collective-permute-start | bytes 393224 | tf_op jit(solution)/shard_map/ppermute | solution.py:147
  115.5 6.8 %collective-permute-start.57 = (f32[128,128]{1,0:T(8,128)S(1)}, f32[128,128]{1,0:T(8,128)S(1)}, u32[]{:S(2)}, u32[]{:S(2)}) collective-permute-start(f32[128,128]{1,0:T(8,128)S(1)} %update.5), channel_id=1, source_target_pairs={{0,16},{1,17},{2,18},{3,19},{4,20},{5,21},{6,22},{7,23},{8,24},{9,... | collective-permute-start | bytes 196616 | tf_op jit(solution)/shard_map/ppermute | solution.py:147
  122.3 8.9 %collective-permute-start.58 = (f32[256,128]{1,0:T(8,128)S(1)}, f32[256,128]{1,0:T(8,128)S(1)}, u32[]{:S(2)}, u32[]{:S(2)}) collective-permute-start(f32[256,128]{1,0:T(8,128)S(1)} %pad_maximum_fusion.refs_7_), channel_id=1, source_target_pairs={{0,14},{1,15},{2,12},{3,13},{4,10},{5,11},{6,8},{7,9},{8,6},{9,7},... | collective-permute-start | bytes 393224 | tf_op jit(solution)/shard_map/ppermute | solution.py:147
  123.7 9.7 %collective-permute-start.59 = (f32[256,128]{1,0:T(8,128)S(1)}, f32[256,128]{1,0:T(8,128)S(1)}, u32[]{:S(2)}, u32[]{:S(2)}) collective-permute-start(f32[256,128]{1,0:T(8,128)S(1)} %pad_maximum_fusion.refs_7_), channel_id=1, source_target_pairs={{0,12},{1,13},{2,14},{3,15},{4,8},{5,9},{6,10},{7,11},{8,4},{9,5},... | collective-permute-start | bytes 393224 | tf_op jit(solution)/shard_map/ppermute | solution.py:147
  125.7 10.0 %collective-permute-start.60 = (f32[256,128]{1,0:T(8,128)S(1)}, f32[256,128]{1,0:T(8,128)S(1)}, u32[]{:S(2)}, u32[]{:S(2)}) collective-permute-start(f32[256,128]{1,0:T(8,128)S(1)} %pad_maximum_fusion.refs_7_), channel_id=1, source_target_pairs={{0,10},{1,11},{2,8},{3,9},{4,14},{5,15},{6,12},{7,13},{8,2},{9,3},... | collective-permute-start | bytes 393224 | tf_op jit(solution)/shard_map/ppermute | solution.py:147
  126.6 10.1 %collective-permute-start.61 = (f32[256,128]{1,0:T(8,128)S(1)}, f32[256,128]{1,0:T(8,128)S(1)}, u32[]{:S(2)}, u32[]{:S(2)}) collective-permute-start(f32[256,128]{1,0:T(8,128)S(1)} %pad_maximum_fusion.refs_7_), channel_id=1, source_target_pairs={{0,8},{1,9},{2,10},{3,11},{4,12},{5,13},{6,14},{7,15},{8,0},{9,1},... | collective-permute-start | bytes 393224 | tf_op jit(solution)/shard_map/ppermute | solution.py:147
  128.2 9.1 %collective-permute-start.62 = (f32[256,128]{1,0:T(8,128)S(1)}, f32[256,128]{1,0:T(8,128)S(1)}, u32[]{:S(2)}, u32[]{:S(2)}) collective-permute-start(f32[256,128]{1,0:T(8,128)S(1)} %pad_maximum_fusion.refs_7_), channel_id=1, source_target_pairs={{0,6},{1,7},{2,4},{3,5},{4,2},{5,3},{6,0},{7,1},{8,14},{9,15},{10,... | collective-permute-start | bytes 393224 | tf_op jit(solution)/shard_map/ppermute | solution.py:147
  131.2 6.4 %collective-permute-start.63 = (f32[256,128]{1,0:T(8,128)S(1)}, f32[256,128]{1,0:T(8,128)S(1)}, u32[]{:S(2)}, u32[]{:S(2)}) collective-permute-start(f32[256,128]{1,0:T(8,128)S(1)} %pad_maximum_fusion.refs_7_), channel_id=1, source_target_pairs={{0,4},{1,5},{2,6},{3,7},{4,0},{5,1},{6,2},{7,3},{8,12},{9,13},{10,... | collective-permute-start | bytes 393224 | tf_op jit(solution)/shard_map/ppermute | solution.py:147
  133.4 5.0 %collective-permute-start.64 = (f32[256,128]{1,0:T(8,128)S(1)}, f32[256,128]{1,0:T(8,128)S(1)}, u32[]{:S(2)}, u32[]{:S(2)}) collective-permute-start(f32[256,128]{1,0:T(8,128)S(1)} %pad_maximum_fusion.refs_7_), channel_id=1, source_target_pairs={{0,2},{1,3},{2,0},{3,1},{4,6},{5,7},{6,4},{7,5},{8,10},{9,11},{10,... | collective-permute-start | bytes 393224 | tf_op jit(solution)/shard_map/ppermute | solution.py:147
  135.7 2.7 %collective-permute-start.72 = (f32[256,128]{1,0:T(8,128)S(1)}, f32[256,128]{1,0:T(8,128)S(1)}, u32[]{:S(2)}, u32[]{:S(2)}) collective-permute-start(f32[256,128]{1,0:T(8,128)S(1)} %pad_maximum_fusion.refs_7_), channel_id=1, source_target_pairs={{0,1},{1,0},{2,3},{3,2},{4,5},{5,4},{6,7},{7,6},{8,9},{9,8},{10,11... | collective-permute-start | bytes 393224 | tf_op jit(solution)/shard_map/ppermute | solution.py:147
  136.7 2.2 %collective-permute-start.65 = (f32[256,128]{1,0:T(8,128)S(1)}, f32[256,128]{1,0:T(8,128)S(1)}, u32[]{:S(2)}, u32[]{:S(2)}) collective-permute-start(f32[256,128]{1,0:T(8,128)S(1)} %collective-permute-done.58.refs_0_), channel_id=1, source_target_pairs={{0,1},{1,0},{2,3},{3,2},{4,5},{5,4},{6,7},{7,6},{8,9},{9,8},{10,11... | collective-permute-start | bytes 393224 | tf_op jit(solution)/shard_map/ppermute | solution.py:147
  137.2 1.7 %collective-permute-start.66 = (f32[256,128]{1,0:T(8,128)S(1)}, f32[256,128]{1,0:T(8,128)S(1)}, u32[]{:S(2)}, u32[]{:S(2)}) collective-permute-start(f32[256,128]{1,0:T(8,128)S(1)} %collective-permute-done.59.refs_1_), channel_id=1, source_target_pairs={{0,1},{1,0},{2,3},{3,2},{4,5},{5,4},{6,7},{7,6},{8,9},{9,8},{10,11... | collective-permute-start | bytes 393224 | tf_op jit(solution)/shard_map/ppermute | solution.py:147
  137.6 1.8 %collective-permute-start.67 = (f32[256,128]{1,0:T(8,128)S(1)}, f32[256,128]{1,0:T(8,128)S(1)}, u32[]{:S(2)}, u32[]{:S(2)}) collective-permute-start(f32[256,128]{1,0:T(8,128)S(1)} %collective-permute-done.60.refs_2_), channel_id=1, source_target_pairs={{0,1},{1,0},{2,3},{3,2},{4,5},{5,4},{6,7},{7,6},{8,9},{9,8},{10,11... | collective-permute-start | bytes 393224 | tf_op jit(solution)/shard_map/ppermute | solution.py:147
  138.4 1.5 %collective-permute-start.69 = (f32[256,128]{1,0:T(8,128)S(1)}, f32[256,128]{1,0:T(8,128)S(1)}, u32[]{:S(2)}, u32[]{:S(2)}) collective-permute-start(f32[256,128]{1,0:T(8,128)S(1)} %collective-permute-done.62.refs_4_), channel_id=1, source_target_pairs={{0,1},{1,0},{2,3},{3,2},{4,5},{5,4},{6,7},{7,6},{8,9},{9,8},{10,11... | collective-permute-start | bytes 393224 | tf_op jit(solution)/shard_map/ppermute | solution.py:147
  138.9 1.5 %collective-permute-start.71 = (f32[256,128]{1,0:T(8,128)S(1)}, f32[256,128]{1,0:T(8,128)S(1)}, u32[]{:S(2)}, u32[]{:S(2)}) collective-permute-start(f32[256,128]{1,0:T(8,128)S(1)} %collective-permute-done.64.refs_6_), channel_id=1, source_target_pairs={{0,1},{1,0},{2,3},{3,2},{4,5},{5,4},{6,7},{7,6},{8,9},{9,8},{10,11... | collective-permute-start | bytes 393224 | tf_op jit(solution)/shard_map/ppermute | solution.py:147
  (16 other events, 50.4 us)

commit v4 on v3

--- a/solution.py
+++ b/solution.py
@@ -46,9 +46,9 @@
 
 
 def subtree_kernel(
-    bounds, pattern_in, rhs_in, dinv_in, off_in, upd_in, y_out, w, *scratch
+    bounds, pattern_in, rhs_in, dinv_in, off_in, upd_in, factor_in, y_out, w, factor_out, *scratch
 ):
-    pattern, rhs, dinv, off, upd, y, coef, lead, solved, sems, end_sems = scratch
+    pattern, rhs, dinv, off, upd, y, coef, lead, solved, factor, split, sems, end_sems, split_sems = scratch
     rounds = len(bounds) - 1
 
     def loads(r):
@@ -70,11 +70,15 @@
 
     pattern_copy = pltpu.make_async_copy(pattern_in, pattern, end_sems.at[0])
     upd_copy = pltpu.make_async_copy(upd_in, upd, end_sems.at[1])
+    factor_copy = pltpu.make_async_copy(
+        factor_in.at[: factor.shape[0]], factor, end_sems.at[2]
+    )
     pattern_copy.start()
     for r in range(rounds):
         for copy in loads(r):
             copy.start()
     upd_copy.start()
+    factor_copy.start()
 
     def put(i, value):
         rows = slice(i * B, (i + 1) * B)
@@ -92,6 +96,23 @@
         second = pl.multiple_of(pattern[1, i - 1] * B, B)
         known = jnp.concatenate([solved[pl.ds(first, B), :], solved[pl.ds(second, B), :]], 0)
         put(i, lead[i] + product(coef[i], known))
+
+    count = dinv.shape[0]
+    late = count - count // 3
+    share = factor.shape[0] // (count - late)
+
+    def split_factor(n):
+        rows = slice(n * share, (n + 1) * share)
+        for k, part in enumerate(halves(factor[rows, :])):
+            split[k, rows, :] = part
+            store_factor(n, k).start()
+
+    def store_factor(n, k):
+        rows = slice(n * share, (n + 1) * share)
+        first = k * factor.shape[0] + n * share
+        return pltpu.make_async_copy(
+            split.at[k, rows], factor_out.at[first : first + share], split_sems.at[n, k]
+        )
 
     pattern_copy.wait()
     for r in range(rounds):
@@ -105,14 +126,21 @@
             if i + 1 < high:
                 prepare(i + 1)
             step(i)
+            if i == late:
+                factor_copy.wait()
+            if i >= late:
+                split_factor(i - late)
         store(r).start()
     upd_copy.wait()
     w[...] = -product(tall(upd[...]), solved[...])
     for r in range(rounds):
         store(r).wait()
-
-
-def solve_subtree(rhs, dinv, off, pattern, upd):
+    for n in range(count - late):
+        for k in range(2):
+            store_factor(n, k).wait()
+
+
+def solve_subtree(rhs, dinv, off, pattern, upd, factor, rows):
     count = dinv.shape[0]
     bounds = [0, count // 6, count // 2, count]
     return pl.pallas_call(
@@ -120,9 +148,10 @@
         out_shape=(
             jax.ShapeDtypeStruct(rhs.shape, F32),
             jax.ShapeDtypeStruct((upd.shape[0], rhs.shape[1]), F32),
+            pltpu.HBM((2 * rows, factor.shape[1]), BF16),
         ),
-        in_specs=[HBM] * 5,
-        out_specs=(HBM, VMEM),
+        in_specs=[HBM] * 6,
+        out_specs=(HBM, VMEM, HBM),
         scratch_shapes=[
             pltpu.SMEM(pattern.shape, jnp.int32),
             pltpu.VMEM(rhs.shape, F32),
@@ -133,13 +162,16 @@
             pltpu.VMEM((count, 2 * B, 2 * B), BF16),
             pltpu.VMEM((count, B, B), F32),
             pltpu.VMEM((count * B, 2 * B), BF16),
+            pltpu.VMEM((rows, factor.shape[1]), F32),
+            pltpu.VMEM((2, rows, factor.shape[1]), BF16),
             pltpu.SemaphoreType.DMA((len(bounds) - 1, 4)),
-            pltpu.SemaphoreType.DMA((2,)),
+            pltpu.SemaphoreType.DMA((3,)),
+            pltpu.SemaphoreType.DMA((count // 3, 2)),
         ],
-        compiler_params=pltpu.CompilerParams(vmem_limit_bytes=32 * MIB),
+        compiler_params=pltpu.CompilerParams(vmem_limit_bytes=40 * MIB),
         cost_estimate=pl.CostEstimate(flops=10**6, bytes_accessed=10**5, transcendentals=0),
         name="subtree",
-    )(*[in_hbm(x) for x in (pattern, rhs, dinv, off, upd)])
+    )(*[in_hbm(x) for x in (pattern, rhs, dinv, off, upd, factor)])
 
 
 def exchange(x, mask):
@@ -161,7 +193,7 @@
             arrays[n] = (arrays[n][0], through(arrays[n][1]))
         arrays.append((0, x))
     else:
-        arrays.append((0, throughs[0](x)))
+        arrays.append((0, throughs[0](x) if throughs else x))
     arrays += [(mask ^ 1, exchange(array, 1)) for mask, array in arrays]
     return [(array, [mask ^ high for high in masks]) for mask, array in arrays]
 
@@ -432,8 +464,10 @@
     sizes = [p_size // group for group in groups]
     rhs = Rhs(front_rhs, p_size, groups)
 
-    flat, update = solve_subtree(sub_rhs, sub_dinv, sub_off, sub_pattern.T, sub_update)
     kept = {}
+    flat, update, kept["pivots"] = solve_subtree(
+        sub_rhs, sub_dinv, sub_off, sub_pattern.T, sub_update, piv_inverse, sizes[0]
+    )
 
     def keep(name, factor, block):
         def through(x):
@@ -443,8 +477,8 @@
 
         return through
 
-    pieces = spread(update, front_size, keep("pivots", piv_inverse, (0, sizes[0])))
-    rhs.next_level(update)
+    pieces = spread(update, front_size)
+    rhs.next_level(pieces[0][0])
     maps, map_offset, child_span = sub_map.T, 0, 0
     earlier = []
     for level in range(1, level_count + 1):

time: 143 us -> 141 us (0.986)
  waiting for transfers between devices: 44.2 us -> 47.3 us
  starting transfers between devices: 57.3 us -> 55.1 us
  local copies, waits for them, and re-layouts: 5.95 us -> 3.93 us
    ppermute x73, waiting for transfers between devices: 44.2 us -> 47.3 us  [exchange(): lax.ppermute(x, AXES, [(source, source ^ mask) for source in range(size)])]
    pallas_call x7 -> x6, Pallas kernels: 12.3 us -> 9.92 us  [prepare_factor(): pl.pallas_call(functools.partial(factor_kernel, block), out_shape=(jax.Sh...]
    ppermute x73, starting transfers between devices: 57.3 us -> 55.1 us  [exchange(): lax.ppermute(x, AXES, [(source, source ^ mask) for source in range(size)])]
    unnamed x15 -> x13, local copies, waits for them, and re-layouts: 5.95 us -> 3.93 us
    pallas_call x1, Pallas kernels: 8.48 us -> 9.92 us  [solve_subtree(): pl.pallas_call(functools.partial(subtree_kernel, bounds), out_shape=(jax....]
where the time goes in v4:
time: 141 us
  starting transfers between devices  55.1 us (39%)
  waiting for transfers between devices  47.3 us (34%)
  Pallas kernels  33.4 us (24%)
  local copies, waits for them, and re-layouts  3.93 us (3%)
    ppermute x73, starting transfers between devices, exchange(): lax.ppermute(x, AXES, [(source, source ^ mask) for source in range(size)])  55.1 us
    ppermute x73, waiting for transfers between devices, exchange(): lax.ppermute(x, AXES, [(source, source ^ mask) for source in range(size)])  47.3 us
    pallas_call x1, Pallas kernels, solve_subtree(): pl.pallas_call(functools.partial(subtree_kernel, bounds), out_shape=(jax....  9.92 us
    pallas_call x6, Pallas kernels, prepare_factor(): pl.pallas_call(functools.partial(factor_kernel, block), out_shape=(jax.Sh...  9.92 us
    pallas_call x4, Pallas kernels, solve_pivots(): pl.pallas_call(functools.partial(pivot_kernel, [masks for _, masks in pie...  8.67 us
    unnamed x13, local copies, waits for them, and re-layouts  3.93 us
    pallas_call x3, Pallas kernels, solve_update(): pl.pallas_call(functools.partial(update_kernel, [masks for _, masks in pi...  2.98 us
  transfers between devices with their start and end apart: 73, of which 40 were waited for; matrix products, arithmetic and copies ran while one was open for 0% of the time, Pallas kernels for 19%

profile of v4, /device:TPU:0, one launch (start us, length us, event | category | flops | bytes accessed | tf_op | source)
XLA Modules:
  0.0 140.6 jit_solution(9575185693165340155)
XLA Ops:
  0.6 3.0 %collective-permute-start.3 = (f32[960,128]{1,0:T(8,128)}, f32[960,128]{1,0:T(8,128)S(1)}, u32[]{:S(2)}, u32[]{:S(2)}) collective-permute-start(f32[960,128]{1,0:T(8,128)} %refs_0_.1), channel_id=1, source_target_pairs={{0,2},{1,3},{2,0},{3,1},{4,6},{5,7},{6,4},{7,5},{8,10},{9,11},{10,... | collective-permute-start | bytes 1474568 | tf_op jit(solution)/shard_map/ppermute | solution.py:179
  3.6 9.9 %subtree.1 = (f32[3072,128]{1,0:T(8,128)}, f32[256,128]{1,0:T(8,128)S(1)}, bf16[1024,2048]{1,0:T(8,128)(2,1)}) custom-call(s32[2,23]{1,0:T(2,128)} %bitcast.8, f32[3072,128]{1,0:T(8,128)} %rhs_in.1, f32[24,128,128]{2,1,0:T(8,128)} %dinv_in.1, f32[23,2,128,128]{3,2,1,0:T(8,128)} %off_in.1, f32[256,3072]{1,0:T(8,128)} %upd_in.1, f32[960,2048]{1,0:T(8,128)} %factor.23), custom_call_target="tpu_custom_call" | custom-call | flops 1000000 | bytes 100000 | tf_op jit(solution)/shard_map/subtree/pallas_call | solution.py:146
  13.7 4.9 %collective-permute-done.after.refs_0_ = f32[256,128]{1,0:T(8,128)S(1)} collective-permute-done((f32[256,128]{1,0:T(8,128)S(1)}, f32[256,128]{1,0:T(8,128)S(1)}, u32[]{:S(2)}, u32[]{:S(2)}) %collective-permute-start) | collective-permute-done | bytes 131104 | tf_op jit(solution)/shard_map/ppermute | solution.py:179
  19.3 1.5 %collective-permute-done.2.refs_3_ = f32[256,128]{1,0:T(8,128)S(1)} collective-permute-done((f32[256,128]{1,0:T(8,128)S(1)}, f32[256,128]{1,0:T(8,128)S(1)}, u32[]{:S(2)}, u32[]{:S(2)}) %collective-permute-start.2) | collective-permute-done | bytes 131104 | tf_op jit(solution)/shard_map/ppermute | solution.py:179
  21.0 2.2 %copy-done = bf16[1024,2048]{1,0:T(8,128)(2,1)S(1)} copy-done((bf16[1024,2048]{1,0:T(8,128)(2,1)S(1)}, bf16[1024,2048]{1,0:T(8,128)(2,1)}, u32[]{:S(2)}) %copy-start) | copy-done | bytes 4194328
  23.2 2.0 %pivots.4 = (f32[512,128]{1,0:T(8,128)S(1)}, f32[512,128]{1,0:T(8,128)S(1)}) custom-call(s32[1]{0:T(128)} %bitcast.1.me, s32[2,32]{1,0:T(2,128)S(1)} %bitcast.7, f32[256,128]{1,0:T(8,128)S(1)} %collective-permute-done.after.refs_0_, f32[256,128]{1,0:T(8,128)S(1)} %get-tuple-element.28.refs_1_, f32[256,128]{1,0:T(8,128)S(1)} %collective-permute-done.1.refs_2_, ...), custom_call_target="tpu_custom_call" | custom-call | flops 805306368 | bytes 8000000 | tf_op jit(solution)/shard_map/pivots/pallas_call | solution.py:331
  25.2 1.1 collective-permute-start.5
  26.3 1.5 %collective-permute-start.15 = (f32[768,128]{1,0:T(8,128)S(1)}, f32[768,128]{1,0:T(8,128)S(1)}, u32[]{:S(2)}, u32[]{:S(2)}) collective-permute-start(f32[768,128]{1,0:T(8,128)S(1)} %get-tuple-element.36.refs_0_), channel_id=1, source_target_pairs={{0,4},{1,5},{2,6},{3,7},{4,0},{5,1},{6,2},{7,3},{8,12},{9,13},{10,... | collective-permute-start | bytes 1179656 | tf_op jit(solution)/shard_map/ppermute | solution.py:179
  27.8 2.3 %factor.12 = (bf16[1024,2048]{1,0:T(8,128)(2,1)S(1)}, f32[512,128]{1,0:T(8,128)S(1)}) custom-call(f32[896,2048]{1,0:T(8,128)} %factor.21, f32[512,128]{1,0:T(8,128)S(1)} %get-tuple-element.31.own.refs_33_), custom_call_target="tpu_custom_call" | custom-call | bytes 8388608 | tf_op jit(solution)/shard_map/factor/pallas_call | solution.py:222
  30.3 3.4 %collective-permute-done.5.refs_0_ = f32[512,128]{1,0:T(8,128)S(1)} collective-permute-done((f32[512,128]{1,0:T(8,128)S(1)}, f32[512,128]{1,0:T(8,128)S(1)}, u32[]{:S(2)}, u32[]{:S(2)}) %collective-permute-start.5) | collective-permute-done | bytes 262176 | tf_op jit(solution)/shard_map/ppermute | solution.py:179
  33.7 1.5 %collective-permute-done.6.refs_2_ = f32[512,128]{1,0:T(8,128)S(1)} collective-permute-done((f32[512,128]{1,0:T(8,128)S(1)}, f32[512,128]{1,0:T(8,128)S(1)}, u32[]{:S(2)}, u32[]{:S(2)}) %collective-permute-start.6) | collective-permute-done | bytes 262176 | tf_op jit(solution)/shard_map/ppermute | solution.py:179
  35.2 1.5 %update.3.after.refs_3_ = f32[512,128]{1,0:T(8,128)S(1)} custom-call(s32[1]{0:T(128)} %bitcast.1.me, f32[512,128]{1,0:T(8,128)S(1)} %collective-permute-done.5.refs_0_, f32[512,128]{1,0:T(8,128)S(1)} %get-tuple-element.32.refs_1_, f32[512,128]{1,0:T(8,128)S(1)} %collective-permute-done.6.refs_2_, f32[512,128]{1,0:T(8,128)S(1)} %collective-permute-done.7.refs_3_, ...), custom_call_target="tpu_custom_call" | custom-call | flops 805306368 | bytes 8000000 | tf_op jit(solution)/shard_map/update/pallas_call | solution.py:366
  36.7 2.0 %collective-permute-start.8 = (f32[512,128]{1,0:T(8,128)S(1)}, f32[512,128]{1,0:T(8,128)S(1)}, u32[]{:S(2)}, u32[]{:S(2)}) collective-permute-start(f32[512,128]{1,0:T(8,128)S(1)} %update.3.after.refs_3_), channel_id=1, source_target_pairs={{0,6},{1,7},{2,4},{3,5},{4,2},{5,3},{6,0},{7,1},{8,14},{9,15},{10,... | collective-permute-start | bytes 786440 | tf_op jit(solution)/shard_map/ppermute | solution.py:179
  39.2 1.0 collective-permute-start.10
  40.2 0.8 join.5
  41.5 5.3 %collective-permute-done.8.own = f32[512,128]{1,0:T(8,128)S(1)} collective-permute-done((f32[512,128]{1,0:T(8,128)S(1)}, f32[512,128]{1,0:T(8,128)S(1)}, u32[]{:S(2)}, u32[]{:S(2)}) %collective-permute-start.8) | collective-permute-done | bytes 262176 | tf_op jit(solution)/shard_map/ppermute | solution.py:179
  46.9 2.6 %collective-permute-start.17 = (f32[64,128]{1,0:T(8,128)S(1)}, f32[64,128]{1,0:T(8,128)S(1)}, u32[]{:S(2)}, u32[]{:S(2)}) collective-permute-start(f32[64,128]{1,0:T(8,128)S(1)} %slice.3.refs_0_), channel_id=1, source_target_pairs={{0,16},{1,17},{2,18},{3,19},{4,20},{5,21},{6,22},{7,23},{8,24},{9,... | collective-permute-start | bytes 98312 | tf_op jit(solution)/shard_map/ppermute | solution.py:179
  49.4 2.3 %factor.14 = (bf16[512,2048]{1,0:T(8,128)(2,1)S(1)}, f32[512,128]{1,0:T(8,128)}) custom-call(f32[960,2048]{1,0:T(8,128)} %factor.23, f32[512,128]{1,0:T(8,128)S(1)} %collective-permute-done.8.own), custom_call_target="tpu_custom_call" | custom-call | bytes 4194304 | tf_op jit(solution)/shard_map/factor/pallas_call | solution.py:222
  53.3 1.6 %collective-permute-start.40 = (f32[512,128]{1,0:T(8,128)}, f32[512,128]{1,0:T(8,128)}, u32[]{:S(2)}, u32[]{:S(2)}) collective-permute-start(f32[512,128]{1,0:T(8,128)} %get-tuple-element.44.refs_0_), channel_id=1, source_target_pairs={{0,8},{1,9},{2,10},{3,11},{4,12},{5,13},{6,14},{7,15},{8,0},{9,1},... | collective-permute-start | bytes 786440 | tf_op jit(solution)/shard_map/ppermute | solution.py:179
  55.0 0.9 copy-done.3
  55.9 2.6 %pivots.5 = (f32[256,128]{1,0:T(8,128)S(1)}, f32[256,128]{1,0:T(8,128)S(1)}) custom-call(s32[1]{0:T(128)} %bitcast.1.me, s32[16,14]{1,0:T(8,128)S(1)} %bitcast.4, f32[512,128]{1,0:T(8,128)} %get-tuple-element.35.refs_0_, f32[512,128]{1,0:T(8,128)S(1)} %collective-permute-done.9.refs_1_, f32[512,128]{1,0:T(8,128)} %collective-permute-done.10.refs_2_, ...), custom_call_target="tpu_custom_call" | custom-call | flops 402653184 | bytes 8000000 | tf_op jit(solution)/shard_map/pivots/pallas_call | solution.py:331
  58.5 2.0 %collective-permute-start.18 = (f32[256,128]{1,0:T(8,128)S(1)}, f32[256,128]{1,0:T(8,128)S(1)}, u32[]{:S(2)}, u32[]{:S(2)}) collective-permute-start(f32[256,128]{1,0:T(8,128)S(1)} %get-tuple-element.39.refs_3_.after.refs_34_), channel_id=1, source_target_pairs={{0,6},{1,7},{2,4},{3,5},{4,2},{5,3},{6,0},{7,1},{8,14},{9,15},{10,... | collective-permute-start | bytes 393224 | tf_op jit(solution)/shard_map/ppermute | solution.py:179
  61.1 1.0 collective-permute-start.20
  62.1 3.8 %collective-permute-done.18.own = f32[256,128]{1,0:T(8,128)S(1)} collective-permute-done((f32[256,128]{1,0:T(8,128)S(1)}, f32[256,128]{1,0:T(8,128)S(1)}, u32[]{:S(2)}, u32[]{:S(2)}) %collective-permute-start.18) | collective-permute-done | bytes 131104 | tf_op jit(solution)/shard_map/ppermute | solution.py:179
  65.8 1.6 %factor.16 = (bf16[512,2048]{1,0:T(8,128)(2,1)S(1)}, f32[256,128]{1,0:T(8,128)S(1)}) custom-call(f32[896,2048]{1,0:T(8,128)} %factor.21, f32[256,128]{1,0:T(8,128)S(1)} %collective-permute-done.18.own), custom_call_target="tpu_custom_call" | custom-call | bytes 4194304 | tf_op jit(solution)/shard_map/factor/pallas_call | solution.py:222
  68.4 1.1 join.7.refs_16_
  69.7 0.9 update.4.refs_7_
  70.7 2.7 %collective-permute-start.25 = (f32[256,128]{1,0:T(8,128)S(1)}, f32[256,128]{1,0:T(8,128)S(1)}, u32[]{:S(2)}, u32[]{:S(2)}) collective-permute-start(f32[256,128]{1,0:T(8,128)S(1)} %update.4.refs_7_), channel_id=1, source_target_pairs={{0,14},{1,15},{2,12},{3,13},{4,10},{5,11},{6,8},{7,9},{8,6},{9,7},... | collective-permute-start | bytes 393224 | tf_op jit(solution)/shard_map/ppermute | solution.py:179
  74.1 1.6 %collective-permute-start.27 = (f32[256,128]{1,0:T(8,128)S(1)}, f32[256,128]{1,0:T(8,128)S(1)}, u32[]{:S(2)}, u32[]{:S(2)}) collective-permute-start(f32[256,128]{1,0:T(8,128)S(1)} %update.4.refs_7_), channel_id=1, source_target_pairs={{0,10},{1,11},{2,8},{3,9},{4,14},{5,15},{6,12},{7,13},{8,2},{9,3},... | collective-permute-start | bytes 393224 | tf_op jit(solution)/shard_map/ppermute | solution.py:179
  75.7 0.8 collective-permute-start.28
  76.6 2.7 %collective-permute-done.25.own = f32[256,128]{1,0:T(8,128)S(1)} collective-permute-done((f32[256,128]{1,0:T(8,128)S(1)}, f32[256,128]{1,0:T(8,128)S(1)}, u32[]{:S(2)}, u32[]{:S(2)}) %collective-permute-start.25) | collective-permute-done | bytes 131104 | tf_op jit(solution)/shard_map/ppermute | solution.py:179
  79.3 2.0 %collective-permute-start.29 = (f32[256,128]{1,0:T(8,128)S(1)}, f32[256,128]{1,0:T(8,128)S(1)}, u32[]{:S(2)}, u32[]{:S(2)}) collective-permute-start(f32[256,128]{1,0:T(8,128)S(1)} %update.4.refs_7_), channel_id=1, source_target_pairs={{0,6},{1,7},{2,4},{3,5},{4,2},{5,3},{6,0},{7,1},{8,14},{9,15},{10,... | collective-permute-start | bytes 393224 | tf_op jit(solution)/shard_map/ppermute | solution.py:179
  81.6 1.4 %collective-permute-start.30 = (f32[256,128]{1,0:T(8,128)S(1)}, f32[256,128]{1,0:T(8,128)S(1)}, u32[]{:S(2)}, u32[]{:S(2)}) collective-permute-start(f32[256,128]{1,0:T(8,128)S(1)} %update.4.refs_7_), channel_id=1, source_target_pairs={{0,4},{1,5},{2,6},{3,7},{4,0},{5,1},{6,2},{7,3},{8,12},{9,13},{10,... | collective-permute-start | bytes 393224 | tf_op jit(solution)/shard_map/ppermute | solution.py:179
  83.0 1.8 %collective-permute-done.27.refs_2_ = f32[256,128]{1,0:T(8,128)S(1)} collective-permute-done((f32[256,128]{1,0:T(8,128)S(1)}, f32[256,128]{1,0:T(8,128)S(1)}, u32[]{:S(2)}, u32[]{:S(2)}) %collective-permute-start.27) | collective-permute-done | bytes 131104 | tf_op jit(solution)/shard_map/ppermute | solution.py:179
  84.9 1.0 collective-permute-start.31
  86.4 1.3 factor.18
  88.3 1.5 %collective-permute-done.31.refs_6_ = f32[256,128]{1,0:T(8,128)S(1)} collective-permute-done((f32[256,128]{1,0:T(8,128)S(1)}, f32[256,128]{1,0:T(8,128)S(1)}, u32[]{:S(2)}, u32[]{:S(2)}) %collective-permute-start.31) | collective-permute-done | bytes 131104 | tf_op jit(solution)/shard_map/ppermute | solution.py:179
  92.2 1.6 %pivots.6 = (f32[256,128]{1,0:T(8,128)S(1)}, f32[128,128]{1,0:T(8,128)S(1)}) custom-call(s32[1]{0:T(128)} %bitcast.1.me, s32[16,14]{1,0:T(8,128)S(1)} %bitcast.5, f32[256,128]{1,0:T(8,128)S(1)} %get-tuple-element.43.refs_0_, f32[256,128]{1,0:T(8,128)S(1)} %collective-permute-done.26.refs_1_, f32[256,128]{1,0:T(8,128)S(1)} %collective-permute-done.27.refs_2_, ...), custom_call_target="tpu_custom_call" | custom-call | flops 201326592 | bytes 8000000 | tf_op jit(solution)/shard_map/pivots/pallas_call | solution.py:331
  93.8 1.7 %collective-permute-start.42 = (f32[256,128]{1,0:T(8,128)S(1)}, f32[256,128]{1,0:T(8,128)S(1)}, u32[]{:S(2)}, u32[]{:S(2)}) collective-permute-start(f32[256,128]{1,0:T(8,128)S(1)} %get-tuple-element.46.refs_7_.refs_23_.refs_35_), channel_id=1, source_target_pairs={{0,14},{1,15},{2,12},{3,13},{4,10},{5,11},{6,8},{7,9},{8,6},{9,7},... | collective-permute-start | bytes 393224 | tf_op jit(solution)/shard_map/ppermute | solution.py:179
  95.6 1.7 %collective-permute-start.43 = (f32[256,128]{1,0:T(8,128)S(1)}, f32[256,128]{1,0:T(8,128)S(1)}, u32[]{:S(2)}, u32[]{:S(2)}) collective-permute-start(f32[256,128]{1,0:T(8,128)S(1)} %get-tuple-element.46.refs_7_.refs_23_.refs_35_), channel_id=1, source_target_pairs={{0,12},{1,13},{2,14},{3,15},{4,8},{5,9},{6,10},{7,11},{8,4},{9,5},... | collective-permute-start | bytes 393224 | tf_op jit(solution)/shard_map/ppermute | solution.py:179
  97.3 1.6 %collective-permute-start.44 = (f32[256,128]{1,0:T(8,128)S(1)}, f32[256,128]{1,0:T(8,128)S(1)}, u32[]{:S(2)}, u32[]{:S(2)}) collective-permute-start(f32[256,128]{1,0:T(8,128)S(1)} %get-tuple-element.46.refs_7_.refs_23_.refs_35_), channel_id=1, source_target_pairs={{0,10},{1,11},{2,8},{3,9},{4,14},{5,15},{6,12},{7,13},{8,2},{9,3},... | collective-permute-start | bytes 393224 | tf_op jit(solution)/shard_map/ppermute | solution.py:179
  98.9 0.8 collective-permute-start.45
  99.8 1.0 collective-permute-start.46
  100.8 1.7 %collective-permute-done.42.own = f32[256,128]{1,0:T(8,128)S(1)} collective-permute-done((f32[256,128]{1,0:T(8,128)S(1)}, f32[256,128]{1,0:T(8,128)S(1)}, u32[]{:S(2)}, u32[]{:S(2)}) %collective-permute-start.42) | collective-permute-done | bytes 131104 | tf_op jit(solution)/shard_map/ppermute | solution.py:179
  103.1 1.3 factor.20
  104.4 1.3 collective-permute-done.43.own
  105.7 1.0 collective-permute-start.48
  106.7 1.1 factor.22
  108.0 0.8 collective-permute-done.45.refs_3_.refs_19_
  109.7 0.9 collective-permute-done.48.refs_6_.refs_22_
  113.3 2.6 %collective-permute-start.57 = (f32[128,128]{1,0:T(8,128)S(1)}, f32[128,128]{1,0:T(8,128)S(1)}, u32[]{:S(2)}, u32[]{:S(2)}) collective-permute-start(f32[128,128]{1,0:T(8,128)S(1)} %update.5), channel_id=1, source_target_pairs={{0,16},{1,17},{2,18},{3,19},{4,20},{5,21},{6,22},{7,23},{8,24},{9,... | collective-permute-start | bytes 196616 | tf_op jit(solution)/shard_map/ppermute | solution.py:179
  115.9 4.1 %collective-permute-done.57 = f32[128,128]{1,0:T(8,128)S(1)} collective-permute-done((f32[128,128]{1,0:T(8,128)S(1)}, f32[128,128]{1,0:T(8,128)S(1)}, u32[]{:S(2)}, u32[]{:S(2)}) %collective-permute-start.57) | collective-permute-done | bytes 65568 | tf_op jit(solution)/shard_map/ppermute | solution.py:179
  120.0 1.3 collective-permute-start.58
  121.4 2.1 %collective-permute-start.59 = (f32[256,128]{1,0:T(8,128)S(1)}, f32[256,128]{1,0:T(8,128)S(1)}, u32[]{:S(2)}, u32[]{:S(2)}) collective-permute-start(f32[256,128]{1,0:T(8,128)S(1)} %pad_maximum_fusion.refs_7_), channel_id=1, source_target_pairs={{0,12},{1,13},{2,14},{3,15},{4,8},{5,9},{6,10},{7,11},{8,4},{9,5},... | collective-permute-start | bytes 393224 | tf_op jit(solution)/shard_map/ppermute | solution.py:179
  123.5 0.8 collective-permute-start.60
  124.3 1.7 %collective-permute-start.61 = (f32[256,128]{1,0:T(8,128)S(1)}, f32[256,128]{1,0:T(8,128)S(1)}, u32[]{:S(2)}, u32[]{:S(2)}) collective-permute-start(f32[256,128]{1,0:T(8,128)S(1)} %pad_maximum_fusion.refs_7_), channel_id=1, source_target_pairs={{0,8},{1,9},{2,10},{3,11},{4,12},{5,13},{6,14},{7,15},{8,0},{9,1},... | collective-permute-start | bytes 393224 | tf_op jit(solution)/shard_map/ppermute | solution.py:179
  125.9 1.5 %collective-permute-start.62 = (f32[256,128]{1,0:T(8,128)S(1)}, f32[256,128]{1,0:T(8,128)S(1)}, u32[]{:S(2)}, u32[]{:S(2)}) collective-permute-start(f32[256,128]{1,0:T(8,128)S(1)} %pad_maximum_fusion.refs_7_), channel_id=1, source_target_pairs={{0,6},{1,7},{2,4},{3,5},{4,2},{5,3},{6,0},{7,1},{8,14},{9,15},{10,... | collective-permute-start | bytes 393224 | tf_op jit(solution)/shard_map/ppermute | solution.py:179
  127.4 1.4 collective-permute-done.58.refs_0_
  128.8 1.1 collective-permute-start.63
  129.8 1.2 collective-permute-done.59.refs_1_
  131.0 1.0 collective-permute-start.64
  132.0 1.4 collective-permute-done.60.refs_2_
  133.4 0.9 collective-permute-done.61.refs_3_
  138.2 2.4 %pivots.7 = f32[960,128]{1,0:T(8,128)} custom-call(s32[1]{0:T(128)} %bitcast.1.me, s32[16,14]{1,0:T(8,128)S(1)} %bitcast.6, f32[256,128]{1,0:T(8,128)S(1)} %collective-permute-done.58.refs_0_, f32[256,128]{1,0:T(8,128)S(1)} %collective-permute-done.59.refs_1_, f32[256,128]{1,0:T(8,128)S(1)} %collective-permute-done.60.refs_2_, ...), custom_call_target="tpu_custom_call" | custom-call | flops 100663296 | bytes 8000000 | tf_op jit(solution)/shard_map/pivots/pallas_call | solution.py:331
  (115 shorter events, 18.0 us)
Async XLA Ops:
  0.6 18.0 %collective-permute-start.3 = (f32[960,128]{1,0:T(8,128)}, f32[960,128]{1,0:T(8,128)S(1)}, u32[]{:S(2)}, u32[]{:S(2)}) collective-permute-start(f32[960,128]{1,0:T(8,128)} %refs_0_.1), channel_id=1, source_target_pairs={{0,2},{1,3},{2,0},{3,1},{4,6},{5,7},{6,4},{7,5},{8,10},{9,11},{10,... | collective-permute-start | bytes 1474568 | tf_op jit(solution)/shard_map/ppermute | solution.py:179
  13.6 5.0 %collective-permute-start = (f32[256,128]{1,0:T(8,128)S(1)}, f32[256,128]{1,0:T(8,128)S(1)}, u32[]{:S(2)}, u32[]{:S(2)}) collective-permute-start(f32[256,128]{1,0:T(8,128)S(1)} %get-tuple-element.28.refs_1_), channel_id=1, source_target_pairs={{0,2},{1,3},{2,0},{3,1},{4,6},{5,7},{6,4},{7,5},{8,10},{9,11},{10,... | collective-permute-start | bytes 393224 | tf_op jit(solution)/shard_map/ppermute | solution.py:179
  18.7 2.4 %collective-permute-start.4 = (f32[1024,128]{1,0:T(8,128)S(1)}, f32[1024,128]{1,0:T(8,128)S(1)}, u32[]{:S(2)}, u32[]{:S(2)}) collective-permute-start(f32[1024,128]{1,0:T(8,128)S(1)} %get-tuple-element.29.refs_4_), channel_id=1, source_target_pairs={{0,1},{1,0},{2,3},{3,2},{4,5},{5,4},{6,7},{7,6},{8,9},{9,8},{10,11... | collective-permute-start | bytes 1572872 | tf_op jit(solution)/shard_map/ppermute | solution.py:179
  18.8 2.1 %collective-permute-start.2 = (f32[256,128]{1,0:T(8,128)S(1)}, f32[256,128]{1,0:T(8,128)S(1)}, u32[]{:S(2)}, u32[]{:S(2)}) collective-permute-start(f32[256,128]{1,0:T(8,128)S(1)} %get-tuple-element.28.refs_1_), channel_id=1, source_target_pairs={{0,1},{1,0},{2,3},{3,2},{4,5},{5,4},{6,7},{7,6},{8,9},{9,8},{10,11... | collective-permute-start | bytes 393224 | tf_op jit(solution)/shard_map/ppermute | solution.py:179
  19.3 1.8 %collective-permute-start.1 = (f32[256,128]{1,0:T(8,128)S(1)}, f32[256,128]{1,0:T(8,128)S(1)}, u32[]{:S(2)}, u32[]{:S(2)}) collective-permute-start(f32[256,128]{1,0:T(8,128)S(1)} %collective-permute-done.after.refs_0_), channel_id=1, source_target_pairs={{0,1},{1,0},{2,3},{3,2},{4,5},{5,4},{6,7},{7,6},{8,9},{9,8},{10,11... | collective-permute-start | bytes 393224 | tf_op jit(solution)/shard_map/ppermute | solution.py:179
  25.2 8.4 %collective-permute-start.5 = (f32[512,128]{1,0:T(8,128)S(1)}, f32[512,128]{1,0:T(8,128)S(1)}, u32[]{:S(2)}, u32[]{:S(2)}) collective-permute-start(f32[512,128]{1,0:T(8,128)S(1)} %get-tuple-element.31.own.refs_33_), channel_id=1, source_target_pairs={{0,2},{1,3},{2,0},{3,1},{4,6},{5,7},{6,4},{7,5},{8,10},{9,11},{10,... | collective-permute-start | bytes 786440 | tf_op jit(solution)/shard_map/ppermute | solution.py:179
  26.3 13.9 %collective-permute-start.15 = (f32[768,128]{1,0:T(8,128)S(1)}, f32[768,128]{1,0:T(8,128)S(1)}, u32[]{:S(2)}, u32[]{:S(2)}) collective-permute-start(f32[768,128]{1,0:T(8,128)S(1)} %get-tuple-element.36.refs_0_), channel_id=1, source_target_pairs={{0,4},{1,5},{2,6},{3,7},{4,0},{5,1},{6,2},{7,3},{8,12},{9,13},{10,... | collective-permute-start | bytes 1179656 | tf_op jit(solution)/shard_map/ppermute | solution.py:179
  30.2 3.5 %collective-permute-start.7 = (f32[512,128]{1,0:T(8,128)S(1)}, f32[512,128]{1,0:T(8,128)S(1)}, u32[]{:S(2)}, u32[]{:S(2)}) collective-permute-start(f32[512,128]{1,0:T(8,128)S(1)} %get-tuple-element.32.refs_1_), channel_id=1, source_target_pairs={{0,1},{1,0},{2,3},{3,2},{4,5},{5,4},{6,7},{7,6},{8,9},{9,8},{10,11... | collective-permute-start | bytes 786440 | tf_op jit(solution)/shard_map/ppermute | solution.py:179
  33.7 1.5 %collective-permute-start.6 = (f32[512,128]{1,0:T(8,128)S(1)}, f32[512,128]{1,0:T(8,128)S(1)}, u32[]{:S(2)}, u32[]{:S(2)}) collective-permute-start(f32[512,128]{1,0:T(8,128)S(1)} %collective-permute-done.5.refs_0_), channel_id=1, source_target_pairs={{0,1},{1,0},{2,3},{3,2},{4,5},{5,4},{6,7},{7,6},{8,9},{9,8},{10,11... | collective-permute-start | bytes 786440 | tf_op jit(solution)/shard_map/ppermute | solution.py:179
  36.7 10.2 %collective-permute-start.8 = (f32[512,128]{1,0:T(8,128)S(1)}, f32[512,128]{1,0:T(8,128)S(1)}, u32[]{:S(2)}, u32[]{:S(2)}) collective-permute-start(f32[512,128]{1,0:T(8,128)S(1)} %update.3.after.refs_3_), channel_id=1, source_target_pairs={{0,6},{1,7},{2,4},{3,5},{4,2},{5,3},{6,0},{7,1},{8,14},{9,15},{10,... | collective-permute-start | bytes 786440 | tf_op jit(solution)/shard_map/ppermute | solution.py:179
  38.7 13.3 %collective-permute-start.9 = (f32[512,128]{1,0:T(8,128)S(1)}, f32[512,128]{1,0:T(8,128)S(1)}, u32[]{:S(2)}, u32[]{:S(2)}) collective-permute-start(f32[512,128]{1,0:T(8,128)S(1)} %update.3.after.refs_3_), channel_id=1, source_target_pairs={{0,4},{1,5},{2,6},{3,7},{4,0},{5,1},{6,2},{7,3},{8,12},{9,13},{10,... | collective-permute-start | bytes 786440 | tf_op jit(solution)/shard_map/ppermute | solution.py:179
  39.2 13.3 %collective-permute-start.10 = (f32[512,128]{1,0:T(8,128)S(1)}, f32[512,128]{1,0:T(8,128)}, u32[]{:S(2)}, u32[]{:S(2)}) collective-permute-start(f32[512,128]{1,0:T(8,128)S(1)} %update.3.after.refs_3_), channel_id=1, source_target_pairs={{0,2},{1,3},{2,0},{3,1},{4,6},{5,7},{6,4},{7,5},{8,10},{9,11},{10,... | collective-permute-start | bytes 786440 | tf_op jit(solution)/shard_map/ppermute | solution.py:179
  41.0 13.9 %collective-permute-start.16 = (f32[1024,128]{1,0:T(8,128)S(1)}, f32[1024,128]{1,0:T(8,128)}, u32[]{:S(2)}, u32[]{:S(2)}) collective-permute-start(f32[1024,128]{1,0:T(8,128)S(1)} %get-tuple-element.37.refs_8_), channel_id=1, source_target_pairs={{0,1},{1,0},{2,3},{3,2},{4,5},{5,4},{6,7},{7,6},{8,9},{9,8},{10,11... | collective-permute-start | bytes 1572872 | tf_op jit(solution)/shard_map/ppermute | solution.py:179
  41.0 11.5 %collective-permute-start.14 = (f32[512,128]{1,0:T(8,128)S(1)}, f32[512,128]{1,0:T(8,128)S(1)}, u32[]{:S(2)}, u32[]{:S(2)}) collective-permute-start(f32[512,128]{1,0:T(8,128)S(1)} %update.3.after.refs_3_), channel_id=1, source_target_pairs={{0,1},{1,0},{2,3},{3,2},{4,5},{5,4},{6,7},{7,6},{8,9},{9,8},{10,11... | collective-permute-start | bytes 786440 | tf_op jit(solution)/shard_map/ppermute | solution.py:179
  46.9 4.9 %collective-permute-start.17 = (f32[64,128]{1,0:T(8,128)S(1)}, f32[64,128]{1,0:T(8,128)S(1)}, u32[]{:S(2)}, u32[]{:S(2)}) collective-permute-start(f32[64,128]{1,0:T(8,128)S(1)} %slice.3.refs_0_), channel_id=1, source_target_pairs={{0,16},{1,17},{2,18},{3,19},{4,20},{5,21},{6,22},{7,23},{8,24},{9,... | collective-permute-start | bytes 98312 | tf_op jit(solution)/shard_map/ppermute | solution.py:179
  51.7 3.2 %collective-permute-start.11 = (f32[512,128]{1,0:T(8,128)}, f32[512,128]{1,0:T(8,128)}, u32[]{:S(2)}, u32[]{:S(2)}) collective-permute-start(f32[512,128]{1,0:T(8,128)} %get-tuple-element.35.refs_0_), channel_id=1, source_target_pairs={{0,1},{1,0},{2,3},{3,2},{4,5},{5,4},{6,7},{7,6},{8,9},{9,8},{10,11... | collective-permute-start | bytes 786440 | tf_op jit(solution)/shard_map/ppermute | solution.py:179
  52.0 3.0 %collective-permute-start.12 = (f32[512,128]{1,0:T(8,128)S(1)}, f32[512,128]{1,0:T(8,128)}, u32[]{:S(2)}, u32[]{:S(2)}) collective-permute-start(f32[512,128]{1,0:T(8,128)S(1)} %collective-permute-done.9.refs_1_), channel_id=1, source_target_pairs={{0,1},{1,0},{2,3},{3,2},{4,5},{5,4},{6,7},{7,6},{8,9},{9,8},{10,11... | collective-permute-start | bytes 786440 | tf_op jit(solution)/shard_map/ppermute | solution.py:179
  52.5 2.5 %collective-permute-start.13 = (f32[512,128]{1,0:T(8,128)}, f32[512,128]{1,0:T(8,128)}, u32[]{:S(2)}, u32[]{:S(2)}) collective-permute-start(f32[512,128]{1,0:T(8,128)} %collective-permute-done.10.refs_2_), channel_id=1, source_target_pairs={{0,1},{1,0},{2,3},{3,2},{4,5},{5,4},{6,7},{7,6},{8,9},{9,8},{10,11... | collective-permute-start | bytes 786440 | tf_op jit(solution)/shard_map/ppermute | solution.py:179
  53.3 15.1 %collective-permute-start.40 = (f32[512,128]{1,0:T(8,128)}, f32[512,128]{1,0:T(8,128)}, u32[]{:S(2)}, u32[]{:S(2)}) collective-permute-start(f32[512,128]{1,0:T(8,128)} %get-tuple-element.44.refs_0_), channel_id=1, source_target_pairs={{0,8},{1,9},{2,10},{3,11},{4,12},{5,13},{6,14},{7,15},{8,0},{9,1},... | collective-permute-start | bytes 786440 | tf_op jit(solution)/shard_map/ppermute | solution.py:179
  58.5 7.3 %collective-permute-start.18 = (f32[256,128]{1,0:T(8,128)S(1)}, f32[256,128]{1,0:T(8,128)S(1)}, u32[]{:S(2)}, u32[]{:S(2)}) collective-permute-start(f32[256,128]{1,0:T(8,128)S(1)} %get-tuple-element.39.refs_3_.after.refs_34_), channel_id=1, source_target_pairs={{0,6},{1,7},{2,4},{3,5},{4,2},{5,3},{6,0},{7,1},{8,14},{9,15},{10,... | collective-permute-start | bytes 393224 | tf_op jit(solution)/shard_map/ppermute | solution.py:179
  60.6 7.3 %collective-permute-start.19 = (f32[256,128]{1,0:T(8,128)S(1)}, f32[256,128]{1,0:T(8,128)S(1)}, u32[]{:S(2)}, u32[]{:S(2)}) collective-permute-start(f32[256,128]{1,0:T(8,128)S(1)} %get-tuple-element.39.refs_3_.after.refs_34_), channel_id=1, source_target_pairs={{0,4},{1,5},{2,6},{3,7},{4,0},{5,1},{6,2},{7,3},{8,12},{9,13},{10,... | collective-permute-start | bytes 393224 | tf_op jit(solution)/shard_map/ppermute | solution.py:179
  61.1 7.0 %collective-permute-start.20 = (f32[256,128]{1,0:T(8,128)S(1)}, f32[256,128]{1,0:T(8,128)S(1)}, u32[]{:S(2)}, u32[]{:S(2)}) collective-permute-start(f32[256,128]{1,0:T(8,128)S(1)} %get-tuple-element.39.refs_3_.after.refs_34_), channel_id=1, source_target_pairs={{0,2},{1,3},{2,0},{3,1},{4,6},{5,7},{6,4},{7,5},{8,10},{9,11},{10,... | collective-permute-start | bytes 393224 | tf_op jit(solution)/shard_map/ppermute | solution.py:179
  62.1 7.6 %collective-permute-start.24 = (f32[256,128]{1,0:T(8,128)S(1)}, f32[256,128]{1,0:T(8,128)S(1)}, u32[]{:S(2)}, u32[]{:S(2)}) collective-permute-start(f32[256,128]{1,0:T(8,128)S(1)} %get-tuple-element.39.refs_3_.after.refs_34_), channel_id=1, source_target_pairs={{0,1},{1,0},{2,3},{3,2},{4,5},{5,4},{6,7},{7,6},{8,9},{9,8},{10,11... | collective-permute-start | bytes 393224 | tf_op jit(solution)/shard_map/ppermute | solution.py:179
  67.5 2.2 %collective-permute-start.21 = (f32[256,128]{1,0:T(8,128)S(1)}, f32[256,128]{1,0:T(8,128)S(1)}, u32[]{:S(2)}, u32[]{:S(2)}) collective-permute-start(f32[256,128]{1,0:T(8,128)S(1)} %get-tuple-element.40.refs_0_), channel_id=1, source_target_pairs={{0,1},{1,0},{2,3},{3,2},{4,5},{5,4},{6,7},{7,6},{8,9},{9,8},{10,11... | collective-permute-start | bytes 393224 | tf_op jit(solution)/shard_map/ppermute | solution.py:179
  67.9 1.9 %collective-permute-start.22 = (f32[256,128]{1,0:T(8,128)S(1)}, f32[256,128]{1,0:T(8,128)S(1)}, u32[]{:S(2)}, u32[]{:S(2)}) collective-permute-start(f32[256,128]{1,0:T(8,128)S(1)} %collective-permute-done.19.refs_1_), channel_id=1, source_target_pairs={{0,1},{1,0},{2,3},{3,2},{4,5},{5,4},{6,7},{7,6},{8,9},{9,8},{10,11... | collective-permute-start | bytes 393224 | tf_op jit(solution)/shard_map/ppermute | solution.py:179
  68.1 1.7 %collective-permute-start.23 = (f32[256,128]{1,0:T(8,128)S(1)}, f32[256,128]{1,0:T(8,128)S(1)}, u32[]{:S(2)}, u32[]{:S(2)}) collective-permute-start(f32[256,128]{1,0:T(8,128)S(1)} %collective-permute-done.20.refs_2_), channel_id=1, source_target_pairs={{0,1},{1,0},{2,3},{3,2},{4,5},{5,4},{6,7},{7,6},{8,9},{9,8},{10,11... | collective-permute-start | bytes 393224 | tf_op jit(solution)/shard_map/ppermute | solution.py:179
  69.5 20.9 %collective-permute-start.41 = (f32[1024,128]{1,0:T(8,128)S(1)}, f32[1024,128]{1,0:T(8,128)S(1)}, u32[]{:S(2)}, u32[]{:S(2)}) collective-permute-start(f32[1024,128]{1,0:T(8,128)S(1)} %join.7.refs_16_), channel_id=1, source_target_pairs={{0,1},{1,0},{2,3},{3,2},{4,5},{5,4},{6,7},{7,6},{8,9},{9,8},{10,11... | collective-permute-start | bytes 1572872 | tf_op jit(solution)/shard_map/ppermute | solution.py:179
  70.7 8.6 %collective-permute-start.25 = (f32[256,128]{1,0:T(8,128)S(1)}, f32[256,128]{1,0:T(8,128)S(1)}, u32[]{:S(2)}, u32[]{:S(2)}) collective-permute-start(f32[256,128]{1,0:T(8,128)S(1)} %update.4.refs_7_), channel_id=1, source_target_pairs={{0,14},{1,15},{2,12},{3,13},{4,10},{5,11},{6,8},{7,9},{8,6},{9,7},... | collective-permute-start | bytes 393224 | tf_op jit(solution)/shard_map/ppermute | solution.py:179
  73.4 8.2 %collective-permute-start.26 = (f32[256,128]{1,0:T(8,128)S(1)}, f32[256,128]{1,0:T(8,128)S(1)}, u32[]{:S(2)}, u32[]{:S(2)}) collective-permute-start(f32[256,128]{1,0:T(8,128)S(1)} %update.4.refs_7_), channel_id=1, source_target_pairs={{0,12},{1,13},{2,14},{3,15},{4,8},{5,9},{6,10},{7,11},{8,4},{9,5},... | collective-permute-start | bytes 393224 | tf_op jit(solution)/shard_map/ppermute | solution.py:179
  74.1 10.8 %collective-permute-start.27 = (f32[256,128]{1,0:T(8,128)S(1)}, f32[256,128]{1,0:T(8,128)S(1)}, u32[]{:S(2)}, u32[]{:S(2)}) collective-permute-start(f32[256,128]{1,0:T(8,128)S(1)} %update.4.refs_7_), channel_id=1, source_target_pairs={{0,10},{1,11},{2,8},{3,9},{4,14},{5,15},{6,12},{7,13},{8,2},{9,3},... | collective-permute-start | bytes 393224 | tf_op jit(solution)/shard_map/ppermute | solution.py:179
  75.7 10.6 %collective-permute-start.28 = (f32[256,128]{1,0:T(8,128)S(1)}, f32[256,128]{1,0:T(8,128)S(1)}, u32[]{:S(2)}, u32[]{:S(2)}) collective-permute-start(f32[256,128]{1,0:T(8,128)S(1)} %update.4.refs_7_), channel_id=1, source_target_pairs={{0,8},{1,9},{2,10},{3,11},{4,12},{5,13},{6,14},{7,15},{8,0},{9,1},... | collective-permute-start | bytes 393224 | tf_op jit(solution)/shard_map/ppermute | solution.py:179
  79.3 8.3 %collective-permute-start.29 = (f32[256,128]{1,0:T(8,128)S(1)}, f32[256,128]{1,0:T(8,128)S(1)}, u32[]{:S(2)}, u32[]{:S(2)}) collective-permute-start(f32[256,128]{1,0:T(8,128)S(1)} %update.4.refs_7_), channel_id=1, source_target_pairs={{0,6},{1,7},{2,4},{3,5},{4,2},{5,3},{6,0},{7,1},{8,14},{9,15},{10,... | collective-permute-start | bytes 393224 | tf_op jit(solution)/shard_map/ppermute | solution.py:179
  81.6 6.6 %collective-permute-start.30 = (f32[256,128]{1,0:T(8,128)S(1)}, f32[256,128]{1,0:T(8,128)S(1)}, u32[]{:S(2)}, u32[]{:S(2)}) collective-permute-start(f32[256,128]{1,0:T(8,128)S(1)} %update.4.refs_7_), channel_id=1, source_target_pairs={{0,4},{1,5},{2,6},{3,7},{4,0},{5,1},{6,2},{7,3},{8,12},{9,13},{10,... | collective-permute-start | bytes 393224 | tf_op jit(solution)/shard_map/ppermute | solution.py:179
  84.9 5.0 %collective-permute-start.31 = (f32[256,128]{1,0:T(8,128)S(1)}, f32[256,128]{1,0:T(8,128)S(1)}, u32[]{:S(2)}, u32[]{:S(2)}) collective-permute-start(f32[256,128]{1,0:T(8,128)S(1)} %update.4.refs_7_), channel_id=1, source_target_pairs={{0,2},{1,3},{2,0},{3,1},{4,6},{5,7},{6,4},{7,5},{8,10},{9,11},{10,... | collective-permute-start | bytes 393224 | tf_op jit(solution)/shard_map/ppermute | solution.py:179
  86.4 3.5 %collective-permute-start.39 = (f32[256,128]{1,0:T(8,128)S(1)}, f32[256,128]{1,0:T(8,128)S(1)}, u32[]{:S(2)}, u32[]{:S(2)}) collective-permute-start(f32[256,128]{1,0:T(8,128)S(1)} %update.4.refs_7_), channel_id=1, source_target_pairs={{0,1},{1,0},{2,3},{3,2},{4,5},{5,4},{6,7},{7,6},{8,9},{9,8},{10,11... | collective-permute-start | bytes 393224 | tf_op jit(solution)/shard_map/ppermute | solution.py:179
  87.6 2.8 %collective-permute-start.32 = (f32[256,128]{1,0:T(8,128)S(1)}, f32[256,128]{1,0:T(8,128)S(1)}, u32[]{:S(2)}, u32[]{:S(2)}) collective-permute-start(f32[256,128]{1,0:T(8,128)S(1)} %get-tuple-element.43.refs_0_), channel_id=1, source_target_pairs={{0,1},{1,0},{2,3},{3,2},{4,5},{5,4},{6,7},{7,6},{8,9},{9,8},{10,11... | collective-permute-start | bytes 393224 | tf_op jit(solution)/shard_map/ppermute | solution.py:179
  88.2 2.7 %collective-permute-start.33 = (f32[256,128]{1,0:T(8,128)S(1)}, f32[256,128]{1,0:T(8,128)S(1)}, u32[]{:S(2)}, u32[]{:S(2)}) collective-permute-start(f32[256,128]{1,0:T(8,128)S(1)} %collective-permute-done.26.refs_1_), channel_id=1, source_target_pairs={{0,1},{1,0},{2,3},{3,2},{4,5},{5,4},{6,7},{7,6},{8,9},{9,8},{10,11... | collective-permute-start | bytes 393224 | tf_op jit(solution)/shard_map/ppermute | solution.py:179
  89.8 1.5 %collective-permute-start.35 = (f32[256,128]{1,0:T(8,128)S(1)}, f32[256,128]{1,0:T(8,128)S(1)}, u32[]{:S(2)}, u32[]{:S(2)}) collective-permute-start(f32[256,128]{1,0:T(8,128)S(1)} %collective-permute-done.28.refs_3_), channel_id=1, source_target_pairs={{0,1},{1,0},{2,3},{3,2},{4,5},{5,4},{6,7},{7,6},{8,9},{9,8},{10,11... | collective-permute-start | bytes 393224 | tf_op jit(solution)/shard_map/ppermute | solution.py:179
  93.8 8.7 %collective-permute-start.42 = (f32[256,128]{1,0:T(8,128)S(1)}, f32[256,128]{1,0:T(8,128)S(1)}, u32[]{:S(2)}, u32[]{:S(2)}) collective-permute-start(f32[256,128]{1,0:T(8,128)S(1)} %get-tuple-element.46.refs_7_.refs_23_.refs_35_), channel_id=1, source_target_pairs={{0,14},{1,15},{2,12},{3,13},{4,10},{5,11},{6,8},{7,9},{8,6},{9,7},... | collective-permute-start | bytes 393224 | tf_op jit(solution)/shard_map/ppermute | solution.py:179
  95.6 10.1 %collective-permute-start.43 = (f32[256,128]{1,0:T(8,128)S(1)}, f32[256,128]{1,0:T(8,128)S(1)}, u32[]{:S(2)}, u32[]{:S(2)}) collective-permute-start(f32[256,128]{1,0:T(8,128)S(1)} %get-tuple-element.46.refs_7_.refs_23_.refs_35_), channel_id=1, source_target_pairs={{0,12},{1,13},{2,14},{3,15},{4,8},{5,9},{6,10},{7,11},{8,4},{9,5},... | collective-permute-start | bytes 393224 | tf_op jit(solution)/shard_map/ppermute | solution.py:179
  97.3 10.6 %collective-permute-start.44 = (f32[256,128]{1,0:T(8,128)S(1)}, f32[256,128]{1,0:T(8,128)S(1)}, u32[]{:S(2)}, u32[]{:S(2)}) collective-permute-start(f32[256,128]{1,0:T(8,128)S(1)} %get-tuple-element.46.refs_7_.refs_23_.refs_35_), channel_id=1, source_target_pairs={{0,10},{1,11},{2,8},{3,9},{4,14},{5,15},{6,12},{7,13},{8,2},{9,3},... | collective-permute-start | bytes 393224 | tf_op jit(solution)/shard_map/ppermute | solution.py:179
  98.9 9.9 %collective-permute-start.45 = (f32[256,128]{1,0:T(8,128)S(1)}, f32[256,128]{1,0:T(8,128)S(1)}, u32[]{:S(2)}, u32[]{:S(2)}) collective-permute-start(f32[256,128]{1,0:T(8,128)S(1)} %get-tuple-element.46.refs_7_.refs_23_.refs_35_), channel_id=1, source_target_pairs={{0,8},{1,9},{2,10},{3,11},{4,12},{5,13},{6,14},{7,15},{8,0},{9,1},... | collective-permute-start | bytes 393224 | tf_op jit(solution)/shard_map/ppermute | solution.py:179
  99.8 9.5 %collective-permute-start.46 = (f32[256,128]{1,0:T(8,128)S(1)}, f32[256,128]{1,0:T(8,128)S(1)}, u32[]{:S(2)}, u32[]{:S(2)}) collective-permute-start(f32[256,128]{1,0:T(8,128)S(1)} %get-tuple-element.46.refs_7_.refs_23_.refs_35_), channel_id=1, source_target_pairs={{0,6},{1,7},{2,4},{3,5},{4,2},{5,3},{6,0},{7,1},{8,14},{9,15},{10,... | collective-permute-start | bytes 393224 | tf_op jit(solution)/shard_map/ppermute | solution.py:179
  102.5 7.2 %collective-permute-start.47 = (f32[256,128]{1,0:T(8,128)S(1)}, f32[256,128]{1,0:T(8,128)S(1)}, u32[]{:S(2)}, u32[]{:S(2)}) collective-permute-start(f32[256,128]{1,0:T(8,128)S(1)} %get-tuple-element.46.refs_7_.refs_23_.refs_35_), channel_id=1, source_target_pairs={{0,4},{1,5},{2,6},{3,7},{4,0},{5,1},{6,2},{7,3},{8,12},{9,13},{10,... | collective-permute-start | bytes 393224 | tf_op jit(solution)/shard_map/ppermute | solution.py:179
  105.7 5.0 %collective-permute-start.48 = (f32[256,128]{1,0:T(8,128)S(1)}, f32[256,128]{1,0:T(8,128)S(1)}, u32[]{:S(2)}, u32[]{:S(2)}) collective-permute-start(f32[256,128]{1,0:T(8,128)S(1)} %get-tuple-element.46.refs_7_.refs_23_.refs_35_), channel_id=1, source_target_pairs={{0,2},{1,3},{2,0},{3,1},{4,6},{5,7},{6,4},{7,5},{8,10},{9,11},{10,... | collective-permute-start | bytes 393224 | tf_op jit(solution)/shard_map/ppermute | solution.py:179
  107.9 2.8 %collective-permute-start.56 = (f32[256,128]{1,0:T(8,128)S(1)}, f32[256,128]{1,0:T(8,128)S(1)}, u32[]{:S(2)}, u32[]{:S(2)}) collective-permute-start(f32[256,128]{1,0:T(8,128)S(1)} %get-tuple-element.46.refs_7_.refs_23_.refs_35_), channel_id=1, source_target_pairs={{0,1},{1,0},{2,3},{3,2},{4,5},{5,4},{6,7},{7,6},{8,9},{9,8},{10,11... | collective-permute-start | bytes 393224 | tf_op jit(solution)/shard_map/ppermute | solution.py:179
  108.8 2.4 %collective-permute-start.49 = (f32[256,128]{1,0:T(8,128)S(1)}, f32[256,128]{1,0:T(8,128)S(1)}, u32[]{:S(2)}, u32[]{:S(2)}) collective-permute-start(f32[256,128]{1,0:T(8,128)S(1)} %get-tuple-element.47.refs_0_.refs_16_), channel_id=1, source_target_pairs={{0,1},{1,0},{2,3},{3,2},{4,5},{5,4},{6,7},{7,6},{8,9},{9,8},{10,11... | collective-permute-start | bytes 393224 | tf_op jit(solution)/shard_map/ppermute | solution.py:179
  109.2 2.0 %collective-permute-start.50 = (f32[256,128]{1,0:T(8,128)S(1)}, f32[256,128]{1,0:T(8,128)S(1)}, u32[]{:S(2)}, u32[]{:S(2)}) collective-permute-start(f32[256,128]{1,0:T(8,128)S(1)} %get-tuple-element.48.refs_1_.refs_17_), channel_id=1, source_target_pairs={{0,1},{1,0},{2,3},{3,2},{4,5},{5,4},{6,7},{7,6},{8,9},{9,8},{10,11... | collective-permute-start | bytes 393224 | tf_op jit(solution)/shard_map/ppermute | solution.py:179
  109.7 2.0 %collective-permute-start.51 = (f32[256,128]{1,0:T(8,128)S(1)}, f32[256,128]{1,0:T(8,128)S(1)}, u32[]{:S(2)}, u32[]{:S(2)}) collective-permute-start(f32[256,128]{1,0:T(8,128)S(1)} %collective-permute-done.44.refs_2_.refs_18_), channel_id=1, source_target_pairs={{0,1},{1,0},{2,3},{3,2},{4,5},{5,4},{6,7},{7,6},{8,9},{9,8},{10,11... | collective-permute-start | bytes 393224 | tf_op jit(solution)/shard_map/ppermute | solution.py:179
  110.7 1.5 %collective-permute-start.53 = (f32[256,128]{1,0:T(8,128)S(1)}, f32[256,128]{1,0:T(8,128)S(1)}, u32[]{:S(2)}, u32[]{:S(2)}) collective-permute-start(f32[256,128]{1,0:T(8,128)S(1)} %collective-permute-done.46.refs_4_.refs_20_), channel_id=1, source_target_pairs={{0,1},{1,0},{2,3},{3,2},{4,5},{5,4},{6,7},{7,6},{8,9},{9,8},{10,11... | collective-permute-start | bytes 393224 | tf_op jit(solution)/shard_map/ppermute | solution.py:179
  111.3 1.5 %collective-permute-start.55 = (f32[256,128]{1,0:T(8,128)S(1)}, f32[256,128]{1,0:T(8,128)S(1)}, u32[]{:S(2)}, u32[]{:S(2)}) collective-permute-start(f32[256,128]{1,0:T(8,128)S(1)} %collective-permute-done.48.refs_6_.refs_22_), channel_id=1, source_target_pairs={{0,1},{1,0},{2,3},{3,2},{4,5},{5,4},{6,7},{7,6},{8,9},{9,8},{10,11... | collective-permute-start | bytes 393224 | tf_op jit(solution)/shard_map/ppermute | solution.py:179
  113.3 6.7 %collective-permute-start.57 = (f32[128,128]{1,0:T(8,128)S(1)}, f32[128,128]{1,0:T(8,128)S(1)}, u32[]{:S(2)}, u32[]{:S(2)}) collective-permute-start(f32[128,128]{1,0:T(8,128)S(1)} %update.5), channel_id=1, source_target_pairs={{0,16},{1,17},{2,18},{3,19},{4,20},{5,21},{6,22},{7,23},{8,24},{9,... | collective-permute-start | bytes 196616 | tf_op jit(solution)/shard_map/ppermute | solution.py:179
  120.0 8.8 %collective-permute-start.58 = (f32[256,128]{1,0:T(8,128)S(1)}, f32[256,128]{1,0:T(8,128)S(1)}, u32[]{:S(2)}, u32[]{:S(2)}) collective-permute-start(f32[256,128]{1,0:T(8,128)S(1)} %pad_maximum_fusion.refs_7_), channel_id=1, source_target_pairs={{0,14},{1,15},{2,12},{3,13},{4,10},{5,11},{6,8},{7,9},{8,6},{9,7},... | collective-permute-start | bytes 393224 | tf_op jit(solution)/shard_map/ppermute | solution.py:179
  121.4 9.7 %collective-permute-start.59 = (f32[256,128]{1,0:T(8,128)S(1)}, f32[256,128]{1,0:T(8,128)S(1)}, u32[]{:S(2)}, u32[]{:S(2)}) collective-permute-start(f32[256,128]{1,0:T(8,128)S(1)} %pad_maximum_fusion.refs_7_), channel_id=1, source_target_pairs={{0,12},{1,13},{2,14},{3,15},{4,8},{5,9},{6,10},{7,11},{8,4},{9,5},... | collective-permute-start | bytes 393224 | tf_op jit(solution)/shard_map/ppermute | solution.py:179
  123.5 10.0 %collective-permute-start.60 = (f32[256,128]{1,0:T(8,128)S(1)}, f32[256,128]{1,0:T(8,128)S(1)}, u32[]{:S(2)}, u32[]{:S(2)}) collective-permute-start(f32[256,128]{1,0:T(8,128)S(1)} %pad_maximum_fusion.refs_7_), channel_id=1, source_target_pairs={{0,10},{1,11},{2,8},{3,9},{4,14},{5,15},{6,12},{7,13},{8,2},{9,3},... | collective-permute-start | bytes 393224 | tf_op jit(solution)/shard_map/ppermute | solution.py:179
  124.3 10.1 %collective-permute-start.61 = (f32[256,128]{1,0:T(8,128)S(1)}, f32[256,128]{1,0:T(8,128)S(1)}, u32[]{:S(2)}, u32[]{:S(2)}) collective-permute-start(f32[256,128]{1,0:T(8,128)S(1)} %pad_maximum_fusion.refs_7_), channel_id=1, source_target_pairs={{0,8},{1,9},{2,10},{3,11},{4,12},{5,13},{6,14},{7,15},{8,0},{9,1},... | collective-permute-start | bytes 393224 | tf_op jit(solution)/shard_map/ppermute | solution.py:179
  125.9 9.0 %collective-permute-start.62 = (f32[256,128]{1,0:T(8,128)S(1)}, f32[256,128]{1,0:T(8,128)S(1)}, u32[]{:S(2)}, u32[]{:S(2)}) collective-permute-start(f32[256,128]{1,0:T(8,128)S(1)} %pad_maximum_fusion.refs_7_), channel_id=1, source_target_pairs={{0,6},{1,7},{2,4},{3,5},{4,2},{5,3},{6,0},{7,1},{8,14},{9,15},{10,... | collective-permute-start | bytes 393224 | tf_op jit(solution)/shard_map/ppermute | solution.py:179
  128.8 6.5 %collective-permute-start.63 = (f32[256,128]{1,0:T(8,128)S(1)}, f32[256,128]{1,0:T(8,128)S(1)}, u32[]{:S(2)}, u32[]{:S(2)}) collective-permute-start(f32[256,128]{1,0:T(8,128)S(1)} %pad_maximum_fusion.refs_7_), channel_id=1, source_target_pairs={{0,4},{1,5},{2,6},{3,7},{4,0},{5,1},{6,2},{7,3},{8,12},{9,13},{10,... | collective-permute-start | bytes 393224 | tf_op jit(solution)/shard_map/ppermute | solution.py:179
  131.0 5.0 %collective-permute-start.64 = (f32[256,128]{1,0:T(8,128)S(1)}, f32[256,128]{1,0:T(8,128)S(1)}, u32[]{:S(2)}, u32[]{:S(2)}) collective-permute-start(f32[256,128]{1,0:T(8,128)S(1)} %pad_maximum_fusion.refs_7_), channel_id=1, source_target_pairs={{0,2},{1,3},{2,0},{3,1},{4,6},{5,7},{6,4},{7,5},{8,10},{9,11},{10,... | collective-permute-start | bytes 393224 | tf_op jit(solution)/shard_map/ppermute | solution.py:179
  133.4 2.7 %collective-permute-start.72 = (f32[256,128]{1,0:T(8,128)S(1)}, f32[256,128]{1,0:T(8,128)S(1)}, u32[]{:S(2)}, u32[]{:S(2)}) collective-permute-start(f32[256,128]{1,0:T(8,128)S(1)} %pad_maximum_fusion.refs_7_), channel_id=1, source_target_pairs={{0,1},{1,0},{2,3},{3,2},{4,5},{5,4},{6,7},{7,6},{8,9},{9,8},{10,11... | collective-permute-start | bytes 393224 | tf_op jit(solution)/shard_map/ppermute | solution.py:179
  134.4 2.3 %collective-permute-start.65 = (f32[256,128]{1,0:T(8,128)S(1)}, f32[256,128]{1,0:T(8,128)S(1)}, u32[]{:S(2)}, u32[]{:S(2)}) collective-permute-start(f32[256,128]{1,0:T(8,128)S(1)} %collective-permute-done.58.refs_0_), channel_id=1, source_target_pairs={{0,1},{1,0},{2,3},{3,2},{4,5},{5,4},{6,7},{7,6},{8,9},{9,8},{10,11... | collective-permute-start | bytes 393224 | tf_op jit(solution)/shard_map/ppermute | solution.py:179
  134.9 1.7 %collective-permute-start.66 = (f32[256,128]{1,0:T(8,128)S(1)}, f32[256,128]{1,0:T(8,128)S(1)}, u32[]{:S(2)}, u32[]{:S(2)}) collective-permute-start(f32[256,128]{1,0:T(8,128)S(1)} %collective-permute-done.59.refs_1_), channel_id=1, source_target_pairs={{0,1},{1,0},{2,3},{3,2},{4,5},{5,4},{6,7},{7,6},{8,9},{9,8},{10,11... | collective-permute-start | bytes 393224 | tf_op jit(solution)/shard_map/ppermute | solution.py:179
  135.2 1.9 %collective-permute-start.67 = (f32[256,128]{1,0:T(8,128)S(1)}, f32[256,128]{1,0:T(8,128)S(1)}, u32[]{:S(2)}, u32[]{:S(2)}) collective-permute-start(f32[256,128]{1,0:T(8,128)S(1)} %collective-permute-done.60.refs_2_), channel_id=1, source_target_pairs={{0,1},{1,0},{2,3},{3,2},{4,5},{5,4},{6,7},{7,6},{8,9},{9,8},{10,11... | collective-permute-start | bytes 393224 | tf_op jit(solution)/shard_map/ppermute | solution.py:179
  136.1 1.5 %collective-permute-start.69 = (f32[256,128]{1,0:T(8,128)S(1)}, f32[256,128]{1,0:T(8,128)S(1)}, u32[]{:S(2)}, u32[]{:S(2)}) collective-permute-start(f32[256,128]{1,0:T(8,128)S(1)} %collective-permute-done.62.refs_4_), channel_id=1, source_target_pairs={{0,1},{1,0},{2,3},{3,2},{4,5},{5,4},{6,7},{7,6},{8,9},{9,8},{10,11... | collective-permute-start | bytes 393224 | tf_op jit(solution)/shard_map/ppermute | solution.py:179
  (15 other events, 61.9 us)

commit v5 on v4

--- a/solution.py
+++ b/solution.py
@@ -504,8 +504,6 @@
             return flat, out[0]
         z, side = out
         earlier.append(z)
-        if level > 1 and len(rhs.done) < level_count - 1:
-            rhs.next_level(z)
         throughs = [keep("update", upd_factor, (2**level - 2, u_size // group))]
         following = [keep("pivots", piv_inverse, (2 ** (level + 1) - 2, sizes[level]))]
         if level == level_count - 1:
@@ -515,7 +513,7 @@
         pieces = spread(update, 2 * group, *following)
         if level == 1:
             rhs.pair_root(update)
-        if level == 1:
+        if level < level_count - 1:
             rhs.next_level(update)
         if level == level_count - 1:
             parts = []

time: 141 us -> 139 us (0.986)
  Pallas kernels: 33.4 us -> 31.7 us
    pallas_call x4, Pallas kernels: 1.9 us -> 0.15 us  [join_rows(): pl.pallas_call(functools.partial(join_kernel, plans), out_shape=tuple((ja...]
  transfers between devices with their start and end apart: 73 -> 73, of which waited for: 40 -> 46; matrix products, arithmetic and copies ran while one was open for 0% -> 0% of each run, Pallas kernels for 19% -> 16%
where the time goes in v5:
time: 139 us; the launch traced here: 138 us
  starting transfers between devices  55 us (40%)
  waiting for transfers between devices  47.6 us (34%)
  Pallas kernels  31.7 us (23%)
  local copies, waits for them, and re-layouts  3 us (2%)
    ppermute x73, starting transfers between devices, exchange(): lax.ppermute(x, AXES, [(source, source ^ mask) for source in range(size)])  55 us
    ppermute x73, waiting for transfers between devices, exchange(): lax.ppermute(x, AXES, [(source, source ^ mask) for source in range(size)])  47.6 us
    pallas_call x1, Pallas kernels, solve_subtree(): pl.pallas_call(functools.partial(subtree_kernel, bounds), out_shape=(jax....  9.92 us
    pallas_call x6, Pallas kernels, prepare_factor(): pl.pallas_call(functools.partial(factor_kernel, block), out_shape=(jax.Sh...  9.92 us
    pallas_call x4, Pallas kernels, solve_pivots(): pl.pallas_call(functools.partial(pivot_kernel, [masks for _, masks in pie...  8.75 us
    unnamed x13, local copies, waits for them, and re-layouts  3 us
    pallas_call x3, Pallas kernels, solve_update(): pl.pallas_call(functools.partial(update_kernel, [masks for _, masks in pi...  2.98 us
  transfers between devices with their start and end apart: 73, of which 46 were waited for; matrix products, arithmetic and copies ran while one was open for 0% of the time, Pallas kernels for 16%

profile of v5, /device:TPU:0, one launch (start us, length us, event | category | flops | bytes accessed | tf_op | source)
XLA Modules:
  0.0 138.3 jit_solution(8110583784493676767)
XLA Ops:
  0.6 3.0 %collective-permute-start.3 = (f32[960,128]{1,0:T(8,128)}, f32[960,128]{1,0:T(8,128)S(1)}, u32[]{:S(2)}, u32[]{:S(2)}) collective-permute-start(f32[960,128]{1,0:T(8,128)} %refs_0_.1), channel_id=1, source_target_pairs={{0,2},{1,3},{2,0},{3,1},{4,6},{5,7},{6,4},{7,5},{8,10},{9,11},{10,... | collective-permute-start | bytes 1474568 | tf_op jit(solution)/shard_map/ppermute | solution.py:179
  3.6 9.9 %subtree.1 = (f32[3072,128]{1,0:T(8,128)}, f32[256,128]{1,0:T(8,128)S(1)}, bf16[1024,2048]{1,0:T(8,128)(2,1)}) custom-call(s32[2,23]{1,0:T(2,128)} %bitcast.8, f32[3072,128]{1,0:T(8,128)} %rhs_in.1, f32[24,128,128]{2,1,0:T(8,128)} %dinv_in.1, f32[23,2,128,128]{3,2,1,0:T(8,128)} %off_in.1, f32[256,3072]{1,0:T(8,128)} %upd_in.1, f32[960,2048]{1,0:T(8,128)} %factor.23), custom_call_target="tpu_custom_call" | custom-call | flops 1000000 | bytes 100000 | tf_op jit(solution)/shard_map/subtree/pallas_call | solution.py:146
  13.7 4.9 %collective-permute-done.after.refs_0_ = f32[256,128]{1,0:T(8,128)S(1)} collective-permute-done((f32[256,128]{1,0:T(8,128)S(1)}, f32[256,128]{1,0:T(8,128)S(1)}, u32[]{:S(2)}, u32[]{:S(2)}) %collective-permute-start) | collective-permute-done | bytes 131104 | tf_op jit(solution)/shard_map/ppermute | solution.py:179
  19.3 1.5 %collective-permute-done.2.refs_3_ = f32[256,128]{1,0:T(8,128)S(1)} collective-permute-done((f32[256,128]{1,0:T(8,128)S(1)}, f32[256,128]{1,0:T(8,128)S(1)}, u32[]{:S(2)}, u32[]{:S(2)}) %collective-permute-start.2) | collective-permute-done | bytes 131104 | tf_op jit(solution)/shard_map/ppermute | solution.py:179
  21.0 2.2 %copy-done = bf16[1024,2048]{1,0:T(8,128)(2,1)S(1)} copy-done((bf16[1024,2048]{1,0:T(8,128)(2,1)S(1)}, bf16[1024,2048]{1,0:T(8,128)(2,1)}, u32[]{:S(2)}) %copy-start) | copy-done | bytes 4194328
  23.2 2.0 %pivots.4 = (f32[512,128]{1,0:T(8,128)S(1)}, f32[512,128]{1,0:T(8,128)S(1)}) custom-call(s32[1]{0:T(128)} %bitcast.1.me, s32[2,32]{1,0:T(2,128)S(1)} %bitcast.7, f32[256,128]{1,0:T(8,128)S(1)} %collective-permute-done.after.refs_0_, f32[256,128]{1,0:T(8,128)S(1)} %get-tuple-element.28.refs_1_, f32[256,128]{1,0:T(8,128)S(1)} %collective-permute-done.1.refs_2_, ...), custom_call_target="tpu_custom_call" | custom-call | flops 805306368 | bytes 8000000 | tf_op jit(solution)/shard_map/pivots/pallas_call | solution.py:331
  25.2 1.1 collective-permute-start.5
  26.3 1.5 %collective-permute-start.15 = (f32[768,128]{1,0:T(8,128)S(1)}, f32[768,128]{1,0:T(8,128)S(1)}, u32[]{:S(2)}, u32[]{:S(2)}) collective-permute-start(f32[768,128]{1,0:T(8,128)S(1)} %get-tuple-element.36.refs_0_), channel_id=1, source_target_pairs={{0,4},{1,5},{2,6},{3,7},{4,0},{5,1},{6,2},{7,3},{8,12},{9,13},{10,... | collective-permute-start | bytes 1179656 | tf_op jit(solution)/shard_map/ppermute | solution.py:179
  27.8 2.3 %factor.12 = (bf16[1024,2048]{1,0:T(8,128)(2,1)S(1)}, f32[512,128]{1,0:T(8,128)S(1)}) custom-call(f32[896,2048]{1,0:T(8,128)} %factor.21, f32[512,128]{1,0:T(8,128)S(1)} %get-tuple-element.31.own.refs_33_), custom_call_target="tpu_custom_call" | custom-call | bytes 8388608 | tf_op jit(solution)/shard_map/factor/pallas_call | solution.py:222
  30.3 3.4 %collective-permute-done.5.refs_0_ = f32[512,128]{1,0:T(8,128)S(1)} collective-permute-done((f32[512,128]{1,0:T(8,128)S(1)}, f32[512,128]{1,0:T(8,128)S(1)}, u32[]{:S(2)}, u32[]{:S(2)}) %collective-permute-start.5) | collective-permute-done | bytes 262176 | tf_op jit(solution)/shard_map/ppermute | solution.py:179
  33.7 1.5 %collective-permute-done.6.refs_2_ = f32[512,128]{1,0:T(8,128)S(1)} collective-permute-done((f32[512,128]{1,0:T(8,128)S(1)}, f32[512,128]{1,0:T(8,128)S(1)}, u32[]{:S(2)}, u32[]{:S(2)}) %collective-permute-start.6) | collective-permute-done | bytes 262176 | tf_op jit(solution)/shard_map/ppermute | solution.py:179
  35.2 1.5 %update.3.after.refs_3_ = f32[512,128]{1,0:T(8,128)S(1)} custom-call(s32[1]{0:T(128)} %bitcast.1.me, f32[512,128]{1,0:T(8,128)S(1)} %collective-permute-done.5.refs_0_, f32[512,128]{1,0:T(8,128)S(1)} %get-tuple-element.32.refs_1_, f32[512,128]{1,0:T(8,128)S(1)} %collective-permute-done.6.refs_2_, f32[512,128]{1,0:T(8,128)S(1)} %collective-permute-done.7.refs_3_, ...), custom_call_target="tpu_custom_call" | custom-call | flops 805306368 | bytes 8000000 | tf_op jit(solution)/shard_map/update/pallas_call | solution.py:366
  36.7 2.0 %collective-permute-start.8 = (f32[512,128]{1,0:T(8,128)S(1)}, f32[512,128]{1,0:T(8,128)S(1)}, u32[]{:S(2)}, u32[]{:S(2)}) collective-permute-start(f32[512,128]{1,0:T(8,128)S(1)} %update.3.after.refs_3_), channel_id=1, source_target_pairs={{0,6},{1,7},{2,4},{3,5},{4,2},{5,3},{6,0},{7,1},{8,14},{9,15},{10,... | collective-permute-start | bytes 786440 | tf_op jit(solution)/shard_map/ppermute | solution.py:179
  39.2 1.0 collective-permute-start.10
  41.0 2.7 %collective-permute-start.17 = (f32[64,128]{1,0:T(8,128)S(1)}, f32[64,128]{1,0:T(8,128)S(1)}, u32[]{:S(2)}, u32[]{:S(2)}) collective-permute-start(f32[64,128]{1,0:T(8,128)S(1)} %slice.3.refs_0_), channel_id=1, source_target_pairs={{0,16},{1,17},{2,18},{3,19},{4,20},{5,21},{6,22},{7,23},{8,24},{9,... | collective-permute-start | bytes 98312 | tf_op jit(solution)/shard_map/ppermute | solution.py:179
  43.7 3.1 %collective-permute-done.8.own = f32[512,128]{1,0:T(8,128)S(1)} collective-permute-done((f32[512,128]{1,0:T(8,128)S(1)}, f32[512,128]{1,0:T(8,128)S(1)}, u32[]{:S(2)}, u32[]{:S(2)}) %collective-permute-start.8) | collective-permute-done | bytes 262176 | tf_op jit(solution)/shard_map/ppermute | solution.py:179
  46.9 2.3 %factor.14 = (bf16[512,2048]{1,0:T(8,128)(2,1)S(1)}, f32[512,128]{1,0:T(8,128)}) custom-call(f32[960,2048]{1,0:T(8,128)} %factor.23, f32[512,128]{1,0:T(8,128)S(1)} %collective-permute-done.8.own), custom_call_target="tpu_custom_call" | custom-call | bytes 4194304 | tf_op jit(solution)/shard_map/factor/pallas_call | solution.py:222
  49.1 0.8 collective-permute-start.11
  49.9 1.7 %collective-permute-done.9.refs_1_ = f32[512,128]{1,0:T(8,128)S(1)} collective-permute-done((f32[512,128]{1,0:T(8,128)S(1)}, f32[512,128]{1,0:T(8,128)S(1)}, u32[]{:S(2)}, u32[]{:S(2)}) %collective-permute-start.9) | collective-permute-done | bytes 262176 | tf_op jit(solution)/shard_map/ppermute | solution.py:179
  52.3 1.0 collective-permute-done.12.refs_5_
  53.9 2.7 %pivots.5 = (f32[256,128]{1,0:T(8,128)S(1)}, f32[256,128]{1,0:T(8,128)S(1)}) custom-call(s32[1]{0:T(128)} %bitcast.1.me, s32[16,14]{1,0:T(8,128)S(1)} %bitcast.4, f32[512,128]{1,0:T(8,128)} %get-tuple-element.35.refs_0_, f32[512,128]{1,0:T(8,128)S(1)} %collective-permute-done.9.refs_1_, f32[512,128]{1,0:T(8,128)} %collective-permute-done.10.refs_2_, ...), custom_call_target="tpu_custom_call" | custom-call | flops 402653184 | bytes 8000000 | tf_op jit(solution)/shard_map/pivots/pallas_call | solution.py:331
  56.6 1.8 %collective-permute-start.18 = (f32[256,128]{1,0:T(8,128)S(1)}, f32[256,128]{1,0:T(8,128)S(1)}, u32[]{:S(2)}, u32[]{:S(2)}) collective-permute-start(f32[256,128]{1,0:T(8,128)S(1)} %get-tuple-element.39.refs_3_.refs_34_), channel_id=1, source_target_pairs={{0,6},{1,7},{2,4},{3,5},{4,2},{5,3},{6,0},{7,1},{8,14},{9,15},{10,... | collective-permute-start | bytes 393224 | tf_op jit(solution)/shard_map/ppermute | solution.py:179
  58.4 0.7 collective-permute-start.19
  59.1 1.0 collective-permute-start.20
  60.1 1.6 %collective-permute-start.40 = (f32[512,128]{1,0:T(8,128)S(1)}, f32[512,128]{1,0:T(8,128)S(1)}, u32[]{:S(2)}, u32[]{:S(2)}) collective-permute-start(f32[512,128]{1,0:T(8,128)S(1)} %copy-done.3), channel_id=1, source_target_pairs={{0,8},{1,9},{2,10},{3,11},{4,12},{5,13},{6,14},{7,15},{8,0},{9,1},... | collective-permute-start | bytes 786440 | tf_op jit(solution)/shard_map/ppermute | solution.py:179
  61.7 2.2 %collective-permute-done.18.own = f32[256,128]{1,0:T(8,128)S(1)} collective-permute-done((f32[256,128]{1,0:T(8,128)S(1)}, f32[256,128]{1,0:T(8,128)S(1)}, u32[]{:S(2)}, u32[]{:S(2)}) %collective-permute-start.18) | collective-permute-done | bytes 131104 | tf_op jit(solution)/shard_map/ppermute | solution.py:179
  63.9 1.6 %factor.16 = (bf16[512,2048]{1,0:T(8,128)(2,1)S(1)}, f32[256,128]{1,0:T(8,128)S(1)}) custom-call(f32[896,2048]{1,0:T(8,128)} %factor.21, f32[256,128]{1,0:T(8,128)S(1)} %collective-permute-done.18.own), custom_call_target="tpu_custom_call" | custom-call | bytes 4194304 | tf_op jit(solution)/shard_map/factor/pallas_call | solution.py:222
  67.5 0.9 update.4.after.refs_7_
  68.4 2.9 %collective-permute-start.25 = (f32[256,128]{1,0:T(8,128)S(1)}, f32[256,128]{1,0:T(8,128)S(1)}, u32[]{:S(2)}, u32[]{:S(2)}) collective-permute-start(f32[256,128]{1,0:T(8,128)S(1)} %update.4.after.refs_7_), channel_id=1, source_target_pairs={{0,14},{1,15},{2,12},{3,13},{4,10},{5,11},{6,8},{7,9},{8,6},{9,7},... | collective-permute-start | bytes 393224 | tf_op jit(solution)/shard_map/ppermute | solution.py:179
  71.8 2.0 %collective-permute-start.27 = (f32[256,128]{1,0:T(8,128)S(1)}, f32[256,128]{1,0:T(8,128)S(1)}, u32[]{:S(2)}, u32[]{:S(2)}) collective-permute-start(f32[256,128]{1,0:T(8,128)S(1)} %update.4.after.refs_7_), channel_id=1, source_target_pairs={{0,10},{1,11},{2,8},{3,9},{4,14},{5,15},{6,12},{7,13},{8,2},{9,3},... | collective-permute-start | bytes 393224 | tf_op jit(solution)/shard_map/ppermute | solution.py:179
  74.5 2.5 %collective-permute-done.25.own = f32[256,128]{1,0:T(8,128)S(1)} collective-permute-done((f32[256,128]{1,0:T(8,128)S(1)}, f32[256,128]{1,0:T(8,128)S(1)}, u32[]{:S(2)}, u32[]{:S(2)}) %collective-permute-start.25) | collective-permute-done | bytes 131104 | tf_op jit(solution)/shard_map/ppermute | solution.py:179
  77.0 1.8 %collective-permute-start.29 = (f32[256,128]{1,0:T(8,128)S(1)}, f32[256,128]{1,0:T(8,128)S(1)}, u32[]{:S(2)}, u32[]{:S(2)}) collective-permute-start(f32[256,128]{1,0:T(8,128)S(1)} %update.4.after.refs_7_), channel_id=1, source_target_pairs={{0,6},{1,7},{2,4},{3,5},{4,2},{5,3},{6,0},{7,1},{8,14},{9,15},{10,... | collective-permute-start | bytes 393224 | tf_op jit(solution)/shard_map/ppermute | solution.py:179
  79.3 1.3 collective-permute-start.30
  80.7 1.8 %collective-permute-done.27.refs_2_ = f32[256,128]{1,0:T(8,128)S(1)} collective-permute-done((f32[256,128]{1,0:T(8,128)S(1)}, f32[256,128]{1,0:T(8,128)S(1)}, u32[]{:S(2)}, u32[]{:S(2)}) %collective-permute-start.27) | collective-permute-done | bytes 131104 | tf_op jit(solution)/shard_map/ppermute | solution.py:179
  82.5 1.0 collective-permute-start.31
  83.5 1.3 factor.18
  85.8 1.6 %collective-permute-done.31.refs_6_ = f32[256,128]{1,0:T(8,128)S(1)} collective-permute-done((f32[256,128]{1,0:T(8,128)S(1)}, f32[256,128]{1,0:T(8,128)S(1)}, u32[]{:S(2)}, u32[]{:S(2)}) %collective-permute-start.31) | collective-permute-done | bytes 131104 | tf_op jit(solution)/shard_map/ppermute | solution.py:179
  90.2 1.6 %pivots.6 = (f32[256,128]{1,0:T(8,128)S(1)}, f32[128,128]{1,0:T(8,128)S(1)}) custom-call(s32[1]{0:T(128)} %bitcast.1.me, s32[16,14]{1,0:T(8,128)S(1)} %bitcast.5, f32[256,128]{1,0:T(8,128)S(1)} %get-tuple-element.43.refs_0_, f32[256,128]{1,0:T(8,128)S(1)} %collective-permute-done.26.refs_1_, f32[256,128]{1,0:T(8,128)S(1)} %collective-permute-done.27.refs_2_, ...), custom_call_target="tpu_custom_call" | custom-call | flops 201326592 | bytes 8000000 | tf_op jit(solution)/shard_map/pivots/pallas_call | solution.py:331
  91.8 2.2 %collective-permute-start.42 = (f32[256,128]{1,0:T(8,128)S(1)}, f32[256,128]{1,0:T(8,128)S(1)}, u32[]{:S(2)}, u32[]{:S(2)}) collective-permute-start(f32[256,128]{1,0:T(8,128)S(1)} %get-tuple-element.46.refs_7_.refs_23_.refs_35_), channel_id=1, source_target_pairs={{0,14},{1,15},{2,12},{3,13},{4,10},{5,11},{6,8},{7,9},{8,6},{9,7},... | collective-permute-start | bytes 393224 | tf_op jit(solution)/shard_map/ppermute | solution.py:179
  94.0 1.2 collective-permute-start.43
  95.2 2.0 %collective-permute-start.44 = (f32[256,128]{1,0:T(8,128)S(1)}, f32[256,128]{1,0:T(8,128)S(1)}, u32[]{:S(2)}, u32[]{:S(2)}) collective-permute-start(f32[256,128]{1,0:T(8,128)S(1)} %get-tuple-element.46.refs_7_.refs_23_.refs_35_), channel_id=1, source_target_pairs={{0,10},{1,11},{2,8},{3,9},{4,14},{5,15},{6,12},{7,13},{8,2},{9,3},... | collective-permute-start | bytes 393224 | tf_op jit(solution)/shard_map/ppermute | solution.py:179
  97.7 1.1 collective-permute-start.46
  98.8 1.6 %collective-permute-done.42.own = f32[256,128]{1,0:T(8,128)S(1)} collective-permute-done((f32[256,128]{1,0:T(8,128)S(1)}, f32[256,128]{1,0:T(8,128)S(1)}, u32[]{:S(2)}, u32[]{:S(2)}) %collective-permute-start.42) | collective-permute-done | bytes 131104 | tf_op jit(solution)/shard_map/ppermute | solution.py:179
  101.0 1.3 factor.20
  102.3 1.3 collective-permute-done.43.own
  103.6 1.0 collective-permute-start.48
  104.6 1.1 factor.22
  105.9 1.0 collective-permute-done.45.refs_3_.refs_19_
  107.6 0.9 collective-permute-done.48.refs_6_.refs_22_
  111.2 2.6 %collective-permute-start.57 = (f32[128,128]{1,0:T(8,128)S(1)}, f32[128,128]{1,0:T(8,128)S(1)}, u32[]{:S(2)}, u32[]{:S(2)}) collective-permute-start(f32[128,128]{1,0:T(8,128)S(1)} %update.5), channel_id=1, source_target_pairs={{0,16},{1,17},{2,18},{3,19},{4,20},{5,21},{6,22},{7,23},{8,24},{9,... | collective-permute-start | bytes 196616 | tf_op jit(solution)/shard_map/ppermute | solution.py:179
  113.9 4.1 %collective-permute-done.57 = f32[128,128]{1,0:T(8,128)S(1)} collective-permute-done((f32[128,128]{1,0:T(8,128)S(1)}, f32[128,128]{1,0:T(8,128)S(1)}, u32[]{:S(2)}, u32[]{:S(2)}) %collective-permute-start.57) | collective-permute-done | bytes 65568 | tf_op jit(solution)/shard_map/ppermute | solution.py:179
  117.9 1.6 %collective-permute-start.58 = (f32[256,128]{1,0:T(8,128)S(1)}, f32[256,128]{1,0:T(8,128)S(1)}, u32[]{:S(2)}, u32[]{:S(2)}) collective-permute-start(f32[256,128]{1,0:T(8,128)S(1)} %pad_maximum_fusion.refs_7_), channel_id=1, source_target_pairs={{0,14},{1,15},{2,12},{3,13},{4,10},{5,11},{6,8},{7,9},{8,6},{9,7},... | collective-permute-start | bytes 393224 | tf_op jit(solution)/shard_map/ppermute | solution.py:179
  119.6 1.8 %collective-permute-start.59 = (f32[256,128]{1,0:T(8,128)S(1)}, f32[256,128]{1,0:T(8,128)S(1)}, u32[]{:S(2)}, u32[]{:S(2)}) collective-permute-start(f32[256,128]{1,0:T(8,128)S(1)} %pad_maximum_fusion.refs_7_), channel_id=1, source_target_pairs={{0,12},{1,13},{2,14},{3,15},{4,8},{5,9},{6,10},{7,11},{8,4},{9,5},... | collective-permute-start | bytes 393224 | tf_op jit(solution)/shard_map/ppermute | solution.py:179
  121.4 1.1 collective-permute-start.60
  122.5 1.3 collective-permute-start.61
  123.9 1.5 %collective-permute-start.62 = (f32[256,128]{1,0:T(8,128)S(1)}, f32[256,128]{1,0:T(8,128)S(1)}, u32[]{:S(2)}, u32[]{:S(2)}) collective-permute-start(f32[256,128]{1,0:T(8,128)S(1)} %pad_maximum_fusion.refs_7_), channel_id=1, source_target_pairs={{0,6},{1,7},{2,4},{3,5},{4,2},{5,3},{6,0},{7,1},{8,14},{9,15},{10,... | collective-permute-start | bytes 393224 | tf_op jit(solution)/shard_map/ppermute | solution.py:179
  125.3 1.4 %collective-permute-done.58.refs_0_ = f32[256,128]{1,0:T(8,128)S(1)} collective-permute-done((f32[256,128]{1,0:T(8,128)S(1)}, f32[256,128]{1,0:T(8,128)S(1)}, u32[]{:S(2)}, u32[]{:S(2)}) %collective-permute-start.58) | collective-permute-done | bytes 131104 | tf_op jit(solution)/shard_map/ppermute | solution.py:179
  126.7 1.0 collective-permute-start.63
  127.7 1.2 collective-permute-done.59.refs_1_
  128.9 1.0 collective-permute-start.64
  129.9 1.4 collective-permute-done.60.refs_2_
  131.3 1.0 collective-permute-done.61.refs_3_
  133.1 0.8 collective-permute-done.64.refs_6_
  135.9 2.4 %pivots.7 = f32[960,128]{1,0:T(8,128)} custom-call(s32[1]{0:T(128)} %bitcast.1.me, s32[16,14]{1,0:T(8,128)S(1)} %bitcast.6, f32[256,128]{1,0:T(8,128)S(1)} %collective-permute-done.58.refs_0_, f32[256,128]{1,0:T(8,128)S(1)} %collective-permute-done.59.refs_1_, f32[256,128]{1,0:T(8,128)S(1)} %collective-permute-done.60.refs_2_, ...), custom_call_target="tpu_custom_call" | custom-call | flops 100663296 | bytes 8000000 | tf_op jit(solution)/shard_map/pivots/pallas_call | solution.py:331
  (115 shorter events, 18.3 us)
Async XLA Ops:
  0.6 18.0 %collective-permute-start.3 = (f32[960,128]{1,0:T(8,128)}, f32[960,128]{1,0:T(8,128)S(1)}, u32[]{:S(2)}, u32[]{:S(2)}) collective-permute-start(f32[960,128]{1,0:T(8,128)} %refs_0_.1), channel_id=1, source_target_pairs={{0,2},{1,3},{2,0},{3,1},{4,6},{5,7},{6,4},{7,5},{8,10},{9,11},{10,... | collective-permute-start | bytes 1474568 | tf_op jit(solution)/shard_map/ppermute | solution.py:179
  13.6 5.0 %collective-permute-start = (f32[256,128]{1,0:T(8,128)S(1)}, f32[256,128]{1,0:T(8,128)S(1)}, u32[]{:S(2)}, u32[]{:S(2)}) collective-permute-start(f32[256,128]{1,0:T(8,128)S(1)} %get-tuple-element.28.refs_1_), channel_id=1, source_target_pairs={{0,2},{1,3},{2,0},{3,1},{4,6},{5,7},{6,4},{7,5},{8,10},{9,11},{10,... | collective-permute-start | bytes 393224 | tf_op jit(solution)/shard_map/ppermute | solution.py:179
  18.7 2.4 %collective-permute-start.4 = (f32[1024,128]{1,0:T(8,128)S(1)}, f32[1024,128]{1,0:T(8,128)S(1)}, u32[]{:S(2)}, u32[]{:S(2)}) collective-permute-start(f32[1024,128]{1,0:T(8,128)S(1)} %get-tuple-element.29.refs_4_), channel_id=1, source_target_pairs={{0,1},{1,0},{2,3},{3,2},{4,5},{5,4},{6,7},{7,6},{8,9},{9,8},{10,11... | collective-permute-start | bytes 1572872 | tf_op jit(solution)/shard_map/ppermute | solution.py:179
  18.8 2.1 %collective-permute-start.2 = (f32[256,128]{1,0:T(8,128)S(1)}, f32[256,128]{1,0:T(8,128)S(1)}, u32[]{:S(2)}, u32[]{:S(2)}) collective-permute-start(f32[256,128]{1,0:T(8,128)S(1)} %get-tuple-element.28.refs_1_), channel_id=1, source_target_pairs={{0,1},{1,0},{2,3},{3,2},{4,5},{5,4},{6,7},{7,6},{8,9},{9,8},{10,11... | collective-permute-start | bytes 393224 | tf_op jit(solution)/shard_map/ppermute | solution.py:179
  19.3 1.8 %collective-permute-start.1 = (f32[256,128]{1,0:T(8,128)S(1)}, f32[256,128]{1,0:T(8,128)S(1)}, u32[]{:S(2)}, u32[]{:S(2)}) collective-permute-start(f32[256,128]{1,0:T(8,128)S(1)} %collective-permute-done.after.refs_0_), channel_id=1, source_target_pairs={{0,1},{1,0},{2,3},{3,2},{4,5},{5,4},{6,7},{7,6},{8,9},{9,8},{10,11... | collective-permute-start | bytes 393224 | tf_op jit(solution)/shard_map/ppermute | solution.py:179
  25.2 8.4 %collective-permute-start.5 = (f32[512,128]{1,0:T(8,128)S(1)}, f32[512,128]{1,0:T(8,128)S(1)}, u32[]{:S(2)}, u32[]{:S(2)}) collective-permute-start(f32[512,128]{1,0:T(8,128)S(1)} %get-tuple-element.31.own.refs_33_), channel_id=1, source_target_pairs={{0,2},{1,3},{2,0},{3,1},{4,6},{5,7},{6,4},{7,5},{8,10},{9,11},{10,... | collective-permute-start | bytes 786440 | tf_op jit(solution)/shard_map/ppermute | solution.py:179
  26.3 13.9 %collective-permute-start.15 = (f32[768,128]{1,0:T(8,128)S(1)}, f32[768,128]{1,0:T(8,128)S(1)}, u32[]{:S(2)}, u32[]{:S(2)}) collective-permute-start(f32[768,128]{1,0:T(8,128)S(1)} %get-tuple-element.36.refs_0_), channel_id=1, source_target_pairs={{0,4},{1,5},{2,6},{3,7},{4,0},{5,1},{6,2},{7,3},{8,12},{9,13},{10,... | collective-permute-start | bytes 1179656 | tf_op jit(solution)/shard_map/ppermute | solution.py:179
  30.2 3.5 %collective-permute-start.7 = (f32[512,128]{1,0:T(8,128)S(1)}, f32[512,128]{1,0:T(8,128)S(1)}, u32[]{:S(2)}, u32[]{:S(2)}) collective-permute-start(f32[512,128]{1,0:T(8,128)S(1)} %get-tuple-element.32.refs_1_), channel_id=1, source_target_pairs={{0,1},{1,0},{2,3},{3,2},{4,5},{5,4},{6,7},{7,6},{8,9},{9,8},{10,11... | collective-permute-start | bytes 786440 | tf_op jit(solution)/shard_map/ppermute | solution.py:179
  33.7 1.5 %collective-permute-start.6 = (f32[512,128]{1,0:T(8,128)S(1)}, f32[512,128]{1,0:T(8,128)S(1)}, u32[]{:S(2)}, u32[]{:S(2)}) collective-permute-start(f32[512,128]{1,0:T(8,128)S(1)} %collective-permute-done.5.refs_0_), channel_id=1, source_target_pairs={{0,1},{1,0},{2,3},{3,2},{4,5},{5,4},{6,7},{7,6},{8,9},{9,8},{10,11... | collective-permute-start | bytes 786440 | tf_op jit(solution)/shard_map/ppermute | solution.py:179
  36.7 10.2 %collective-permute-start.8 = (f32[512,128]{1,0:T(8,128)S(1)}, f32[512,128]{1,0:T(8,128)S(1)}, u32[]{:S(2)}, u32[]{:S(2)}) collective-permute-start(f32[512,128]{1,0:T(8,128)S(1)} %update.3.after.refs_3_), channel_id=1, source_target_pairs={{0,6},{1,7},{2,4},{3,5},{4,2},{5,3},{6,0},{7,1},{8,14},{9,15},{10,... | collective-permute-start | bytes 786440 | tf_op jit(solution)/shard_map/ppermute | solution.py:179
  38.7 12.9 %collective-permute-start.9 = (f32[512,128]{1,0:T(8,128)S(1)}, f32[512,128]{1,0:T(8,128)S(1)}, u32[]{:S(2)}, u32[]{:S(2)}) collective-permute-start(f32[512,128]{1,0:T(8,128)S(1)} %update.3.after.refs_3_), channel_id=1, source_target_pairs={{0,4},{1,5},{2,6},{3,7},{4,0},{5,1},{6,2},{7,3},{8,12},{9,13},{10,... | collective-permute-start | bytes 786440 | tf_op jit(solution)/shard_map/ppermute | solution.py:179
  39.2 12.6 %collective-permute-start.10 = (f32[512,128]{1,0:T(8,128)S(1)}, f32[512,128]{1,0:T(8,128)}, u32[]{:S(2)}, u32[]{:S(2)}) collective-permute-start(f32[512,128]{1,0:T(8,128)S(1)} %update.3.after.refs_3_), channel_id=1, source_target_pairs={{0,2},{1,3},{2,0},{3,1},{4,6},{5,7},{6,4},{7,5},{8,10},{9,11},{10,... | collective-permute-start | bytes 786440 | tf_op jit(solution)/shard_map/ppermute | solution.py:179
  41.0 12.9 %collective-permute-start.16 = (f32[1024,128]{1,0:T(8,128)S(1)}, f32[1024,128]{1,0:T(8,128)}, u32[]{:S(2)}, u32[]{:S(2)}) collective-permute-start(f32[1024,128]{1,0:T(8,128)S(1)} %get-tuple-element.37.refs_8_), channel_id=1, source_target_pairs={{0,1},{1,0},{2,3},{3,2},{4,5},{5,4},{6,7},{7,6},{8,9},{9,8},{10,11... | collective-permute-start | bytes 1572872 | tf_op jit(solution)/shard_map/ppermute | solution.py:179
  41.0 8.1 %collective-permute-start.17 = (f32[64,128]{1,0:T(8,128)S(1)}, f32[64,128]{1,0:T(8,128)S(1)}, u32[]{:S(2)}, u32[]{:S(2)}) collective-permute-start(f32[64,128]{1,0:T(8,128)S(1)} %slice.3.refs_0_), channel_id=1, source_target_pairs={{0,16},{1,17},{2,18},{3,19},{4,20},{5,21},{6,22},{7,23},{8,24},{9,... | collective-permute-start | bytes 98312 | tf_op jit(solution)/shard_map/ppermute | solution.py:179
  46.9 5.4 %collective-permute-start.14 = (f32[512,128]{1,0:T(8,128)S(1)}, f32[512,128]{1,0:T(8,128)}, u32[]{:S(2)}, u32[]{:S(2)}) collective-permute-start(f32[512,128]{1,0:T(8,128)S(1)} %update.3.after.refs_3_), channel_id=1, source_target_pairs={{0,1},{1,0},{2,3},{3,2},{4,5},{5,4},{6,7},{7,6},{8,9},{9,8},{10,11... | collective-permute-start | bytes 786440 | tf_op jit(solution)/shard_map/ppermute | solution.py:179
  49.1 3.1 %collective-permute-start.11 = (f32[512,128]{1,0:T(8,128)}, f32[512,128]{1,0:T(8,128)}, u32[]{:S(2)}, u32[]{:S(2)}) collective-permute-start(f32[512,128]{1,0:T(8,128)} %get-tuple-element.35.refs_0_), channel_id=1, source_target_pairs={{0,1},{1,0},{2,3},{3,2},{4,5},{5,4},{6,7},{7,6},{8,9},{9,8},{10,11... | collective-permute-start | bytes 786440 | tf_op jit(solution)/shard_map/ppermute | solution.py:179
  51.6 1.7 %collective-permute-start.12 = (f32[512,128]{1,0:T(8,128)S(1)}, f32[512,128]{1,0:T(8,128)}, u32[]{:S(2)}, u32[]{:S(2)}) collective-permute-start(f32[512,128]{1,0:T(8,128)S(1)} %collective-permute-done.9.refs_1_), channel_id=1, source_target_pairs={{0,1},{1,0},{2,3},{3,2},{4,5},{5,4},{6,7},{7,6},{8,9},{9,8},{10,11... | collective-permute-start | bytes 786440 | tf_op jit(solution)/shard_map/ppermute | solution.py:179
  51.8 2.0 %collective-permute-start.13 = (f32[512,128]{1,0:T(8,128)}, f32[512,128]{1,0:T(8,128)}, u32[]{:S(2)}, u32[]{:S(2)}) collective-permute-start(f32[512,128]{1,0:T(8,128)} %collective-permute-done.10.refs_2_), channel_id=1, source_target_pairs={{0,1},{1,0},{2,3},{3,2},{4,5},{5,4},{6,7},{7,6},{8,9},{9,8},{10,11... | collective-permute-start | bytes 786440 | tf_op jit(solution)/shard_map/ppermute | solution.py:179
  56.6 7.3 %collective-permute-start.18 = (f32[256,128]{1,0:T(8,128)S(1)}, f32[256,128]{1,0:T(8,128)S(1)}, u32[]{:S(2)}, u32[]{:S(2)}) collective-permute-start(f32[256,128]{1,0:T(8,128)S(1)} %get-tuple-element.39.refs_3_.refs_34_), channel_id=1, source_target_pairs={{0,6},{1,7},{2,4},{3,5},{4,2},{5,3},{6,0},{7,1},{8,14},{9,15},{10,... | collective-permute-start | bytes 393224 | tf_op jit(solution)/shard_map/ppermute | solution.py:179
  58.4 7.5 %collective-permute-start.19 = (f32[256,128]{1,0:T(8,128)S(1)}, f32[256,128]{1,0:T(8,128)S(1)}, u32[]{:S(2)}, u32[]{:S(2)}) collective-permute-start(f32[256,128]{1,0:T(8,128)S(1)} %get-tuple-element.39.refs_3_.refs_34_), channel_id=1, source_target_pairs={{0,4},{1,5},{2,6},{3,7},{4,0},{5,1},{6,2},{7,3},{8,12},{9,13},{10,... | collective-permute-start | bytes 393224 | tf_op jit(solution)/shard_map/ppermute | solution.py:179
  59.1 7.0 %collective-permute-start.20 = (f32[256,128]{1,0:T(8,128)S(1)}, f32[256,128]{1,0:T(8,128)S(1)}, u32[]{:S(2)}, u32[]{:S(2)}) collective-permute-start(f32[256,128]{1,0:T(8,128)S(1)} %get-tuple-element.39.refs_3_.refs_34_), channel_id=1, source_target_pairs={{0,2},{1,3},{2,0},{3,1},{4,6},{5,7},{6,4},{7,5},{8,10},{9,11},{10,... | collective-permute-start | bytes 393224 | tf_op jit(solution)/shard_map/ppermute | solution.py:179
  60.1 13.7 %collective-permute-start.40 = (f32[512,128]{1,0:T(8,128)S(1)}, f32[512,128]{1,0:T(8,128)S(1)}, u32[]{:S(2)}, u32[]{:S(2)}) collective-permute-start(f32[512,128]{1,0:T(8,128)S(1)} %copy-done.3), channel_id=1, source_target_pairs={{0,8},{1,9},{2,10},{3,11},{4,12},{5,13},{6,14},{7,15},{8,0},{9,1},... | collective-permute-start | bytes 786440 | tf_op jit(solution)/shard_map/ppermute | solution.py:179
  61.7 4.7 %collective-permute-start.24 = (f32[256,128]{1,0:T(8,128)S(1)}, f32[256,128]{1,0:T(8,128)S(1)}, u32[]{:S(2)}, u32[]{:S(2)}) collective-permute-start(f32[256,128]{1,0:T(8,128)S(1)} %get-tuple-element.39.refs_3_.refs_34_), channel_id=1, source_target_pairs={{0,1},{1,0},{2,3},{3,2},{4,5},{5,4},{6,7},{7,6},{8,9},{9,8},{10,11... | collective-permute-start | bytes 393224 | tf_op jit(solution)/shard_map/ppermute | solution.py:179
  65.5 1.4 %collective-permute-start.21 = (f32[256,128]{1,0:T(8,128)S(1)}, f32[256,128]{1,0:T(8,128)S(1)}, u32[]{:S(2)}, u32[]{:S(2)}) collective-permute-start(f32[256,128]{1,0:T(8,128)S(1)} %get-tuple-element.40.refs_0_), channel_id=1, source_target_pairs={{0,1},{1,0},{2,3},{3,2},{4,5},{5,4},{6,7},{7,6},{8,9},{9,8},{10,11... | collective-permute-start | bytes 393224 | tf_op jit(solution)/shard_map/ppermute | solution.py:179
  68.4 8.6 %collective-permute-start.25 = (f32[256,128]{1,0:T(8,128)S(1)}, f32[256,128]{1,0:T(8,128)S(1)}, u32[]{:S(2)}, u32[]{:S(2)}) collective-permute-start(f32[256,128]{1,0:T(8,128)S(1)} %update.4.after.refs_7_), channel_id=1, source_target_pairs={{0,14},{1,15},{2,12},{3,13},{4,10},{5,11},{6,8},{7,9},{8,6},{9,7},... | collective-permute-start | bytes 393224 | tf_op jit(solution)/shard_map/ppermute | solution.py:179
  71.2 8.1 %collective-permute-start.26 = (f32[256,128]{1,0:T(8,128)S(1)}, f32[256,128]{1,0:T(8,128)S(1)}, u32[]{:S(2)}, u32[]{:S(2)}) collective-permute-start(f32[256,128]{1,0:T(8,128)S(1)} %update.4.after.refs_7_), channel_id=1, source_target_pairs={{0,12},{1,13},{2,14},{3,15},{4,8},{5,9},{6,10},{7,11},{8,4},{9,5},... | collective-permute-start | bytes 393224 | tf_op jit(solution)/shard_map/ppermute | solution.py:179
  71.8 10.7 %collective-permute-start.27 = (f32[256,128]{1,0:T(8,128)S(1)}, f32[256,128]{1,0:T(8,128)S(1)}, u32[]{:S(2)}, u32[]{:S(2)}) collective-permute-start(f32[256,128]{1,0:T(8,128)S(1)} %update.4.after.refs_7_), channel_id=1, source_target_pairs={{0,10},{1,11},{2,8},{3,9},{4,14},{5,15},{6,12},{7,13},{8,2},{9,3},... | collective-permute-start | bytes 393224 | tf_op jit(solution)/shard_map/ppermute | solution.py:179
  73.9 16.3 %collective-permute-start.41 = (f32[1024,128]{1,0:T(8,128)S(1)}, f32[1024,128]{1,0:T(8,128)S(1)}, u32[]{:S(2)}, u32[]{:S(2)}) collective-permute-start(f32[1024,128]{1,0:T(8,128)S(1)} %join.7.refs_16_), channel_id=1, source_target_pairs={{0,1},{1,0},{2,3},{3,2},{4,5},{5,4},{6,7},{7,6},{8,9},{9,8},{10,11... | collective-permute-start | bytes 1572872 | tf_op jit(solution)/shard_map/ppermute | solution.py:179
  74.0 10.8 %collective-permute-start.28 = (f32[256,128]{1,0:T(8,128)S(1)}, f32[256,128]{1,0:T(8,128)S(1)}, u32[]{:S(2)}, u32[]{:S(2)}) collective-permute-start(f32[256,128]{1,0:T(8,128)S(1)} %update.4.after.refs_7_), channel_id=1, source_target_pairs={{0,8},{1,9},{2,10},{3,11},{4,12},{5,13},{6,14},{7,15},{8,0},{9,1},... | collective-permute-start | bytes 393224 | tf_op jit(solution)/shard_map/ppermute | solution.py:179
  77.0 7.9 %collective-permute-start.29 = (f32[256,128]{1,0:T(8,128)S(1)}, f32[256,128]{1,0:T(8,128)S(1)}, u32[]{:S(2)}, u32[]{:S(2)}) collective-permute-start(f32[256,128]{1,0:T(8,128)S(1)} %update.4.after.refs_7_), channel_id=1, source_target_pairs={{0,6},{1,7},{2,4},{3,5},{4,2},{5,3},{6,0},{7,1},{8,14},{9,15},{10,... | collective-permute-start | bytes 393224 | tf_op jit(solution)/shard_map/ppermute | solution.py:179
  79.3 6.5 %collective-permute-start.30 = (f32[256,128]{1,0:T(8,128)S(1)}, f32[256,128]{1,0:T(8,128)S(1)}, u32[]{:S(2)}, u32[]{:S(2)}) collective-permute-start(f32[256,128]{1,0:T(8,128)S(1)} %update.4.after.refs_7_), channel_id=1, source_target_pairs={{0,4},{1,5},{2,6},{3,7},{4,0},{5,1},{6,2},{7,3},{8,12},{9,13},{10,... | collective-permute-start | bytes 393224 | tf_op jit(solution)/shard_map/ppermute | solution.py:179
  82.5 5.0 %collective-permute-start.31 = (f32[256,128]{1,0:T(8,128)S(1)}, f32[256,128]{1,0:T(8,128)S(1)}, u32[]{:S(2)}, u32[]{:S(2)}) collective-permute-start(f32[256,128]{1,0:T(8,128)S(1)} %update.4.after.refs_7_), channel_id=1, source_target_pairs={{0,2},{1,3},{2,0},{3,1},{4,6},{5,7},{6,4},{7,5},{8,10},{9,11},{10,... | collective-permute-start | bytes 393224 | tf_op jit(solution)/shard_map/ppermute | solution.py:179
  84.8 2.7 %collective-permute-start.39 = (f32[256,128]{1,0:T(8,128)S(1)}, f32[256,128]{1,0:T(8,128)S(1)}, u32[]{:S(2)}, u32[]{:S(2)}) collective-permute-start(f32[256,128]{1,0:T(8,128)S(1)} %update.4.after.refs_7_), channel_id=1, source_target_pairs={{0,1},{1,0},{2,3},{3,2},{4,5},{5,4},{6,7},{7,6},{8,9},{9,8},{10,11... | collective-permute-start | bytes 393224 | tf_op jit(solution)/shard_map/ppermute | solution.py:179
  84.9 3.1 %collective-permute-start.32 = (f32[256,128]{1,0:T(8,128)S(1)}, f32[256,128]{1,0:T(8,128)S(1)}, u32[]{:S(2)}, u32[]{:S(2)}) collective-permute-start(f32[256,128]{1,0:T(8,128)S(1)} %get-tuple-element.43.refs_0_), channel_id=1, source_target_pairs={{0,1},{1,0},{2,3},{3,2},{4,5},{5,4},{6,7},{7,6},{8,9},{9,8},{10,11... | collective-permute-start | bytes 393224 | tf_op jit(solution)/shard_map/ppermute | solution.py:179
  85.8 2.2 %collective-permute-start.33 = (f32[256,128]{1,0:T(8,128)S(1)}, f32[256,128]{1,0:T(8,128)S(1)}, u32[]{:S(2)}, u32[]{:S(2)}) collective-permute-start(f32[256,128]{1,0:T(8,128)S(1)} %collective-permute-done.26.refs_1_), channel_id=1, source_target_pairs={{0,1},{1,0},{2,3},{3,2},{4,5},{5,4},{6,7},{7,6},{8,9},{9,8},{10,11... | collective-permute-start | bytes 393224 | tf_op jit(solution)/shard_map/ppermute | solution.py:179
  87.5 1.5 %collective-permute-start.35 = (f32[256,128]{1,0:T(8,128)S(1)}, f32[256,128]{1,0:T(8,128)S(1)}, u32[]{:S(2)}, u32[]{:S(2)}) collective-permute-start(f32[256,128]{1,0:T(8,128)S(1)} %collective-permute-done.28.refs_3_), channel_id=1, source_target_pairs={{0,1},{1,0},{2,3},{3,2},{4,5},{5,4},{6,7},{7,6},{8,9},{9,8},{10,11... | collective-permute-start | bytes 393224 | tf_op jit(solution)/shard_map/ppermute | solution.py:179
  88.1 1.5 %collective-permute-start.37 = (f32[256,128]{1,0:T(8,128)S(1)}, f32[256,128]{1,0:T(8,128)S(1)}, u32[]{:S(2)}, u32[]{:S(2)}) collective-permute-start(f32[256,128]{1,0:T(8,128)S(1)} %collective-permute-done.30.refs_5_), channel_id=1, source_target_pairs={{0,1},{1,0},{2,3},{3,2},{4,5},{5,4},{6,7},{7,6},{8,9},{9,8},{10,11... | collective-permute-start | bytes 393224 | tf_op jit(solution)/shard_map/ppermute | solution.py:179
  91.8 8.6 %collective-permute-start.42 = (f32[256,128]{1,0:T(8,128)S(1)}, f32[256,128]{1,0:T(8,128)S(1)}, u32[]{:S(2)}, u32[]{:S(2)}) collective-permute-start(f32[256,128]{1,0:T(8,128)S(1)} %get-tuple-element.46.refs_7_.refs_23_.refs_35_), channel_id=1, source_target_pairs={{0,14},{1,15},{2,12},{3,13},{4,10},{5,11},{6,8},{7,9},{8,6},{9,7},... | collective-permute-start | bytes 393224 | tf_op jit(solution)/shard_map/ppermute | solution.py:179
  94.0 9.6 %collective-permute-start.43 = (f32[256,128]{1,0:T(8,128)S(1)}, f32[256,128]{1,0:T(8,128)S(1)}, u32[]{:S(2)}, u32[]{:S(2)}) collective-permute-start(f32[256,128]{1,0:T(8,128)S(1)} %get-tuple-element.46.refs_7_.refs_23_.refs_35_), channel_id=1, source_target_pairs={{0,12},{1,13},{2,14},{3,15},{4,8},{5,9},{6,10},{7,11},{8,4},{9,5},... | collective-permute-start | bytes 393224 | tf_op jit(solution)/shard_map/ppermute | solution.py:179
  95.2 10.6 %collective-permute-start.44 = (f32[256,128]{1,0:T(8,128)S(1)}, f32[256,128]{1,0:T(8,128)S(1)}, u32[]{:S(2)}, u32[]{:S(2)}) collective-permute-start(f32[256,128]{1,0:T(8,128)S(1)} %get-tuple-element.46.refs_7_.refs_23_.refs_35_), channel_id=1, source_target_pairs={{0,10},{1,11},{2,8},{3,9},{4,14},{5,15},{6,12},{7,13},{8,2},{9,3},... | collective-permute-start | bytes 393224 | tf_op jit(solution)/shard_map/ppermute | solution.py:179
  97.3 9.6 %collective-permute-start.45 = (f32[256,128]{1,0:T(8,128)S(1)}, f32[256,128]{1,0:T(8,128)S(1)}, u32[]{:S(2)}, u32[]{:S(2)}) collective-permute-start(f32[256,128]{1,0:T(8,128)S(1)} %get-tuple-element.46.refs_7_.refs_23_.refs_35_), channel_id=1, source_target_pairs={{0,8},{1,9},{2,10},{3,11},{4,12},{5,13},{6,14},{7,15},{8,0},{9,1},... | collective-permute-start | bytes 393224 | tf_op jit(solution)/shard_map/ppermute | solution.py:179
  97.7 9.2 %collective-permute-start.46 = (f32[256,128]{1,0:T(8,128)S(1)}, f32[256,128]{1,0:T(8,128)S(1)}, u32[]{:S(2)}, u32[]{:S(2)}) collective-permute-start(f32[256,128]{1,0:T(8,128)S(1)} %get-tuple-element.46.refs_7_.refs_23_.refs_35_), channel_id=1, source_target_pairs={{0,6},{1,7},{2,4},{3,5},{4,2},{5,3},{6,0},{7,1},{8,14},{9,15},{10,... | collective-permute-start | bytes 393224 | tf_op jit(solution)/shard_map/ppermute | solution.py:179
  100.4 7.2 %collective-permute-start.47 = (f32[256,128]{1,0:T(8,128)S(1)}, f32[256,128]{1,0:T(8,128)S(1)}, u32[]{:S(2)}, u32[]{:S(2)}) collective-permute-start(f32[256,128]{1,0:T(8,128)S(1)} %get-tuple-element.46.refs_7_.refs_23_.refs_35_), channel_id=1, source_target_pairs={{0,4},{1,5},{2,6},{3,7},{4,0},{5,1},{6,2},{7,3},{8,12},{9,13},{10,... | collective-permute-start | bytes 393224 | tf_op jit(solution)/shard_map/ppermute | solution.py:179
  103.6 5.0 %collective-permute-start.48 = (f32[256,128]{1,0:T(8,128)S(1)}, f32[256,128]{1,0:T(8,128)S(1)}, u32[]{:S(2)}, u32[]{:S(2)}) collective-permute-start(f32[256,128]{1,0:T(8,128)S(1)} %get-tuple-element.46.refs_7_.refs_23_.refs_35_), channel_id=1, source_target_pairs={{0,2},{1,3},{2,0},{3,1},{4,6},{5,7},{6,4},{7,5},{8,10},{9,11},{10,... | collective-permute-start | bytes 393224 | tf_op jit(solution)/shard_map/ppermute | solution.py:179
  105.8 2.8 %collective-permute-start.56 = (f32[256,128]{1,0:T(8,128)S(1)}, f32[256,128]{1,0:T(8,128)S(1)}, u32[]{:S(2)}, u32[]{:S(2)}) collective-permute-start(f32[256,128]{1,0:T(8,128)S(1)} %get-tuple-element.46.refs_7_.refs_23_.refs_35_), channel_id=1, source_target_pairs={{0,1},{1,0},{2,3},{3,2},{4,5},{5,4},{6,7},{7,6},{8,9},{9,8},{10,11... | collective-permute-start | bytes 393224 | tf_op jit(solution)/shard_map/ppermute | solution.py:179
  106.9 2.2 %collective-permute-start.49 = (f32[256,128]{1,0:T(8,128)S(1)}, f32[256,128]{1,0:T(8,128)S(1)}, u32[]{:S(2)}, u32[]{:S(2)}) collective-permute-start(f32[256,128]{1,0:T(8,128)S(1)} %get-tuple-element.47.refs_0_.refs_16_), channel_id=1, source_target_pairs={{0,1},{1,0},{2,3},{3,2},{4,5},{5,4},{6,7},{7,6},{8,9},{9,8},{10,11... | collective-permute-start | bytes 393224 | tf_op jit(solution)/shard_map/ppermute | solution.py:179
  107.0 2.2 %collective-permute-start.50 = (f32[256,128]{1,0:T(8,128)S(1)}, f32[256,128]{1,0:T(8,128)S(1)}, u32[]{:S(2)}, u32[]{:S(2)}) collective-permute-start(f32[256,128]{1,0:T(8,128)S(1)} %get-tuple-element.48.refs_1_.refs_17_), channel_id=1, source_target_pairs={{0,1},{1,0},{2,3},{3,2},{4,5},{5,4},{6,7},{7,6},{8,9},{9,8},{10,11... | collective-permute-start | bytes 393224 | tf_op jit(solution)/shard_map/ppermute | solution.py:179
  107.6 2.0 %collective-permute-start.51 = (f32[256,128]{1,0:T(8,128)S(1)}, f32[256,128]{1,0:T(8,128)S(1)}, u32[]{:S(2)}, u32[]{:S(2)}) collective-permute-start(f32[256,128]{1,0:T(8,128)S(1)} %collective-permute-done.44.refs_2_.refs_18_), channel_id=1, source_target_pairs={{0,1},{1,0},{2,3},{3,2},{4,5},{5,4},{6,7},{7,6},{8,9},{9,8},{10,11... | collective-permute-start | bytes 393224 | tf_op jit(solution)/shard_map/ppermute | solution.py:179
  108.6 1.5 %collective-permute-start.53 = (f32[256,128]{1,0:T(8,128)S(1)}, f32[256,128]{1,0:T(8,128)S(1)}, u32[]{:S(2)}, u32[]{:S(2)}) collective-permute-start(f32[256,128]{1,0:T(8,128)S(1)} %collective-permute-done.46.refs_4_.refs_20_), channel_id=1, source_target_pairs={{0,1},{1,0},{2,3},{3,2},{4,5},{5,4},{6,7},{7,6},{8,9},{9,8},{10,11... | collective-permute-start | bytes 393224 | tf_op jit(solution)/shard_map/ppermute | solution.py:179
  109.2 1.5 %collective-permute-start.55 = (f32[256,128]{1,0:T(8,128)S(1)}, f32[256,128]{1,0:T(8,128)S(1)}, u32[]{:S(2)}, u32[]{:S(2)}) collective-permute-start(f32[256,128]{1,0:T(8,128)S(1)} %collective-permute-done.48.refs_6_.refs_22_), channel_id=1, source_target_pairs={{0,1},{1,0},{2,3},{3,2},{4,5},{5,4},{6,7},{7,6},{8,9},{9,8},{10,11... | collective-permute-start | bytes 393224 | tf_op jit(solution)/shard_map/ppermute | solution.py:179
  111.2 6.7 %collective-permute-start.57 = (f32[128,128]{1,0:T(8,128)S(1)}, f32[128,128]{1,0:T(8,128)S(1)}, u32[]{:S(2)}, u32[]{:S(2)}) collective-permute-start(f32[128,128]{1,0:T(8,128)S(1)} %update.5), channel_id=1, source_target_pairs={{0,16},{1,17},{2,18},{3,19},{4,20},{5,21},{6,22},{7,23},{8,24},{9,... | collective-permute-start | bytes 196616 | tf_op jit(solution)/shard_map/ppermute | solution.py:179
  117.9 8.8 %collective-permute-start.58 = (f32[256,128]{1,0:T(8,128)S(1)}, f32[256,128]{1,0:T(8,128)S(1)}, u32[]{:S(2)}, u32[]{:S(2)}) collective-permute-start(f32[256,128]{1,0:T(8,128)S(1)} %pad_maximum_fusion.refs_7_), channel_id=1, source_target_pairs={{0,14},{1,15},{2,12},{3,13},{4,10},{5,11},{6,8},{7,9},{8,6},{9,7},... | collective-permute-start | bytes 393224 | tf_op jit(solution)/shard_map/ppermute | solution.py:179
  119.6 9.3 %collective-permute-start.59 = (f32[256,128]{1,0:T(8,128)S(1)}, f32[256,128]{1,0:T(8,128)S(1)}, u32[]{:S(2)}, u32[]{:S(2)}) collective-permute-start(f32[256,128]{1,0:T(8,128)S(1)} %pad_maximum_fusion.refs_7_), channel_id=1, source_target_pairs={{0,12},{1,13},{2,14},{3,15},{4,8},{5,9},{6,10},{7,11},{8,4},{9,5},... | collective-permute-start | bytes 393224 | tf_op jit(solution)/shard_map/ppermute | solution.py:179
  121.4 9.9 %collective-permute-start.60 = (f32[256,128]{1,0:T(8,128)S(1)}, f32[256,128]{1,0:T(8,128)S(1)}, u32[]{:S(2)}, u32[]{:S(2)}) collective-permute-start(f32[256,128]{1,0:T(8,128)S(1)} %pad_maximum_fusion.refs_7_), channel_id=1, source_target_pairs={{0,10},{1,11},{2,8},{3,9},{4,14},{5,15},{6,12},{7,13},{8,2},{9,3},... | collective-permute-start | bytes 393224 | tf_op jit(solution)/shard_map/ppermute | solution.py:179
  122.5 9.7 %collective-permute-start.61 = (f32[256,128]{1,0:T(8,128)S(1)}, f32[256,128]{1,0:T(8,128)S(1)}, u32[]{:S(2)}, u32[]{:S(2)}) collective-permute-start(f32[256,128]{1,0:T(8,128)S(1)} %pad_maximum_fusion.refs_7_), channel_id=1, source_target_pairs={{0,8},{1,9},{2,10},{3,11},{4,12},{5,13},{6,14},{7,15},{8,0},{9,1},... | collective-permute-start | bytes 393224 | tf_op jit(solution)/shard_map/ppermute | solution.py:179
  123.9 8.7 %collective-permute-start.62 = (f32[256,128]{1,0:T(8,128)S(1)}, f32[256,128]{1,0:T(8,128)S(1)}, u32[]{:S(2)}, u32[]{:S(2)}) collective-permute-start(f32[256,128]{1,0:T(8,128)S(1)} %pad_maximum_fusion.refs_7_), channel_id=1, source_target_pairs={{0,6},{1,7},{2,4},{3,5},{4,2},{5,3},{6,0},{7,1},{8,14},{9,15},{10,... | collective-permute-start | bytes 393224 | tf_op jit(solution)/shard_map/ppermute | solution.py:179
  126.7 6.2 %collective-permute-start.63 = (f32[256,128]{1,0:T(8,128)S(1)}, f32[256,128]{1,0:T(8,128)S(1)}, u32[]{:S(2)}, u32[]{:S(2)}) collective-permute-start(f32[256,128]{1,0:T(8,128)S(1)} %pad_maximum_fusion.refs_7_), channel_id=1, source_target_pairs={{0,4},{1,5},{2,6},{3,7},{4,0},{5,1},{6,2},{7,3},{8,12},{9,13},{10,... | collective-permute-start | bytes 393224 | tf_op jit(solution)/shard_map/ppermute | solution.py:179
  128.9 5.0 %collective-permute-start.64 = (f32[256,128]{1,0:T(8,128)S(1)}, f32[256,128]{1,0:T(8,128)S(1)}, u32[]{:S(2)}, u32[]{:S(2)}) collective-permute-start(f32[256,128]{1,0:T(8,128)S(1)} %pad_maximum_fusion.refs_7_), channel_id=1, source_target_pairs={{0,2},{1,3},{2,0},{3,1},{4,6},{5,7},{6,4},{7,5},{8,10},{9,11},{10,... | collective-permute-start | bytes 393224 | tf_op jit(solution)/shard_map/ppermute | solution.py:179
  131.3 2.6 %collective-permute-start.72 = (f32[256,128]{1,0:T(8,128)S(1)}, f32[256,128]{1,0:T(8,128)S(1)}, u32[]{:S(2)}, u32[]{:S(2)}) collective-permute-start(f32[256,128]{1,0:T(8,128)S(1)} %pad_maximum_fusion.refs_7_), channel_id=1, source_target_pairs={{0,1},{1,0},{2,3},{3,2},{4,5},{5,4},{6,7},{7,6},{8,9},{9,8},{10,11... | collective-permute-start | bytes 393224 | tf_op jit(solution)/shard_map/ppermute | solution.py:179
  132.2 2.1 %collective-permute-start.65 = (f32[256,128]{1,0:T(8,128)S(1)}, f32[256,128]{1,0:T(8,128)S(1)}, u32[]{:S(2)}, u32[]{:S(2)}) collective-permute-start(f32[256,128]{1,0:T(8,128)S(1)} %collective-permute-done.58.refs_0_), channel_id=1, source_target_pairs={{0,1},{1,0},{2,3},{3,2},{4,5},{5,4},{6,7},{7,6},{8,9},{9,8},{10,11... | collective-permute-start | bytes 393224 | tf_op jit(solution)/shard_map/ppermute | solution.py:179
  132.6 1.9 %collective-permute-start.66 = (f32[256,128]{1,0:T(8,128)S(1)}, f32[256,128]{1,0:T(8,128)S(1)}, u32[]{:S(2)}, u32[]{:S(2)}) collective-permute-start(f32[256,128]{1,0:T(8,128)S(1)} %collective-permute-done.59.refs_1_), channel_id=1, source_target_pairs={{0,1},{1,0},{2,3},{3,2},{4,5},{5,4},{6,7},{7,6},{8,9},{9,8},{10,11... | collective-permute-start | bytes 393224 | tf_op jit(solution)/shard_map/ppermute | solution.py:179
  132.9 2.0 %collective-permute-start.67 = (f32[256,128]{1,0:T(8,128)S(1)}, f32[256,128]{1,0:T(8,128)S(1)}, u32[]{:S(2)}, u32[]{:S(2)}) collective-permute-start(f32[256,128]{1,0:T(8,128)S(1)} %collective-permute-done.60.refs_2_), channel_id=1, source_target_pairs={{0,1},{1,0},{2,3},{3,2},{4,5},{5,4},{6,7},{7,6},{8,9},{9,8},{10,11... | collective-permute-start | bytes 393224 | tf_op jit(solution)/shard_map/ppermute | solution.py:179
  133.9 1.5 %collective-permute-start.69 = (f32[256,128]{1,0:T(8,128)S(1)}, f32[256,128]{1,0:T(8,128)S(1)}, u32[]{:S(2)}, u32[]{:S(2)}) collective-permute-start(f32[256,128]{1,0:T(8,128)S(1)} %collective-permute-done.62.refs_4_), channel_id=1, source_target_pairs={{0,1},{1,0},{2,3},{3,2},{4,5},{5,4},{6,7},{7,6},{8,9},{9,8},{10,11... | collective-permute-start | bytes 393224 | tf_op jit(solution)/shard_map/ppermute | solution.py:179
  134.4 1.5 %collective-permute-start.71 = (f32[256,128]{1,0:T(8,128)S(1)}, f32[256,128]{1,0:T(8,128)S(1)}, u32[]{:S(2)}, u32[]{:S(2)}) collective-permute-start(f32[256,128]{1,0:T(8,128)S(1)} %collective-permute-done.64.refs_6_), channel_id=1, source_target_pairs={{0,1},{1,0},{2,3},{3,2},{4,5},{5,4},{6,7},{7,6},{8,9},{9,8},{10,11... | collective-permute-start | bytes 393224 | tf_op jit(solution)/shard_map/ppermute | solution.py:179
  (15 other events, 66.4 us)
